TPU v7x, 32 devices: a whole 2x2x4 slice. The times are simulated.
32 devices in a mesh: dp: 8 (over y, x, core), seq: 4 (over z).
Axes of the slice: x: 2, y: 2, z: 4, core: 2. Of those that a mesh axis runs over, the one named last changes fastest.
Arguments:
- frames: bfloat16 [16, 1024, 768], P('dp', 'seq'), may hold values from -6 to 6
- output_gradient: bfloat16 [16, 1024, 768], P('dp', 'seq'), may hold values from -6 to 6
- segments: int32 [16, 1024], replicated, may hold values from 0 to 4, as said below
- layer_keep: int32 [16], replicated, may hold values from 0 to 1, as said below
- conv_weight: bfloat16 [128, 768, 48], replicated, may hold values from -0.078125 to 0.078125
- convolution_bias: float32 [768], replicated, may hold values from -3 to 3
- query_matrix: bfloat16 [768, 768], replicated, may hold values from -0.21875 to 0.21875
- query_offset_bias: float32 [768], replicated, may hold values from -3 to 3
- key_matrix: bfloat16 [768, 768], replicated, may hold values from -0.21875 to 0.21875
- value_matrix: bfloat16 [768, 768], replicated, may hold values from -0.21875 to 0.21875
- value_offset_bias: float32 [768], replicated, may hold values from -3 to 3
- attn_weight: bfloat16 [768, 768], replicated, may hold values from -0.875 to 0.875
- attn_bias: float32 [768], replicated, may hold values from -2 to 2
- first_gain: float32 [768], replicated, may hold values from 0.25 to 1.75
- first_shift: float32 [768], replicated, may hold values from -2 to 2
- inner_weight: bfloat16 [768, 3072], replicated, may hold values from -0.21875 to 0.21875
- inner_bias: float32 [3072], replicated, may hold values from -2 to 2
- outer_weight: bfloat16 [3072, 768], replicated, may hold values from -0.109375 to 0.109375
- outer_bias: float32 [768], replicated, may hold values from -2 to 2
- second_gain: float32 [768], replicated, may hold values from 0.25 to 1.75
- second_shift: float32 [768], replicated, may hold values from -2 to 2
Outputs:
- layer_out: bfloat16 [16, 1024, 768], P('dp', 'seq')
- input_grad: bfloat16 [16, 1024, 768], P('dp', 'seq')
- conv_weight_grad: float32 [128, 768, 48], P(None, 'dp')
- conv_bias_grad: float32 [768], P('dp')
- query_weight_grad: float32 [768, 768], P(None, 'dp')
- query_bias_grad: float32 [768], P('dp')
- key_weight_grad: float32 [768, 768], P(None, 'dp')
- value_weight_grad: float32 [768, 768], P(None, 'dp')
- value_bias_grad: float32 [768], P('dp')
- attn_weight_grad: float32 [768, 768], P(None, 'dp')
- attn_bias_grad: float32 [768], P('dp')
- first_gain_grad: float32 [768], P('dp')
- first_shift_grad: float32 [768], P('dp')
- inner_weight_grad: float32 [768, 3072], P(None, 'dp')
- inner_bias_grad: float32 [3072], P('dp')
- outer_weight_grad: float32 [3072, 768], P(None, 'dp')
- outer_bias_grad: float32 [768], P('dp')
- second_gain_grad: float32 [768], P('dp')
- second_shift_grad: float32 [768], P('dp')
Inputs may be any that keep to these rules, and one draw needn't show every extreme that they name: `segments`: in every row, 0 marks padding and the utterances are numbered 1, 2, ... from the row's start with padding only after the last; each utterance has 256 to 1024 frames. `layer_keep`: exactly max(1, 1) rows have 0, the others 1.
All inputs are finite; a program needn't handle non-finite values.
Results may differ from a plain program's by a relative error of at most 0.023.
Values may be sent and summed in bfloat16 or wider, within the bound.
No kernel may reach another device: no remote copies, remote signals or barrier semaphores. Data moves between devices by JAX's collectives and lax.ppermute only.
A program may use at most 512 MiB of HBM per device.

v0:
```python
import jax
import jax.numpy as jnp
from jax import lax
from jax.sharding import PartitionSpec as P

HEAD_SIZE = 64


neg_big = -1e30
root_half = 0.7071067811865476
inv_root_two_pi = 0.3989422804014327


def with_halo(block, sides, width):
    for axis, dim in sides:
        count = lax.axis_size(axis)
        forward = [(i, i + 1) for i in range(count - 1)]
        backward = [(target, source) for source, target in forward]
        low = lax.ppermute(
            lax.slice_in_dim(block, block.shape[dim] - width, None, axis=dim), axis, forward
        )
        high = lax.ppermute(lax.slice_in_dim(block, 0, width, axis=dim), axis, backward)
        block = jnp.concatenate([low, block, high], axis=dim)
    return block


def layer_norm(hidden):
    centred = hidden - jnp.mean(hidden, axis=-1, keepdims=True)
    inv_scale = lax.rsqrt(jnp.mean(centred * centred, axis=-1, keepdims=True) + 1e-05)
    return (centred * inv_scale, inv_scale)


def norm_back(grad_normed, normed, inv_scale):
    return inv_scale * (
        grad_normed
        - jnp.mean(grad_normed, axis=-1, keepdims=True)
        - normed * jnp.mean(grad_normed * normed, axis=-1, keepdims=True)
    )


def gelu_slope(entries):
    return (
        0.5 * (1.0 + lax.erf(entries * root_half))
        + entries * jnp.exp(-0.5 * entries * entries) * inv_root_two_pi
    )


def project(left_side, right_side):
    return jnp.einsum("wtd,de->wte", left_side, right_side, preferred_element_type=jnp.float32)


def project_back(left_side, right_side):
    return jnp.einsum("wte,de->wtd", left_side, right_side, preferred_element_type=jnp.float32)


def weight_grad(left_side, right_side):
    return jnp.einsum("wtd,wte->de", left_side, right_side, preferred_element_type=jnp.float32)


def column_sum(entries):
    return jnp.sum(entries, axis=(0, 1), dtype=jnp.float32)


def block_scores(query_part, key_part, seg_query, seg_keys, score_scale):
    scores = (
        jnp.einsum("wqhd,wkhd->whqk", query_part, key_part, preferred_element_type=jnp.float32)
        * score_scale
    )
    allowed = (seg_query[:, None, :, None] == seg_keys[:, None, None, :]) & (
        seg_query[:, None, :, None] > 0
    )
    return (jnp.where(allowed, scores, neg_big), allowed)


def on_device(
    frames,
    output_gradient,
    segments,
    layer_keep,
    conv_weight,
    convolution_bias,
    query_matrix,
    query_offset_bias,
    key_matrix,
    value_matrix,
    value_offset_bias,
    attn_weight,
    attn_bias,
    first_gain,
    first_shift,
    inner_weight,
    inner_bias,
    outer_weight,
    outer_bias,
    second_gain,
    second_shift,
):
    rows_dev, local_len, width = frames.shape
    total_rows, row_len = segments.shape
    group_index = lax.axis_index("dp")
    seq_index = lax.axis_index("seq")
    kernel = conv_weight.shape[0]
    group_width = conv_weight.shape[2]
    conv_groups = width // group_width
    half_kernel = kernel // 2
    margin = 2 * half_kernel
    kernel_tap_block = min(16, kernel)
    head_count = width // HEAD_SIZE
    score_scale = HEAD_SIZE ** (-0.5)
    row_ids = group_index * rows_dev + jnp.arange(rows_dev, dtype=jnp.int32)
    owned_rows = row_ids >= 0
    rows_win = frames.shape[0]
    in_range = (row_ids >= 0) & (row_ids < total_rows)
    safe_ids = jnp.clip(row_ids, 0, total_rows - 1)
    seg_rows = jnp.take(segments, safe_ids, axis=0)
    seg_rows = jnp.where(in_range[:, None], seg_rows, 0)
    keep_rows = jnp.where(in_range, jnp.take(layer_keep, safe_ids, axis=0), 0)
    keep_flag = (keep_rows > 0).astype(jnp.float32)[:, None, None]
    segment_padded = jnp.pad(seg_rows, ((0, 0), (margin, margin)))
    seg_wide = lax.dynamic_slice_in_dim(
        segment_padded, seq_index * local_len, local_len + 2 * margin, 1
    )
    seg_here = seg_wide[:, margin : margin + local_len]
    active_mask = seg_here > 0

    def tap_mask(kernel_tap_index):
        first_col = margin - half_kernel + kernel_tap_index
        return (seg_wide[:, first_col : first_col + local_len] == seg_here) & active_mask

    def back_mask(kernel_tap_index):
        first_col = margin + half_kernel - kernel_tap_index
        other_seg = seg_wide[:, first_col : first_col + local_len]
        return (other_seg == seg_here) & (other_seg > 0)

    masked_frames = jnp.where(active_mask[:, :, None], frames, jnp.zeros((), frames.dtype))
    rimmed = with_halo(masked_frames, (("seq", 1),), half_kernel)
    grouped_weight = conv_weight.reshape(kernel, conv_groups, group_width, group_width)

    def tap_window(block_index):
        pieces = [
            jnp.where(
                tap_mask(kernel_tap_index)[:, :, None],
                rimmed[:, kernel_tap_index : kernel_tap_index + local_len],
                jnp.zeros((), rimmed.dtype),
            )
            for kernel_tap_index in range(
                block_index * kernel_tap_block, (block_index + 1) * kernel_tap_block
            )
        ]
        return jnp.stack(pieces, 0).reshape(
            kernel_tap_block, rows_win, local_len, conv_groups, group_width
        )

    convolution_total = jnp.zeros((rows_win, local_len, conv_groups, group_width), jnp.float32)
    for block_index in range(kernel // kernel_tap_block):
        convolution_total = convolution_total + jnp.einsum(
            "kwtgi,kgio->wtgo",
            tap_window(block_index),
            grouped_weight[block_index * kernel_tap_block : (block_index + 1) * kernel_tap_block],
            preferred_element_type=jnp.float32,
        )
    convolution_before = convolution_total.reshape(rows_win, local_len, width) + convolution_bias
    pos_out = masked_frames.astype(jnp.float32) + jax.nn.gelu(convolution_before, approximate=False)
    position_lowered = pos_out.astype(jnp.bfloat16)
    query_low = (project(position_lowered, query_matrix) + query_offset_bias).astype(jnp.bfloat16)
    key_low = project(position_lowered, key_matrix).astype(jnp.bfloat16)
    value_low = (project(position_lowered, value_matrix) + value_offset_bias).astype(jnp.bfloat16)
    key_all, value_all = (
        lax.all_gather(key_low, "seq", axis=1, tiled=True),
        lax.all_gather(value_low, "seq", axis=1, tiled=True),
    )
    query_heads = query_low.reshape(rows_win, local_len, head_count, HEAD_SIZE)
    key_heads = key_all.reshape(rows_win, row_len, head_count, HEAD_SIZE)
    value_heads = value_all.reshape(rows_win, row_len, head_count, HEAD_SIZE)
    key_block = min(512, row_len)
    block_count = row_len // key_block

    def scores_of(block_index):
        key_cols = slice(block_index * key_block, (block_index + 1) * key_block)
        return block_scores(
            query_heads, key_heads[:, key_cols], seg_here, seg_rows[:, key_cols], score_scale
        )

    run_max = jnp.full((rows_win, head_count, local_len), neg_big, jnp.float32)
    run_sum = jnp.zeros((rows_win, head_count, local_len), jnp.float32)
    for block_index in range(block_count):
        masked, allowed = scores_of(block_index)
        new_max = jnp.maximum(run_max, jnp.max(masked, axis=-1))
        run_sum = run_sum * jnp.exp(run_max - new_max) + jnp.sum(
            jnp.where(allowed, jnp.exp(masked - new_max[..., None]), 0.0), axis=-1
        )
        run_max = new_max
    run_total = jnp.maximum(run_sum, 1.0)

    def softmax_block(masked, allowed):
        return jnp.where(allowed, jnp.exp(masked - run_max[..., None]), 0.0) / run_total[..., None]

    attn_acc = jnp.zeros((rows_win, local_len, head_count, HEAD_SIZE), jnp.float32)
    for block_index in range(block_count):
        masked, allowed = scores_of(block_index)
        prob_low = softmax_block(masked, allowed).astype(jnp.bfloat16)
        attn_acc = attn_acc + jnp.einsum(
            "whqk,wkhd->wqhd",
            prob_low,
            value_heads[:, block_index * key_block : (block_index + 1) * key_block],
            preferred_element_type=jnp.float32,
        )
    attn_low = attn_acc.reshape(rows_win, local_len, width).astype(jnp.bfloat16)
    attn_out = project(attn_low, attn_weight) + attn_bias
    first_normed, first_scale = layer_norm(pos_out + attn_out)
    first_out = first_normed * first_gain + first_shift
    first_low = first_out.astype(jnp.bfloat16)
    inner_pre = project(first_low, inner_weight) + inner_bias
    inner_low = jax.nn.gelu(inner_pre, approximate=False).astype(jnp.bfloat16)
    outer_out = project(inner_low, outer_weight) + outer_bias
    second_normed, second_scale = layer_norm(first_out + outer_out)
    second_out = second_normed * second_gain + second_shift
    result_win = (keep_flag * second_out + (1.0 - keep_flag) * pos_out).astype(jnp.bfloat16)
    grad_win = jnp.where(owned_rows[:, None, None], output_gradient.astype(jnp.float32), 0.0)
    grad_layer = keep_flag * grad_win
    grad_second_gain = column_sum(grad_layer * second_normed)
    grad_second_shift = column_sum(grad_layer)
    grad_second_sum = norm_back(grad_layer * second_gain, second_normed, second_scale)
    grad_outer_low = grad_second_sum.astype(jnp.bfloat16)
    grad_outer_weight = weight_grad(inner_low, grad_outer_low)
    grad_outer_bias = column_sum(grad_outer_low)
    grad_inner_low = (project_back(grad_outer_low, outer_weight) * gelu_slope(inner_pre)).astype(
        jnp.bfloat16
    )
    grad_inner_weight = weight_grad(first_low, grad_inner_low)
    grad_inner_bias = column_sum(grad_inner_low)
    grad_first_out = grad_second_sum + project_back(grad_inner_low, inner_weight)
    grad_first_gain = column_sum(grad_first_out * first_normed)
    grad_first_shift = column_sum(grad_first_out)
    grad_first_sum = norm_back(grad_first_out * first_gain, first_normed, first_scale)
    grad_attn_low = grad_first_sum.astype(jnp.bfloat16)
    grad_attn_weight = weight_grad(attn_low, grad_attn_low)
    grad_attn_bias = column_sum(grad_attn_low)
    grad_heads_low = project_back(grad_attn_low, attn_weight).astype(jnp.bfloat16)
    grad_heads = grad_heads_low.reshape(rows_win, local_len, head_count, HEAD_SIZE)
    prob_dot = jnp.zeros((rows_win, head_count, local_len), jnp.float32)
    for block_index in range(block_count):
        masked, allowed = scores_of(block_index)
        block_probs = softmax_block(masked, allowed)
        grad_probs = jnp.einsum(
            "wqhd,wkhd->whqk",
            grad_heads,
            value_heads[:, block_index * key_block : (block_index + 1) * key_block],
            preferred_element_type=jnp.float32,
        )
        prob_dot = prob_dot + jnp.sum(block_probs * grad_probs, axis=-1)
    grad_query = jnp.zeros((rows_win, local_len, head_count, HEAD_SIZE), jnp.float32)
    key_terms = []
    value_terms = []
    for block_index in range(block_count):
        key_cols = slice(block_index * key_block, (block_index + 1) * key_block)
        score_key_cols = slice(block_index * key_block, (block_index + 1) * key_block)
        score_masked, score_allowed = scores_of(block_index)
        score_block_probs = softmax_block(score_masked, score_allowed)
        score_grad_probs = jnp.einsum(
            "wqhd,wkhd->whqk",
            grad_heads,
            value_heads[:, score_key_cols],
            preferred_element_type=jnp.float32,
        )
        grad_scores = (score_block_probs * (score_grad_probs - prob_dot[..., None])).astype(
            jnp.bfloat16
        )
        block_probs, grad_scores = (score_block_probs, grad_scores)
        grad_query = grad_query + jnp.einsum(
            "whqk,wkhd->wqhd",
            grad_scores,
            key_heads[:, key_cols],
            preferred_element_type=jnp.float32,
        )
        key_terms.append(
            jnp.einsum(
                "whqk,wqhd->wkhd", grad_scores, query_heads, preferred_element_type=jnp.float32
            )
            * score_scale
        )
        value_terms.append(
            jnp.einsum(
                "whqk,wqhd->wkhd",
                block_probs.astype(jnp.bfloat16),
                grad_heads,
                preferred_element_type=jnp.float32,
            )
        )
    key_term = jnp.concatenate(key_terms, 1).reshape(rows_win, row_len, width)
    value_term = jnp.concatenate(value_terms, 1).reshape(rows_win, row_len, width)
    key_sum, value_sum = (
        lax.psum_scatter(
            key_term.astype(jnp.bfloat16), "seq", scatter_dimension=1, tiled=True
        ).astype(jnp.float32),
        lax.psum_scatter(
            value_term.astype(jnp.bfloat16), "seq", scatter_dimension=1, tiled=True
        ).astype(jnp.float32),
    )
    grad_query_low = (
        (grad_query * score_scale).reshape(rows_win, local_len, width).astype(jnp.bfloat16)
    )
    grad_key_low = key_sum.astype(jnp.bfloat16)
    grad_value_low = value_sum.astype(jnp.bfloat16)
    grad_query_weight = weight_grad(position_lowered, grad_query_low)
    grad_query_bias = column_sum(grad_query_low)
    grad_key_weight = weight_grad(position_lowered, grad_key_low)
    grad_value_weight = weight_grad(position_lowered, grad_value_low)
    grad_value_bias = column_sum(grad_value_low)
    grad_pos = (
        grad_first_sum
        + (1.0 - keep_flag) * grad_win
        + project_back(grad_query_low, query_matrix)
        + project_back(grad_key_low, key_matrix)
        + project_back(grad_value_low, value_matrix)
    )
    grad_conv_low = (grad_pos * gelu_slope(convolution_before)).astype(jnp.bfloat16)
    grad_conv_bias = column_sum(grad_conv_low)
    grad_grouped = grad_conv_low.reshape(rows_win, local_len, conv_groups, group_width)
    weight_blocks = []
    for block_index in range(kernel // kernel_tap_block):
        weight_blocks.append(
            jnp.einsum(
                "kwtgi,wtgo->kgio",
                tap_window(block_index),
                grad_grouped,
                preferred_element_type=jnp.float32,
            )
        )
    grad_conv_weight = jnp.concatenate(weight_blocks, 0).reshape(kernel, width, group_width)
    grad_rim = with_halo(grad_conv_low, (("seq", 1),), half_kernel)
    back_acc = jnp.zeros((rows_win, local_len, conv_groups, group_width), jnp.float32)
    for block_index in range(kernel // kernel_tap_block):
        pieces = [
            jnp.where(
                back_mask(kernel_tap_index)[:, :, None],
                grad_rim[:, margin - kernel_tap_index : margin - kernel_tap_index + local_len],
                jnp.zeros((), grad_rim.dtype),
            )
            for kernel_tap_index in range(
                block_index * kernel_tap_block, (block_index + 1) * kernel_tap_block
            )
        ]
        stacked_arrays = jnp.stack(pieces, 0).reshape(
            kernel_tap_block, rows_win, local_len, conv_groups, group_width
        )
        back_acc = back_acc + jnp.einsum(
            "kwtgo,kgio->wtgi",
            stacked_arrays,
            grouped_weight[block_index * kernel_tap_block : (block_index + 1) * kernel_tap_block],
            preferred_element_type=jnp.float32,
        )
    grad_input = jnp.where(
        active_mask[:, :, None], grad_pos + back_acc.reshape(rows_win, local_len, width), 0.0
    ).astype(jnp.bfloat16)
    shares = (
        lax.psum_scatter(
            grad_conv_weight.astype(jnp.bfloat16), "dp", scatter_dimension=1, tiled=True
        ).astype(jnp.float32),
        lax.psum_scatter(
            grad_conv_bias.astype(jnp.bfloat16), "dp", scatter_dimension=0, tiled=True
        ).astype(jnp.float32),
        lax.psum_scatter(
            grad_query_weight.astype(jnp.bfloat16), "dp", scatter_dimension=1, tiled=True
        ).astype(jnp.float32),
        lax.psum_scatter(
            grad_query_bias.astype(jnp.bfloat16), "dp", scatter_dimension=0, tiled=True
        ).astype(jnp.float32),
        lax.psum_scatter(
            grad_key_weight.astype(jnp.bfloat16), "dp", scatter_dimension=1, tiled=True
        ).astype(jnp.float32),
        lax.psum_scatter(
            grad_value_weight.astype(jnp.bfloat16), "dp", scatter_dimension=1, tiled=True
        ).astype(jnp.float32),
        lax.psum_scatter(
            grad_value_bias.astype(jnp.bfloat16), "dp", scatter_dimension=0, tiled=True
        ).astype(jnp.float32),
        lax.psum_scatter(
            grad_attn_weight.astype(jnp.bfloat16), "dp", scatter_dimension=1, tiled=True
        ).astype(jnp.float32),
        lax.psum_scatter(
            grad_attn_bias.astype(jnp.bfloat16), "dp", scatter_dimension=0, tiled=True
        ).astype(jnp.float32),
        lax.psum_scatter(
            grad_first_gain.astype(jnp.bfloat16), "dp", scatter_dimension=0, tiled=True
        ).astype(jnp.float32),
        lax.psum_scatter(
            grad_first_shift.astype(jnp.bfloat16), "dp", scatter_dimension=0, tiled=True
        ).astype(jnp.float32),
        lax.psum_scatter(
            grad_inner_weight.astype(jnp.bfloat16), "dp", scatter_dimension=1, tiled=True
        ).astype(jnp.float32),
        lax.psum_scatter(
            grad_inner_bias.astype(jnp.bfloat16), "dp", scatter_dimension=0, tiled=True
        ).astype(jnp.float32),
        lax.psum_scatter(
            grad_outer_weight.astype(jnp.bfloat16), "dp", scatter_dimension=1, tiled=True
        ).astype(jnp.float32),
        lax.psum_scatter(
            grad_outer_bias.astype(jnp.bfloat16), "dp", scatter_dimension=0, tiled=True
        ).astype(jnp.float32),
        lax.psum_scatter(
            grad_second_gain.astype(jnp.bfloat16), "dp", scatter_dimension=0, tiled=True
        ).astype(jnp.float32),
        lax.psum_scatter(
            grad_second_shift.astype(jnp.bfloat16), "dp", scatter_dimension=0, tiled=True
        ).astype(jnp.float32),
    )
    totals = (
        lax.psum(shares[0].astype(jnp.bfloat16), "seq").astype(jnp.float32),
        lax.psum(shares[1].astype(jnp.bfloat16), "seq").astype(jnp.float32),
        lax.psum(shares[2].astype(jnp.bfloat16), "seq").astype(jnp.float32),
        lax.psum(shares[3].astype(jnp.bfloat16), "seq").astype(jnp.float32),
        lax.psum(shares[4].astype(jnp.bfloat16), "seq").astype(jnp.float32),
        lax.psum(shares[5].astype(jnp.bfloat16), "seq").astype(jnp.float32),
        lax.psum(shares[6].astype(jnp.bfloat16), "seq").astype(jnp.float32),
        lax.psum(shares[7].astype(jnp.bfloat16), "seq").astype(jnp.float32),
        lax.psum(shares[8].astype(jnp.bfloat16), "seq").astype(jnp.float32),
        lax.psum(shares[9].astype(jnp.bfloat16), "seq").astype(jnp.float32),
        lax.psum(shares[10].astype(jnp.bfloat16), "seq").astype(jnp.float32),
        lax.psum(shares[11].astype(jnp.bfloat16), "seq").astype(jnp.float32),
        lax.psum(shares[12].astype(jnp.bfloat16), "seq").astype(jnp.float32),
        lax.psum(shares[13].astype(jnp.bfloat16), "seq").astype(jnp.float32),
        lax.psum(shares[14].astype(jnp.bfloat16), "seq").astype(jnp.float32),
        lax.psum(shares[15].astype(jnp.bfloat16), "seq").astype(jnp.float32),
        lax.psum(shares[16].astype(jnp.bfloat16), "seq").astype(jnp.float32),
    )
    return (
        result_win,
        grad_input,
        totals[0],
        totals[1],
        totals[2],
        totals[3],
        totals[4],
        totals[5],
        totals[6],
        totals[7],
        totals[8],
        totals[9],
        totals[10],
        totals[11],
        totals[12],
        totals[13],
        totals[14],
        totals[15],
        totals[16],
    )


def solution(mesh):
    in_specs = (
        P("dp", "seq", None),
        P("dp", "seq", None),
        P(),
        P(),
        P(),
        P(),
        P(),
        P(),
        P(),
        P(),
        P(),
        P(),
        P(),
        P(),
        P(),
        P(),
        P(),
        P(),
        P(),
        P(),
        P(),
    )
    out_specs = (
        P("dp", "seq", None),
        P("dp", "seq", None),
        P(None, "dp", None),
        P("dp"),
        P(None, "dp"),
        P("dp"),
        P(None, "dp"),
        P(None, "dp"),
        P("dp"),
        P(None, "dp"),
        P("dp"),
        P("dp"),
        P("dp"),
        P(None, "dp"),
        P("dp"),
        P(None, "dp"),
        P("dp"),
        P("dp"),
        P("dp"),
    )
    return jax.shard_map(
        on_device, mesh=mesh, in_specs=in_specs, out_specs=out_specs, check_vma=False
    )
```

profile of v0, /device:TPU:0, one launch (start us, length us, event | category | flops | bytes accessed | tf_op | source)
XLA Modules:
  0.0 2006.6 jit_solution(2178016305353547820)
XLA Ops:
  571.9 8.3 fusion.42
  622.3 9.5 fusion.34
  668.6 11.2 fusion.122
  697.3 58.9 %all-gather.5.cloned.1.call-done = bf16[2,1024,768]{2,1,0:T(8,128)(2,1)} async-done(((bf16[2,256,768]{2,1,0:T(8,128)(2,1)}), bf16[2,1024,768]{2,1,0:T(8,128)(2,1)}) %all-gather.5.cloned.1.call-update) | async-done | bytes 3145744 | tf_op jit(solution)/shard_map/all_gather | solution.py:169
  778.6 42.0 %all-gather.3.cloned.1.call-done = bf16[2,1024,768]{2,1,0:T(8,128)(2,1)} async-done(((bf16[2,256,768]{2,1,0:T(8,128)(2,1)}), bf16[2,1024,768]{2,1,0:T(8,128)(2,1)}) %all-gather.3.cloned.1.call-update) | async-done | bytes 3145744 | tf_op jit(solution)/shard_map/all_gather | solution.py:170
  825.3 8.6 fusion.84
  847.9 14.7 fusion.54
  894.2 21.3 %multiply_reduce_fusion = (f32[2,12,256]{2,1,0:T(8,128)}, f32[2,12,256]{2,1,0:T(8,128)}, f32[2,12,256,512]{3,2,1,0:T(8,128)}) fusion(f32[2,12,256]{2,1,0:T(8,128)} %copy-done.310, f32[2,12,256]{2,1,0:T(8,128)} %copy-done.300, f32[2,12,256,512]{3,2,1,0:T(8,128)} %copy-done.4, pred[2,256,512]{2,1,0:T(8,128)(4,1)} %copy-done.28, ...), kind=kOutput, calls=%fused_computation.302 | convolution fusion | flops 446681088 | bytes 53329920 | tf_op jit(solution)/shard_map/wqhd,wkhd->whqk/dot_general | solution.py:245
  916.2 18.2 multiply_convert_fusion.1
  1005.7 56.3 %reduce-scatter.14.cloned.1.call-done = bf16[2,256,768]{1,2,0:T(8,128)(2,1)} async-done(((bf16[2,1024,768]{1,2,0:T(8,128)(2,1)}), bf16[2,256,768]{1,2,0:T(8,128)(2,1)}) %reduce-scatter.14.cloned.1.call-update) | async-done | bytes 786448 | tf_op jit(solution)/shard_map/reduce_scatter | solution.py:296
  1074.1 14.8 fusion.75
  1088.9 13.5 fusion.74
  1102.4 13.6 fusion.80
  1116.0 13.9 fusion.76
  1131.8 13.8 fusion.79
  1145.7 13.6 fusion.78
  1159.6 13.5 fusion.77
  1173.2 13.8 fusion.81
  1187.2 24.3 %all-reduce.11 = (bf16[768]{0:T(1024)(128)(2,1)S(1)}, bf16[768]{0:T(1024)(128)(2,1)S(1)}, bf16[768]{0:T(1024)(128)(2,1)S(1)}, bf16[768]{0:T(1024)(128)(2,1)S(1)}...) all-reduce(bf16[768]{0:T(1024)(128)(2,1)S(1)} %copy-done.471, ...), channel_id=5, replica_groups=mesh['dp'=8,'seq'=4] {'dp'}, use_global_device_ids=true, to_apply=%region_19.20.clone | all-reduce | flops 9984 | bytes 39936
  1212.3 12.7 all-reduce.12
  1230.2 11.2 copy.1333
  1241.4 11.2 copy.1332
  1252.6 11.3 copy.1338
  1263.8 11.3 copy.1334
  1275.1 11.1 copy.1337
  1286.2 11.2 copy.1336
  1297.4 11.2 copy.1335
  1308.6 11.2 copy.1339
  1321.1 66.6 %concatenate.298 = bf16[128,16,48,48]{0,3,2,1:T(8,128)(2,1)} concatenate(bf16[16,16,48,48]{0,3,2,1:T(8,128)(2,1)} %copy.1332, bf16[16,16,48,48]{0,3,2,1:T(8,128)(2,1)} %copy.1333, bf16[16,16,48,48]{0,3,2,1:T(8,128)(2,1)} %copy.1334, bf16[16,16,48,48]{0,3,2,1:T(8,128)(2,1)} %copy.1335, bf16[16,16,48,48]{0,3,2,1:T(8,128)(2,1)} %copy.1336, bf16[16,16,48,48]{0,3,2,1:T(8,128)(2,1)} %copy.1337, ...), dimensions={0} | concatenate | bytes 18874368 | tf_op jit(solution)/shard_map/concatenate | solution.py:330
  1879.4 9.4 fusion.16
  1888.8 9.4 fusion.121
  1903.8 87.5 %all-reduce.16.cloned.1.call-done = (bf16[128,96,48]{0,2,1:T(8,128)(2,1)}, bf16[768,96]{0,1:T(8,128)(2,1)}, bf16[768,96]{0,1:T(8,128)(2,1)}, bf16[768,96]{0,1:T(...) async-done(((bf16[128,96,48]{0,2,1:T(8,128)(2,1)}, bf16[768,96]{0,1:T(8,128)(2,1)}, bf16[768,96]{0,1:T(8,128)(2,1)}, ...) | async-done | bytes 2949136 | tf_op jit(solution)/shard_map/psum | solution.py:410
  (1808 shorter events, 1328.2 us)
Async XLA Ops:
  7.2 684.5 %copy-start = (bf16[768,768]{1,0:T(8,128)(2,1)S(1)}, bf16[768,768]{1,0:T(8,128)(2,1)}, u32[]{:S(2)}) copy-start(bf16[768,768]{1,0:T(8,128)(2,1)} %param.30) | copy-start | bytes 3538948
  7.2 749.1 %all-gather.5.cloned.1.call-start = ((), (), s32[]{:S(2)}) async-start(), calls=%async_computation.10 | async-start | bytes 3932160 | tf_op jit(solution)/shard_map/all_gather | solution.py:169
  8.9 135.3 %copy-start.22 = (s32[2,1024]{1,0:T(2,128)}, s32[2,1024]{1,0:T(2,128)S(1)}, u32[]{:S(2)}) copy-start(s32[2,1024]{1,0:T(2,128)S(1)} %select_select_fusion) | copy-start | bytes 24580
  9.6 134.6 %copy-start.30 = (s32[2,256]{1,0:T(2,128)}, s32[2,256]{1,0:T(2,128)S(1)}, u32[]{:S(2)}) copy-start(s32[2,256]{1,0:T(2,128)S(1)} %get-tuple-element.66) | copy-start | bytes 6148
  10.9 136.1 %copy-start.302 = (pred[2,256]{1,0:T(4,128)(4,1)}, pred[2,256]{1,0:T(4,128)(4,1)S(1)}, u32[]{:S(2)}) copy-start(pred[2,256]{1,0:T(4,128)(4,1)S(1)} %get-tuple-element.768) | copy-start | bytes 1540
  13.9 133.8 %collective-permute-start = (bf16[2,64,768]{2,1,0:T(8,128)(2,1)}, bf16[2,64,768]{2,1,0:T(8,128)(2,1)S(1)}, u32[]{:S(2)}, u32[]{:S(2)}) collective-permute-start(bf16[2,64,768]{2,1,0:T(8,128)(2,1)} %get-tuple-element.591), channel_id=1, source_target_pairs={{0,1},{1,2},{2,3},{4,5},{5,6},{6,7},{8,9},{9,10},{10,11},{12,13},{... | collective-permute-start | bytes 589832 | tf_op jit(solution)/shard_map/ppermute | solution.py:19
  18.8 174.7 %collective-permute-start.1 = (bf16[2,64,768]{2,1,0:T(8,128)(2,1)}, bf16[2,64,768]{2,1,0:T(8,128)(2,1)S(1)}, u32[]{:S(2)}, u32[]{:S(2)}) collective-permute-start(bf16[2,64,768]{2,1,0:T(8,128)(2,1)} %get-tuple-element.592), channel_id=1, source_target_pairs={{1,0},{2,1},{3,2},{5,4},{6,5},{7,6},{9,8},{10,9},{11,10},{13,12},{... | collective-permute-start | bytes 589832 | tf_op jit(solution)/shard_map/ppermute | solution.py:22
  112.1 32.8 %copy-start.459 = (pred[2,256]{1,0:T(4,128)(4,1)S(1)}, pred[2,256]{1,0:T(4,128)(4,1)}, u32[]{:S(2)}) copy-start(pred[2,256]{1,0:T(4,128)(4,1)} %get-tuple-element.282) | copy-start | bytes 1540
  112.1 34.2 %copy-start.460 = (pred[2,256]{1,0:T(4,128)(4,1)S(1)}, pred[2,256]{1,0:T(4,128)(4,1)}, u32[]{:S(2)}) copy-start(pred[2,256]{1,0:T(4,128)(4,1)} %get-tuple-element.65) | copy-start | bytes 1540
  112.1 34.2 %copy-start.463 = (pred[2,256]{1,0:T(4,128)(4,1)S(1)}, pred[2,256]{1,0:T(4,128)(4,1)}, u32[]{:S(2)}) copy-start(pred[2,256]{1,0:T(4,128)(4,1)} %get-tuple-element.312) | copy-start | bytes 1540
  112.1 34.9 %copy-start.458 = (pred[2,256]{1,0:T(4,128)(4,1)S(1)}, pred[2,256]{1,0:T(4,128)(4,1)}, u32[]{:S(2)}) copy-start(pred[2,256]{1,0:T(4,128)(4,1)} %get-tuple-element.620) | copy-start | bytes 1540
  112.1 34.9 %copy-start.461 = (pred[2,256]{1,0:T(4,128)(4,1)S(1)}, pred[2,256]{1,0:T(4,128)(4,1)}, u32[]{:S(2)}) copy-start(pred[2,256]{1,0:T(4,128)(4,1)} %get-tuple-element.602) | copy-start | bytes 1540
  112.1 34.9 %copy-start.462 = (pred[2,256]{1,0:T(4,128)(4,1)S(1)}, pred[2,256]{1,0:T(4,128)(4,1)}, u32[]{:S(2)}) copy-start(pred[2,256]{1,0:T(4,128)(4,1)} %get-tuple-element.604) | copy-start | bytes 1540
  571.9 22.7 %slice-start = ((s8[12582912]{0:T(1024)(128)(4,1)}), s8[4194304]{0:T(1024)(128)(4,1)S(1)}, s32[]{:S(2)}) async-start(s8[12582912]{0:T(1024)(128)(4,1)} %bitcast.568), calls=%async_computation.21 | async-start | bytes 8388608
  690.4 130.3 %all-gather.3.cloned.1.call-start = ((), (), s32[]{:S(2)}) async-start(), calls=%async_computation.9 | async-start | bytes 3932160 | tf_op jit(solution)/shard_map/all_gather | solution.py:170
  693.4 308.8 %reduce-scatter.12.cloned.1.call-start = ((), (), s32[]{:S(2)}) async-start(), calls=%async_computation.11 | async-start | bytes 3932160 | tf_op jit(solution)/shard_map/reduce_scatter | solution.py:293
  694.4 139.5 %copy-start.26 = (pred[2,256,512]{2,1,0:T(8,128)(4,1)}, pred[2,256,512]{2,1,0:T(8,128)(4,1)S(1)}, u32[]{:S(2)}) copy-start(pred[2,256,512]{2,1,0:T(8,128)(4,1)S(1)} %compare_and_fusion.1) | copy-start | bytes 786436
  694.7 130.6 %copy-start.28 = (pred[2,256,512]{2,1,0:T(8,128)(4,1)}, pred[2,256,512]{2,1,0:T(8,128)(4,1)S(1)}, u32[]{:S(2)}) copy-start(pred[2,256,512]{2,1,0:T(8,128)(4,1)S(1)} %compare_and_fusion) | copy-start | bytes 786436
  767.6 66.3 %copy-start.300 = (f32[2,12,256]{2,1,0:T(8,128)}, f32[2,12,256]{2,1,0:T(8,128)S(1)}, u32[]{:S(2)}) copy-start(f32[2,12,256]{2,1,0:T(8,128)S(1)} %get-tuple-element.596) | copy-start | bytes 73732
  778.6 55.4 %copy-start.310 = (f32[2,12,256]{2,1,0:T(8,128)}, f32[2,12,256]{2,1,0:T(8,128)S(1)}, u32[]{:S(2)}) copy-start(f32[2,12,256]{2,1,0:T(8,128)S(1)} %add_maximum_fusion) | copy-start | bytes 73732
  940.4 121.6 %reduce-scatter.14.cloned.1.call-start = ((), (), s32[]{:S(2)}) async-start(), calls=%async_computation.12 | async-start | bytes 3932160 | tf_op jit(solution)/shard_map/reduce_scatter | solution.py:296
  958.7 916.1 %reduce-scatter.28.cloned.1.call-start = ((), (), s32[]{:S(2)}) async-start(), calls=%async_computation.19 | async-start | bytes 5308416
  972.4 904.6 %reduce-scatter.18.cloned.1.call-start = ((), (), s32[]{:S(2)}) async-start(), calls=%async_computation.14 | async-start | bytes 1327104 | tf_op jit(solution)/shard_map/reduce_scatter | solution.py:363
  985.1 891.9 %reduce-scatter.24.cloned.1.call-start = ((), (), s32[]{:S(2)}) async-start(), calls=%async_computation.17 | async-start | bytes 1327104 | tf_op jit(solution)/shard_map/reduce_scatter | solution.py:378
  988.4 888.6 %reduce-scatter.26.cloned.1.call-start = ((), (), s32[]{:S(2)}) async-start(), calls=%async_computation.18 | async-start | bytes 5308416 | tf_op jit(solution)/shard_map/reduce_scatter | solution.py:396
  995.6 881.4 %reduce-scatter.20.cloned.1.call-start = ((), (), s32[]{:S(2)}) async-start(), calls=%async_computation.15 | async-start | bytes 1327104 | tf_op jit(solution)/shard_map/reduce_scatter | solution.py:369
  998.9 63.1 %copy-start.319 = (f32[2,256]{1,0:T(2,128)S(1)}, f32[2,256]{1,0:T(2,128)}, u32[]{:S(2)}) copy-start(f32[2,256]{1,0:T(2,128)} %copy-done.318) | copy-start | bytes 6148
  1069.2 318.8 %collective-permute-start.2 = (bf16[2,64,768]{2,1,0:T(8,128)(2,1)}, bf16[2,64,768]{2,1,0:T(8,128)(2,1)S(1)}, u32[]{:S(2)}, u32[]{:S(2)}) collective-permute-start(bf16[2,64,768]{2,1,0:T(8,128)(2,1)} %get-tuple-element.589), channel_id=1, source_target_pairs={{1,0},{2,1},{3,2},{5,4},{6,5},{7,6},{9,8},{10,9},{11,10},{13,12},{... | collective-permute-start | bytes 589832 | tf_op jit(solution)/shard_map/ppermute | solution.py:22
  1130.0 747.1 %reduce-scatter.22.cloned.1.call-start = ((), (), s32[]{:S(2)}) async-start(), calls=%async_computation.16 | async-start | bytes 1327104 | tf_op jit(solution)/shard_map/reduce_scatter | solution.py:372
  1159.3 717.8 %reduce-scatter.16.cloned.1.call-start = ((), (), s32[]{:S(2)}) async-start(), calls=%async_computation.13 | async-start | bytes 10616832 | tf_op jit(solution)/shard_map/reduce_scatter | solution.py:357
  1319.8 251.0 %collective-permute-start.3 = (bf16[2,64,768]{2,1,0:T(8,128)(2,1)}, bf16[2,64,768]{2,1,0:T(8,128)(2,1)S(1)}, u32[]{:S(2)}, u32[]{:S(2)}) collective-permute-start(bf16[2,64,768]{2,1,0:T(8,128)(2,1)} %get-tuple-element.590), channel_id=1, source_target_pairs={{0,1},{1,2},{2,3},{4,5},{5,6},{6,7},{8,9},{9,10},{10,11},{12,13},{... | collective-permute-start | bytes 589832 | tf_op jit(solution)/shard_map/ppermute | solution.py:19
  1387.8 603.6 %all-reduce.16.cloned.1.call-start = ((), (), s32[]{:S(2)}) async-start(), calls=%async_computation.20 | async-start | bytes 5898240 | tf_op jit(solution)/shard_map/psum | solution.py:410
  (485 other events, 2383.5 us)
Sparse Core Ops, SparseCore 0:
  690.5 65.7 all-gather.4
  758.4 62.1 all-gather.2
  940.5 58.9 reduce-scatter.11
  1001.6 60.2 reduce-scatter.13
  1065.2 53.9 reduce-scatter.27
  1123.2 36.7 reduce-scatter.17
  1163.2 36.8 reduce-scatter.23
  1204.0 53.9 reduce-scatter.25
  1261.7 36.7 reduce-scatter.19
  1301.9 36.7 reduce-scatter.21
  1387.9 73.5 reduce-scatter.15
  1877.2 114.0 all-reduce.15
where the time goes:
time: 2030 us; the launch traced here: 2010 us
  local copies, waits for them, and re-layouts  1060 us (52%)
  matrix products  375 us (18%)
  other arithmetic  260 us (13%)
  waiting for transfers between devices  245 us (12%)
  blocking collectives  37 us (2%)
    select_n x128, local copies, waits for them, and re-layouts, tap_window(): jnp.where(tap_mask(kernel_tap_index)[:, :, None], rimmed[:, kernel_tap_in...  286 us
    select_n x128, local copies, waits for them, and re-layouts, on_device(): jnp.where(back_mask(kernel_tap_index)[:, :, None], grad_rim[:, margin - k...  247 us
    unnamed x1255, local copies, waits for them, and re-layouts  242 us
    dot_general x8, matrix products, on_device(): jnp.einsum('kwtgi,wtgo->kgio', tap_window(block_index), grad_grouped, pre...  111 us
    slice x17, local copies, waits for them, and re-layouts, on_device(): grouped_weight[block_index * kernel_tap_block:(block_index + 1) * kernel_...  93.2 us
    transpose x8, local copies, waits for them, and re-layouts, on_device(): jnp.einsum('kwtgi,wtgo->kgio', tap_window(block_index), grad_grouped, pre...  89.7 us
    psum x1, waiting for transfers between devices, on_device(): lax.psum(shares[0].astype(jnp.bfloat16), 'seq').astype(jnp.float32)  87.5 us
    select_n x33, other arithmetic, tap_window(): jnp.where(tap_mask(kernel_tap_index)[:, :, None], rimmed[:, kernel_tap_in...  76.2 us
  transfers between devices with their start and end apart: 16, of which 4 were waited for; matrix products, arithmetic and copies ran while one was open for 53% of the time, Pallas kernels for 0%

commit v1 on v0

v1 whole, which is shorter than its diff:
```python
import functools
import jax
import jax.numpy as jnp
from jax import lax
from jax.experimental import pallas as pl
from jax.experimental.pallas import tpu as pltpu
from jax.sharding import PartitionSpec as P


DK = 16

def prep_kernel(w_ref, wn_ref, wt_ref):
    gw = w_ref.shape[1]
    nb = w_ref.shape[0] // DK
    parts = [w_ref[DK*b:DK*(b+1)].reshape(DK*gw, gw) for b in range(nb)]
    wn = jnp.concatenate(parts, axis=1)
    wn_ref[0] = wn
    wt_ref[0] = wn.T

def prep(w):
    k, width, gw = w.shape
    g = width // gw
    nb = k // DK
    return pl.pallas_call(
        prep_kernel,
        grid=(g,),
        in_specs=[pl.BlockSpec((k, gw, gw), lambda i: (0, i, 0))],
        out_specs=[pl.BlockSpec((1, DK*gw, nb*gw), lambda i: (i, 0, 0)),
                   pl.BlockSpec((1, nb*gw, DK*gw), lambda i: (i, 0, 0))],
        out_shape=[jax.ShapeDtypeStruct((g, DK*gw, nb*gw), w.dtype),
                   jax.ShapeDtypeStruct((g, nb*gw, DK*gw), w.dtype)],
        name="prep",
    )(w)

def conv_kernel(xt_ref, wt_ref, sel_ref, out_ref, a0_ref, z_ref, *, nb, gw, F, nbound, roll32):
    tin = xt_ref.shape[1]
    x = xt_ref[...]
    if roll32:
        x = x.astype(jnp.float32)
    for dk in range(DK):
        r = x if dk == 0 else pltpu.roll(x, tin - dk, 1)
        a0_ref[gw*dk:gw*(dk+1), :] = r.astype(a0_ref.dtype)
    z_ref[...] = jnp.dot(wt_ref[0], a0_ref[...], preferred_element_type=jnp.float32)
    acc = z_ref[0:gw, :]
    for b in range(1, nb):
        acc = acc + pltpu.roll(z_ref[gw*b:gw*(b+1), :], tin - DK*b, 1)
    out = acc[:, :F]
    for n in range(1, nbound+1):
        sh = pltpu.roll(acc, tin - 64*n, 1)[:, :F]
        out = jnp.where(sel_ref[n:n+1, :] > 0, sh, out)
    out_ref[...] = out

def conv(xt, wt, sel, F, roll32=False):
    width, tin = xt.shape
    g, nbgw, dkgw = wt.shape
    gw = width // g
    nb = nbgw // gw
    nbound = sel.shape[0] - 1
    return pl.pallas_call(
        functools.partial(conv_kernel, nb=nb, gw=gw, F=F, nbound=nbound, roll32=roll32),
        grid=(g,),
        in_specs=[pl.BlockSpec((gw, tin), lambda i: (i, 0)),
                  pl.BlockSpec((1, nbgw, dkgw), lambda i: (i, 0, 0)),
                  pl.BlockSpec(sel.shape, lambda i: (0, 0))],
        out_specs=pl.BlockSpec((gw, F), lambda i: (i, 0)),
        out_shape=jax.ShapeDtypeStruct((width, F), jnp.float32),
        scratch_shapes=[pltpu.VMEM((dkgw, tin), jnp.bfloat16), pltpu.VMEM((nbgw, tin), jnp.float32)],
        name="conv_fwd",
    )(xt, wt, sel)

def dx_kernel(dt_ref, wn_ref, sel_ref, out_ref, ds_ref, y_ref, *, nb, gw, F, nbound, roll32):
    tin = dt_ref.shape[1]
    d = dt_ref[...]
    if roll32:
        d = d.astype(jnp.float32)
    for b in range(nb):
        r = d if b == 0 else pltpu.roll(d, DK*b, 1)
        ds_ref[gw*b:gw*(b+1), :] = r.astype(ds_ref.dtype)
    y_ref[...] = jnp.dot(wn_ref[0], ds_ref[...], preferred_element_type=jnp.float32)
    acc = y_ref[0:gw, :]
    for dk in range(1, DK):
        acc = acc + pltpu.roll(y_ref[gw*dk:gw*(dk+1), :], dk, 1)
    acc = acc[:, 128:]
    out = acc[:, :F]
    for n in range(1, nbound+1):
        sh = pltpu.roll(acc, acc.shape[1] - 64*n, 1)[:, :F]
        out = jnp.where(sel_ref[n:n+1, :] > 0, sh, out)
    out_ref[...] = out

def conv_dx(dt, wn, sel, F, roll32=False):
    width, tin = dt.shape
    g, dkgw, nbgw = wn.shape
    gw = width // g
    nb = nbgw // gw
    nbound = sel.shape[0] - 1
    return pl.pallas_call(
        functools.partial(dx_kernel, nb=nb, gw=gw, F=F, nbound=nbound, roll32=roll32),
        grid=(g,),
        in_specs=[pl.BlockSpec((gw, tin), lambda i: (i, 0)),
                  pl.BlockSpec((1, dkgw, nbgw), lambda i: (i, 0, 0)),
                  pl.BlockSpec(sel.shape, lambda i: (0, 0))],
        out_specs=pl.BlockSpec((gw, F), lambda i: (i, 0)),
        out_shape=jax.ShapeDtypeStruct((width, F), jnp.float32),
        scratch_shapes=[pltpu.VMEM((nbgw, tin), jnp.bfloat16), pltpu.VMEM((dkgw, tin), jnp.float32)],
        name="conv_dx",
    )(dt, wn, sel)

def dw_kernel(xt_ref, dt_ref, out_ref, a0_ref, ds_ref, *, nb, gw, roll32):
    tin = xt_ref.shape[2]
    tout = dt_ref.shape[2]
    x = xt_ref[0]
    d = dt_ref[0]
    if roll32:
        x = x.astype(jnp.float32); d = d.astype(jnp.float32)
    d = jnp.concatenate([d, jnp.zeros((gw, tin - tout), d.dtype)], axis=1)
    for dk in range(DK):
        r = x if dk == 0 else pltpu.roll(x, tin - dk, 1)
        a0_ref[gw*dk:gw*(dk+1), :] = r.astype(a0_ref.dtype)
    for b in range(nb):
        r = d if b == 0 else pltpu.roll(d, DK*b, 1)
        ds_ref[gw*b:gw*(b+1), :] = r.astype(ds_ref.dtype)
    p = lax.dot_general(ds_ref[...], a0_ref[...], (((1,), (1,)), ((), ())), preferred_element_type=jnp.float32)
    first = pl.program_id(1) == 0
    @pl.when(first)
    def _():
        out_ref[0] = p
    @pl.when(jnp.logical_not(first))
    def _():
        out_ref[0] += p

def conv_dw(xt, dt, gw, nb, roll32=False):
    m, chans, tin = xt.shape
    tout = dt.shape[2]
    g = chans // gw
    return pl.pallas_call(
        functools.partial(dw_kernel, nb=nb, gw=gw, roll32=roll32),
        grid=(g, m),
        in_specs=[pl.BlockSpec((1, gw, tin), lambda i, j: (j, i, 0)),
                  pl.BlockSpec((1, gw, tout), lambda i, j: (j, i, 0))],
        out_specs=pl.BlockSpec((1, nb*gw, DK*gw), lambda i, j: (i, 0, 0)),
        out_shape=jax.ShapeDtypeStruct((g, nb*gw, DK*gw), jnp.float32),
        scratch_shapes=[pltpu.VMEM((DK*gw, tin), jnp.bfloat16), pltpu.VMEM((nb*gw, tin), jnp.bfloat16)],
        name="conv_dw",
    )(xt, dt)


def finish_kernel(p_ref, out_ref, e_ref, q_ref, *, nb, gw):
    dkgw = DK * gw

    @pl.when(pl.program_id(0) == 0)
    def _():
        row = lax.broadcasted_iota(jnp.int32, (dkgw, dkgw), 0)
        col = lax.broadcasted_iota(jnp.int32, (1, dkgw), 1)
        e_ref[...] = (row == (col % DK) * gw + col // DK).astype(e_ref.dtype)

    q_ref[...] = jnp.dot(p_ref[0], e_ref[...], preferred_element_type=jnp.float32)
    per = 128 // DK
    lane_block = lax.broadcasted_iota(jnp.int32, (gw, 128), 1) // DK
    for tile in range(dkgw // 128):
        outs = [None] * per
        for b in range(nb):
            piece = q_ref[gw*b:gw*(b+1), 128*tile:128*(tile+1)]
            for i in range(per):
                turn = (b - i) % per
                moved = piece if turn == 0 else pltpu.roll(piece, DK * turn, 1)
                outs[i] = moved if outs[i] is None else jnp.where(lane_block == b, moved, outs[i])
        for i in range(per):
            out_ref[tile * per + i] = outs[i]

def finish_dw(p, gw, nb):
    g = p.shape[0]
    assert nb * DK == 128
    out = pl.pallas_call(
        functools.partial(finish_kernel, nb=nb, gw=gw),
        grid=(g,),
        in_specs=[pl.BlockSpec((1, nb*gw, DK*gw), lambda i: (i, 0, 0))],
        out_specs=pl.BlockSpec((gw, gw, 128), lambda i: (i, 0, 0)),
        out_shape=jax.ShapeDtypeStruct((g*gw, gw, 128), jnp.float32),
        scratch_shapes=[pltpu.VMEM((DK*gw, DK*gw), jnp.bfloat16), pltpu.VMEM((nb*gw, DK*gw), jnp.float32)],
        name="finish_dw",
    )(p)
    return jnp.transpose(out, (2, 0, 1))

HEAD = 64

def nt(a, b):
    return lax.dot_general(a, b, (((1,), (1,)), ((), ())), preferred_element_type=jnp.float32)

def attn_fwd_kernel(*refs, P, chunk):
    q_ref, qc_ref, kc_ref = refs[:3]
    k_refs = refs[3:3+P]
    v_refs = refs[3+P:3+2*P]
    o_ref, lse_ref = refs[3+2*P:5+2*P]
    ka_ref, = refs[5+2*P:]
    F = q_ref.shape[0]
    low_k = lax.broadcasted_iota(jnp.int32, (F, 128), 1) < HEAD
    low_q = lax.broadcasted_iota(jnp.int32, (chunk, 128), 1) < HEAD
    for h in range(2):
        pick = low_k if h == 0 else jnp.logical_not(low_k)
        for p in range(P):
            ka_ref[h, p*F:(p+1)*F, :] = jnp.where(pick, k_refs[p][...], kc_ref[p*F:(p+1)*F, :])
    for c in range(F // chunk):
        rows = slice(c*chunk, (c+1)*chunk)
        q = q_ref[rows, :] * jnp.asarray(0.125, jnp.bfloat16)
        outs, lses = [], []
        for h in range(2):
            pick = low_q if h == 0 else jnp.logical_not(low_q)
            qa = jnp.where(pick, q, qc_ref[rows, :])
            s = nt(qa, ka_ref[h])
            m = jnp.maximum(jnp.max(s, axis=1, keepdims=True), -1e20)
            e = jnp.exp(s - m)
            l = jnp.maximum(jnp.sum(e, axis=1, keepdims=True), 1.0)
            pb = (e * (1.0 / l)).astype(jnp.bfloat16)
            o = sum(jnp.dot(pb[:, p*F:(p+1)*F], v_refs[p][...], preferred_element_type=jnp.float32) for p in range(P))
            outs.append(o)
            lses.append(m + jnp.log(l))
        o_ref[rows, :] = jnp.where(low_q, outs[0], outs[1]).astype(o_ref.dtype)
        lse_ref[rows, :] = jnp.where(low_q, lses[0], lses[1])

def attn_fwd(q, kvs, qc, kc, chunk=128):
    F, W = q.shape
    P = len(kvs)
    T = P * F
    npair = W // 128
    return pl.pallas_call(
        functools.partial(attn_fwd_kernel, P=P, chunk=min(chunk, F)),
        grid=(npair,),
        in_specs=[pl.BlockSpec((F, 128), lambda a: (0, a)),
                  pl.BlockSpec((F, 128), lambda a: (0, 0)),
                  pl.BlockSpec((T, 128), lambda a: (0, 0))]
                 + [pl.BlockSpec((F, 128), lambda a: (0, a))] * P
                 + [pl.BlockSpec((F, 128), lambda a, n=npair: (0, a + n))] * P,
        out_specs=[pl.BlockSpec((F, 128), lambda a: (0, a)), pl.BlockSpec((F, 128), lambda a: (0, a))],
        out_shape=[jax.ShapeDtypeStruct((F, W), jnp.bfloat16), jax.ShapeDtypeStruct((F, W), jnp.float32)],
        scratch_shapes=[pltpu.VMEM((2, T, 128), jnp.bfloat16)],
        name="attn_fwd",
    )(q, qc, kc, *kvs, *kvs)

def attn_bwd_kernel(*refs, P, chunk):
    q_ref, do_ref, o_ref, lse_ref, qc_ref, kc_ref = refs[:6]
    k_refs = refs[6:6+P]
    v_refs = refs[6+P:6+2*P]
    dq_ref = refs[6+2*P]
    dk_refs = refs[7+2*P:7+3*P]
    dv_refs = refs[7+3*P:7+4*P]
    F = q_ref.shape[0]
    low_q = lax.broadcasted_iota(jnp.int32, (F, 128), 1) < HEAD
    low_c = lax.broadcasted_iota(jnp.int32, (chunk, 128), 1) < HEAD
    q = q_ref[...] * jnp.asarray(0.125, jnp.bfloat16)
    do = do_ref[...]
    lse_t = lse_ref[...].T
    prod_t = (do.astype(jnp.float32) * o_ref[...].astype(jnp.float32)).T
    lse_row = [lse_t[h*HEAD:h*HEAD+1, :] for h in range(2)]
    delta_row = [jnp.sum(prod_t[h*HEAD:(h+1)*HEAD, :], axis=0, keepdims=True) for h in range(2)]
    qa = [jnp.where(low_q if h == 0 else jnp.logical_not(low_q), q, qc_ref[...]) for h in range(2)]
    zero = jnp.zeros((), jnp.bfloat16)
    dqt = [jnp.zeros((HEAD, F), jnp.float32) for _ in range(2)]
    for p in range(P):
        for c in range(F // chunk):
            rows = slice(c*chunk, (c+1)*chunk)
            k = k_refs[p][rows, :]
            v = v_refs[p][rows, :]
            kc = kc_ref[p*F + c*chunk: p*F + (c+1)*chunk, :]
            kt = k.T
            dks, dvs = [], []
            for h in range(2):
                pick = low_c if h == 0 else jnp.logical_not(low_c)
                st = nt(jnp.where(pick, k, kc), qa[h])
                pt = jnp.exp(st - lse_row[h])
                dpt = nt(jnp.where(pick, v, zero), do)
                dst = (pt * (dpt - delta_row[h])).astype(jnp.bfloat16)
                dvs.append(jnp.dot(pt.astype(jnp.bfloat16), do, preferred_element_type=jnp.float32))
                dks.append(jnp.dot(dst, q, preferred_element_type=jnp.float32))
                dqt[h] = dqt[h] + jnp.dot(kt[h*HEAD:(h+1)*HEAD, :], dst, preferred_element_type=jnp.float32)
            dk_refs[p][rows, :] = jnp.where(low_c, dks[0], dks[1]).astype(dk_refs[p].dtype)
            dv_refs[p][rows, :] = jnp.where(low_c, dvs[0], dvs[1]).astype(dv_refs[p].dtype)
    dq = jnp.concatenate(dqt, axis=0).T * 0.125
    dq_ref[...] = dq.astype(dq_ref.dtype)

def attn_bwd(q, do, o, lse, kvs, qc, kc, chunk=128):
    F, W = q.shape
    P = len(kvs)
    T = P * F
    npair = W // 128
    own = pl.BlockSpec((F, 128), lambda a: (0, a))
    dts = [jnp.float32] + [jnp.bfloat16] * (P - 1)
    return pl.pallas_call(
        functools.partial(attn_bwd_kernel, P=P, chunk=min(chunk, F)),
        grid=(npair,),
        in_specs=[own, own, own, own,
                  pl.BlockSpec((F, 128), lambda a: (0, 0)),
                  pl.BlockSpec((T, 128), lambda a: (0, 0))]
                 + [own] * P
                 + [pl.BlockSpec((F, 128), lambda a, n=npair: (0, a + n))] * P,
        out_specs=[own] * (1 + 2*P),
        out_shape=[jax.ShapeDtypeStruct((F, W), jnp.bfloat16)] + [jax.ShapeDtypeStruct((F, W), t) for t in dts + dts],
        name="attn_bwd",
    )(q, do, o, lse, qc, kc, *kvs, *kvs)

HALO = 64
UTT_LEAST = 256
root_half = 0.7071067811865476
inv_root_two_pi = 0.3989422804014327
f32 = jnp.float32
bf16 = jnp.bfloat16


def layer_norm(hidden):
    centred = hidden - jnp.mean(hidden, axis=-1, keepdims=True)
    inv_scale = lax.rsqrt(jnp.mean(centred * centred, axis=-1, keepdims=True) + 1e-05)
    return (centred * inv_scale, inv_scale)


def norm_back(grad_normed, normed, inv_scale):
    return inv_scale * (
        grad_normed
        - jnp.mean(grad_normed, axis=-1, keepdims=True)
        - normed * jnp.mean(grad_normed * normed, axis=-1, keepdims=True)
    )


def gelu_slope(entries):
    return (
        0.5 * (1.0 + lax.erf(entries * root_half))
        + entries * jnp.exp(-0.5 * entries * entries) * inv_root_two_pi
    )


def mm(a, b):
    return jnp.dot(a, b, preferred_element_type=f32)


def mm_back(a, b):
    return lax.dot_general(a, b, (((1,), (1,)), ((), ())), preferred_element_type=f32)


def wgrad(a, b):
    return lax.dot_general(a, b, (((0,), (0,)), ((), ())), preferred_element_type=f32)


class Plan:
    def __init__(self, dp, seq, rows_dev):
        self.dp, self.seq, self.n = dp, seq, rows_dev
        self.q = seq // (2 * rows_dev)
        self.P = 2 * self.q
        assert dp % 2 == 0 and self.q * 2 * rows_dev == seq

    def out_pairs(self, m):
        pairs = []
        for d in range(self.dp):
            for z in range(self.seq):
                rho = self.n * (d % 2) + (z + m) % self.n
                u = z // self.n
                pairs.append((d * self.seq + z, self.member(d // 2, rho, u)))
        return pairs

    def member(self, e, rho, u):
        return (2 * e + u % 2) * self.seq + rho * self.q + u // 2

    def team_pairs(self, shift, wrap):
        pairs = []
        for e in range(self.dp // 2):
            for rho in range(2 * self.n):
                for u in range(self.P):
                    to = u + shift
                    if wrap or 0 <= to < self.P:
                        pairs.append((self.member(e, rho, u), self.member(e, rho, to % self.P)))
        return pairs


BOTH = ("dp", "seq")


def on_device(
    frames,
    output_gradient,
    segments,
    layer_keep,
    conv_weight,
    convolution_bias,
    query_matrix,
    query_offset_bias,
    key_matrix,
    value_matrix,
    value_offset_bias,
    attn_weight,
    attn_bias,
    first_gain,
    first_shift,
    inner_weight,
    inner_bias,
    outer_weight,
    outer_bias,
    second_gain,
    second_shift,
):
    rows_dev, local_len, width = frames.shape
    total_rows, row_len = segments.shape
    dp_count, seq_count = lax.axis_size("dp"), lax.axis_size("seq")
    dp_index, seq_index = lax.axis_index("dp"), lax.axis_index("seq")
    plan = Plan(dp_count, seq_count, rows_dev)
    n, q, team = plan.n, plan.q, plan.P
    F = row_len // team
    taps, _, gw = conv_weight.shape
    tap_blocks = taps // DK
    rho = seq_index // q
    member = (seq_index % q) * 2 + dp_index % 2
    row_id = (dp_index // 2) * (2 * n) + rho

    def to_team(a):
        got = []
        for m in range(n):
            sent = lax.dynamic_index_in_dim(a, (seq_index + m) % n, 0, keepdims=False)
            got.append(lax.ppermute(sent, BOTH, plan.out_pairs(m)))
        j = rho % n
        parts = []
        for w in range(n):
            part = got[0]
            for m in range(1, n):
                part = jnp.where((j - m) % n == w, got[m], part)
            parts.append(part)
        return jnp.concatenate(parts, 0)

    def from_team(a):
        blocks = a.reshape(n, local_len, width)
        j = rho % n
        back = []
        for m in range(n):
            sent = lax.dynamic_index_in_dim(blocks, (j - m) % n, 0, keepdims=False)
            back.append(
                lax.ppermute(sent, BOTH, [(t, s) for s, t in plan.out_pairs(m)])
            )
        parts = []
        for row in range(n):
            part = back[0]
            for m in range(1, n):
                part = jnp.where((seq_index + m) % n == row, back[m], part)
            parts.append(part)
        return jnp.stack(parts, 0)

    def with_halo(a):
        low = lax.ppermute(a[F - HALO :], BOTH, plan.team_pairs(1, False))
        high = lax.ppermute(a[:HALO], BOTH, plan.team_pairs(-1, False))
        return jnp.concatenate([low, a, high], 0)

    weight_nat, weight_tr = prep(conv_weight)

    x = to_team(frames)
    grad_out = to_team(output_gradient)

    seg_row = lax.dynamic_index_in_dim(segments, row_id, 0, keepdims=False)
    keep = (lax.dynamic_index_in_dim(layer_keep, row_id, 0, keepdims=False) > 0).astype(f32)
    ordinal = jnp.where(seg_row > 0, seg_row, jnp.max(seg_row) + 1)
    padded = jnp.pad(jnp.stack([seg_row, ordinal]), ((0, 0), (HALO, HALO)))
    around = lax.dynamic_slice_in_dim(padded, member * F, F + 2 * HALO, 1)
    seg_ext, ord_ext = around[0], around[1]
    seg_loc = seg_ext[HALO : HALO + F]
    ord_loc = ord_ext[HALO : HALO + F]
    live = seg_loc > 0
    gaps = 1 + max(F - 2, 0) // UTT_LEAST
    spread = -(-(F + 2 * HALO + HALO * gaps) // 128) * 128
    out_spread = -(-(F + HALO * gaps) // 128) * 128
    before_loc = ord_loc - ord_loc[0]
    before_ext = jnp.concatenate(
        [
            jnp.where(ord_ext[:HALO] == ord_loc[0], 0, -1),
            before_loc,
            jnp.where(ord_ext[HALO + F :] == ord_loc[F - 1], before_loc[F - 1], -1),
        ]
    )
    select = jnp.stack([(before_loc == k).astype(f32) for k in range(gaps + 1)])

    def pull_apart(a, before, length):
        total = None
        for k in range(gaps + 1):
            tail = length - a.shape[0] - HALO * k
            rows = jnp.pad(a, ((HALO * k, max(tail, 0)), (0, 0)))[:length]
            here = jnp.pad(
                before, (HALO * k, max(tail, 0)), constant_values=-1
            )[:length] == k
            total = jnp.where(here[:, None], rows, 0 if total is None else total)
        return total

    masked_frames = jnp.where(live[:, None], x, jnp.zeros((), x.dtype))
    spread_x = pull_apart(with_halo(masked_frames), before_ext, spread).T
    conv_t = conv(spread_x, weight_tr, select, F)
    x_shares = lax.all_to_all(
        spread_x.reshape(dp_count, width // dp_count, spread), "dp", 0, 0, tiled=True
    )

    conv_before = conv_t.T + convolution_bias
    pos_out = masked_frames.astype(f32) + jax.nn.gelu(conv_before, approximate=False)
    pos_low = pos_out.astype(bf16)
    kv = jnp.concatenate(
        [mm(pos_low, key_matrix), mm(pos_low, value_matrix) + value_offset_bias], 1
    ).astype(bf16)
    kvs = [kv] + [lax.ppermute(kv, BOTH, plan.team_pairs(s, True)) for s in range(1, team)]
    query = (mm(pos_low, query_matrix) + query_offset_bias).astype(bf16)
    seg_blocks = [
        lax.dynamic_slice_in_dim(seg_row, ((member - s) % team) * F, F, 0) for s in range(team)
    ]
    seg_keys = jnp.concatenate(seg_blocks, 0)
    classes = jnp.arange(128, dtype=jnp.int32) % HEAD
    q_codes = (seg_loc[:, None] == classes).astype(bf16)
    k_codes = jnp.where(
        (seg_keys[:, None] == classes) & (classes > 0), 0.0, -1e30
    ).astype(bf16)
    attn_low, lse = attn_fwd(query, kvs, q_codes, k_codes, 256)

    attn_out = mm(attn_low, attn_weight) + attn_bias
    first_normed, first_scale = layer_norm(pos_out + attn_out)
    first_out = first_normed * first_gain + first_shift
    first_low = first_out.astype(bf16)
    inner_pre = mm(first_low, inner_weight) + inner_bias
    inner_low = jax.nn.gelu(inner_pre, approximate=False).astype(bf16)
    outer_out = mm(inner_low, outer_weight) + outer_bias
    second_normed, second_scale = layer_norm(first_out + outer_out)
    second_out = second_normed * second_gain + second_shift
    layer_out = from_team((keep * second_out + (1.0 - keep) * pos_out).astype(bf16))

    grad_win = grad_out.astype(f32)
    grad_layer = keep * grad_win
    grad_second_gain = jnp.sum(grad_layer * second_normed, 0)
    grad_second_shift = jnp.sum(grad_layer, 0)
    grad_second_sum = norm_back(grad_layer * second_gain, second_normed, second_scale)
    grad_outer_low = grad_second_sum.astype(bf16)
    grad_outer_bias = jnp.sum(grad_outer_low.astype(f32), 0)
    grad_outer_t = wgrad(grad_outer_low, inner_low).astype(bf16)
    grad_inner_low = (mm_back(grad_outer_low, outer_weight) * gelu_slope(inner_pre)).astype(bf16)
    grad_inner_bias = jnp.sum(grad_inner_low.astype(f32), 0)
    grad_inner_t = wgrad(grad_inner_low, first_low).astype(bf16)
    grad_first_out = grad_second_sum + mm_back(grad_inner_low, inner_weight)
    grad_first_gain = jnp.sum(grad_first_out * first_normed, 0)
    grad_first_shift = jnp.sum(grad_first_out, 0)
    grad_first_sum = norm_back(grad_first_out * first_gain, first_normed, first_scale)
    grad_attn_low = grad_first_sum.astype(bf16)
    grad_attn_bias = jnp.sum(grad_attn_low.astype(f32), 0)
    grad_attn_t = wgrad(grad_attn_low, attn_low).astype(bf16)
    grad_heads = mm_back(grad_attn_low, attn_weight).astype(bf16)

    grads = attn_bwd(query, grad_heads, attn_low, lse, kvs, q_codes, k_codes, 256)
    grad_query_low = grads[0]
    key_sum, value_sum = grads[1], grads[1 + team]
    for s in range(1, team):
        back = plan.team_pairs(-s, True)
        key_sum = key_sum + lax.ppermute(grads[1 + s], BOTH, back).astype(f32)
        value_sum = value_sum + lax.ppermute(grads[1 + team + s], BOTH, back).astype(f32)
    grad_key_low, grad_value_low = key_sum.astype(bf16), value_sum.astype(bf16)
    grad_query_bias = jnp.sum(grad_query_low.astype(f32), 0)
    grad_value_bias = jnp.sum(grad_value_low.astype(f32), 0)
    grad_query_t = wgrad(grad_query_low, pos_low).astype(bf16)
    grad_key_t = wgrad(grad_key_low, pos_low).astype(bf16)
    grad_value_t = wgrad(grad_value_low, pos_low).astype(bf16)
    grad_pos = (
        grad_first_sum
        + (1.0 - keep) * grad_win
        + mm_back(grad_query_low, query_matrix)
        + mm_back(grad_key_low, key_matrix)
        + mm_back(grad_value_low, value_matrix)
    )
    grad_conv_low = (grad_pos * gelu_slope(conv_before)).astype(bf16)
    grad_conv_bias = jnp.sum(grad_conv_low.astype(f32), 0)

    d_shares = lax.all_to_all(
        pull_apart(grad_conv_low, before_loc, out_spread).T.reshape(
            dp_count, width // dp_count, out_spread
        ),
        "dp", 0, 0, tiled=True,
    )
    spread_d = pull_apart(with_halo(grad_conv_low), before_ext, spread).T
    conv_back = conv_dx(spread_d, weight_nat, select, F).T
    grad_input = from_team(jnp.where(live[:, None], grad_pos + conv_back, 0.0).astype(bf16))

    conv_part = conv_dw(x_shares, d_shares, gw, tap_blocks)
    conv_sum = lax.psum(conv_part.astype(bf16), "seq")
    grad_conv_weight = finish_dw(conv_sum, gw, tap_blocks)

    small = jnp.concatenate(
        [
            v.reshape(dp_count, -1)
            for v in (
                grad_inner_bias, grad_query_bias, grad_value_bias, grad_attn_bias, grad_first_gain,
                grad_first_shift, grad_outer_bias, grad_second_gain, grad_second_shift, grad_conv_bias,
            )
        ],
        1,
    ).astype(bf16)
    small = lax.psum(small, BOTH)
    small = lax.dynamic_index_in_dim(small, dp_index, 0, keepdims=False).astype(f32)
    share = width // dp_count
    ff_share = grad_inner_bias.shape[0] // dp_count
    inner_bias_share = small[:ff_share]
    vecs = [small[ff_share + share * i : ff_share + share * (i + 1)] for i in range(9)]

    def reduced(a):
        a = lax.psum_scatter(a, "dp", scatter_dimension=0, tiled=True)
        return lax.psum(a, "seq").astype(f32).T

    q_g, k_g, v_g, a_g, i_g, o_g = map(
        reduced,
        (grad_query_t, grad_key_t, grad_value_t, grad_attn_t, grad_inner_t, grad_outer_t),
    )
    return (
        layer_out,
        grad_input,
        grad_conv_weight,
        vecs[8],
        q_g,
        vecs[0],
        k_g,
        v_g,
        vecs[1],
        a_g,
        vecs[2],
        vecs[3],
        vecs[4],
        i_g,
        inner_bias_share,
        o_g,
        vecs[5],
        vecs[6],
        vecs[7],
    )


def solution(mesh):
    rows = P("dp", "seq", None)
    by_col, vec = P(None, "dp"), P("dp")
    out_specs = (
        rows, rows, P(None, "dp", None), vec, by_col, vec, by_col, by_col, vec, by_col, vec, vec,
        vec, by_col, vec, by_col, vec, vec, vec,
    )
    return jax.shard_map(
        on_device, mesh=mesh, in_specs=(rows, rows) + (P(),) * 19, out_specs=out_specs, check_vma=False
    )
```

time: 2030 us -> 694 us (0.34)
  the two profiles are of different devices: /device:TPU:0 before, /device:TPU:1 now
where the time goes in v1:
time: 694 us; the launch traced here: 689 us
  waiting for transfers between devices  269 us (39%)
  Pallas kernels  126 us (18%)
  matrix products  85.2 us (12%)
  blocking collectives  65.4 us (9%)
  local copies, waits for them, and re-layouts  49.8 us (7%)
  other arithmetic  42.1 us (6%)
  starting transfers between devices  33.9 us (5%)
  between operations  16.5 us (2%)
    reduce_scatter x6, waiting for transfers between devices, reduced(): a = lax.psum_scatter(a, 'dp', scatter_dimension=0, tiled=True)  184 us
    ppermute x4, waiting for transfers between devices, from_team(): lax.ppermute(sent, BOTH, [(t, s) for s, t in plan.out_pairs(m)])  64.6 us
    psum x1, blocking collectives, on_device(): small = lax.psum(small, BOTH)  42.2 us
    dot_general x6, matrix products, mm(): return jnp.dot(a, b, preferred_element_type=f32)  39.8 us
    unnamed x112, local copies, waits for them, and re-layouts  27.9 us
    dot_general x6, matrix products, wgrad(): lax.dot_general(a, b, (((0,), (0,)), ((), ())), preferred_element_type=f32)  26.2 us
    all_to_all x1, blocking collectives, on_device(): lax.all_to_all(pull_apart(grad_conv_low, before_loc, out_spread).T.reshap...  23.3 us
    pallas_call x1, Pallas kernels, prep(): pl.pallas_call(prep_kernel, grid=(g,), in_specs=[pl.BlockSpec((k, gw, gw)...  22.5 us
  transfers between devices with their start and end apart: 23, of which 14 were waited for; matrix products, arithmetic and copies ran while one was open for 14% of the time, Pallas kernels for 9%

profile of v1, /device:TPU:1, one launch (start us, length us, event | category | flops | bytes accessed | tf_op | source)
XLA Modules:
  0.0 688.8 jit_solution(1296025104115344875)
XLA Ops:
  9.9 4.8 collective-permute-start
  20.8 21.9 %copy.42.w_ref = bf16[128,768,48]{2,1,0:T(8,128)(2,1)} copy(bf16[128,768,48]{1,2,0:T(8,128)(2,1)} %param.25) | data formatting | bytes 18874368 | tf_op args[4]
  42.8 22.5 %prep.1 = (bf16[16,768,384]{2,1,0:T(8,128)(2,1)}, bf16[16,384,768]{2,1,0:T(8,128)(2,1)}) custom-call(bf16[128,768,48]{2,1,0:T(8,128)(2,1)} %copy.42.w_ref), custom_call_target="tpu_custom_call" | custom-call | tf_op jit(solution)/shard_map/prep/pallas_call | solution.py:24
  76.4 18.8 %conv_fwd.1 = f32[768,512]{1,0:T(8,128)} custom-call(bf16[768,768]{1,0:T(8,128)(2,1)} %get-tuple-element.88.xt_ref, bf16[16,384,768]{2,1,0:T(8,128)(2,1)} %get-tuple-element.28.wt_ref, f32[3,512]{1,0:T(4,128)} %add_convert_fusion.5.sel_ref), custom_call_target="tpu_custom_call" | custom-call | tf_op jit(solution)/shard_map/conv_fwd/pallas_call | solution.py:59
  95.2 6.0 fusion.72
  117.7 8.9 %collective-permute-done.8 = bf16[256,768]{0,1:T(8,128)(2,1)} collective-permute-done((bf16[256,768]{0,1:T(8,128)(2,1)S(1)}, bf16[256,768]{0,1:T(8,128)(2,1)}, u32[]{:S(2)}, u32[]{:S(2)}) %collective-permute-start.8) | collective-permute-done | bytes 393248 | tf_op jit(solution)/shard_map/ppermute | solution.py:414
  130.6 18.7 %attn_fwd.1 = (bf16[512,768]{1,0:T(8,128)(2,1)}, f32[512,768]{1,0:T(8,128)}) custom-call(bf16[512,768]{1,0:T(8,128)(2,1)} %add_convert_fusion.4.refs_0_, bf16[512,128]{1,0:T(8,128)(2,1)} %compare_convert_fusion.refs_1_.refs_4_, bf16[1024,128]{1,0:T(8,128)(2,1)} %select_convert_fusion.refs_2_.refs_5_, bf16[512,1536]{1,0:T(8,128)(2,1)} %copy-done.1, ...), custom_call_target="tpu_custom_call" | custom-call | tf_op jit(solution)/shard_map/attn_fwd/pallas_call | solution.py:225
  152.6 27.0 %fusion.2 = (bf16[512,3072]{1,0:T(8,128)(2,1)S(1)}, f32[512,3072]{1,0:T(8,128)S(1)}) fusion(f32[3072]{0:T(1024)S(1)} %copy-done.46, bf16[768,3072]{1,0:T(8,128)(2,1)} %param.36, f32[512,768]{0,1:T(8,128)S(1)} %get-tuple-element.135, f32[768]{0:T(1024)S(1)} %copy-done.50, f32[768]{0:T(1024)S(1)} %copy-done.41, f32[512]{0:T(512)S(1)} %add_rsqrt_fusion.1, ...), kind=kOutput, calls=%fused_computation.4 | convolution fusion | flops 2521694208 | bytes 15751168 | tf_op jit(solution)/shard_map/dot_general | solution.py:330
  179.6 6.0 fusion.79
  190.1 7.2 %fusion.80 = (bf16[3072]{0:T(1024)(128)(2,1)}, bf16[512,3072]{1,0:T(8,128)(2,1)S(1)}) fusion(f32[512,3072]{1,0:T(8,128)S(1)} %get-tuple-element.137, f32[3072]{0:T(1024)S(1)} %copy-done.46, bf16[512,768]{0,1:T(8,128)(2,1)S(1)} %get-tuple-element.75, bf16[3072,768]{1,0:T(8,128)(2,1)} %param.38), kind=kOutput, calls=%fused_computation.197 | convolution fusion | flops 2434790400 | bytes 14960640 | tf_op jit(solution)/shard_map/dot_general | solution.py:334
  197.4 4.1 multiply_reduce_fusion
  204.5 20.1 %attn_bwd.1 = (bf16[512,768]{1,0:T(8,128)(2,1)}, f32[512,768]{1,0:T(8,128)}, bf16[512,768]{1,0:T(8,128)(2,1)}, f32[512,768]{1,0:T(8,128)}, bf16[512,768]{1,0:T(8,128)(2,1)}) custom-call(bf16[512,768]{1,0:T(8,128)(2,1)} %add_convert_fusion.4.refs_0_, bf16[512,768]{1,0:T(8,128)(2,1)} %convolution_convert_fusion.6.refs_1_, ...), custom_call_target="tpu_custom_call" | custom-call | tf_op jit(solution)/shard_map/attn_bwd/pallas_call | solution.py:287
  224.6 3.2 convolution_convert_fusion.5
  234.4 3.6 convolution_convert_fusion.4
  246.3 7.5 %convolution_convert_fusion.1 = bf16[3072,768]{1,0:T(8,128)(2,1)} fusion(bf16[512,3072]{1,0:T(8,128)(2,1)} %copy-done.52, f32[512,768]{0,1:T(8,128)} %copy-done.3, f32[768]{0:T(1024)} %param.35, f32[768]{0:T(1024)} %param.34, f32[512]{0:T(512)} %copy-done.32, f32[512]{0:T(512)S(1)} %broadcast_multiply_fusion.5), kind=kOutput, calls=%fused_computation.27 | convolution fusion | flops 2420244480 | bytes 9447424 | tf_op jit(solution)/shard_map/dot_general | solution.py:338
  253.8 7.0 %convolution_convert_fusion = bf16[768,3072]{1,0:T(8,128)(2,1)} fusion(bf16[512,768]{0,1:T(8,128)(2,1)} %copy-done.18, bf16[512,3072]{1,0:T(8,128)(2,1)} %copy-done.51), kind=kOutput, calls=%fused_computation.26 | convolution fusion | flops 2418278400 | bytes 8650752 | tf_op jit(solution)/shard_map/dot_general | solution.py:338
  260.8 4.3 all-to-all-start
  280.0 23.3 %all_to_all.10.dt_ref = bf16[8,96,640]{2,1,0:T(8,128)(2,1)} all-to-all(bf16[8,96,640]{2,1,0:T(8,128)(2,1)} %bitcast.152), channel_id=1, replica_groups=mesh['dp'=8,'seq'=4] {'dp'}, dimensions={0} | all-to-all | bytes 1966080 | tf_op jit(solution)/shard_map/all_to_all | solution.py:564
  303.3 17.1 %conv_dw.1 = f32[2,384,768]{2,1,0:T(8,128)} custom-call(bf16[8,96,768]{2,1,0:T(8,128)(2,1)} %all-to-all-done.xt_ref, bf16[8,96,640]{2,1,0:T(8,128)(2,1)} %all_to_all.10.dt_ref), custom_call_target="tpu_custom_call" | custom-call | tf_op jit(solution)/shard_map/conv_dw/pallas_call | solution.py:135
  323.2 29.3 %reduce-scatter.9.cloned.1.call-done = bf16[96,768]{1,0:T(8,128)(2,1)} async-done(((bf16[768,768]{1,0:T(8,128)(2,1)}), bf16[96,768]{1,0:T(8,128)(2,1)}) %reduce-scatter.9.cloned.1.call-update) | async-done | bytes 147472 | tf_op jit(solution)/shard_map/reduce_scatter | solution.py:596
  352.5 40.2 %reduce-scatter.11.cloned.1.call-done = bf16[96,768]{1,0:T(8,128)(2,1)} async-done(((bf16[768,768]{1,0:T(8,128)(2,1)}), bf16[96,768]{1,0:T(8,128)(2,1)}) %reduce-scatter.11.cloned.1.call-update) | async-done | bytes 147472 | tf_op jit(solution)/shard_map/reduce_scatter | solution.py:596
  392.7 57.3 %reduce-scatter.15.cloned.1.call-done = bf16[384,768]{1,0:T(8,128)(2,1)} async-done(((bf16[3072,768]{1,0:T(8,128)(2,1)}), bf16[384,768]{1,0:T(8,128)(2,1)}) %reduce-scatter.15.cloned.1.call-update) | async-done | bytes 589840 | tf_op jit(solution)/shard_map/reduce_scatter | solution.py:596
  450.0 57.6 %reduce-scatter.17.cloned.1.call-done = bf16[96,3072]{1,0:T(8,128)(2,1)} async-done(((bf16[768,3072]{1,0:T(8,128)(2,1)}), bf16[96,3072]{1,0:T(8,128)(2,1)}) %reduce-scatter.17.cloned.1.call-update) | async-done | bytes 589840 | tf_op jit(solution)/shard_map/reduce_scatter | solution.py:596
  515.6 3.6 collective-permute-start.5
  524.7 12.3 %collective-permute-done.5 = bf16[256,768]{1,0:T(8,128)(2,1)S(1)} collective-permute-done((bf16[256,768]{1,0:T(8,128)(2,1)}, bf16[256,768]{1,0:T(8,128)(2,1)S(1)}, u32[]{:S(2)}, u32[]{:S(2)}) %collective-permute-start.5) | collective-permute-done | bytes 393248 | tf_op jit(solution)/shard_map/ppermute | solution.py:431
  537.0 38.7 %collective-permute-done.6 = bf16[256,768]{1,0:T(8,128)(2,1)S(1)} collective-permute-done((bf16[256,768]{1,0:T(8,128)(2,1)}, bf16[256,768]{1,0:T(8,128)(2,1)S(1)}, u32[]{:S(2)}, u32[]{:S(2)}) %collective-permute-start.6) | collective-permute-done | bytes 393248 | tf_op jit(solution)/shard_map/ppermute | solution.py:431
  577.1 42.2 %psum.57 = bf16[8,1248]{1,0:T(8,128)(2,1)} all-reduce(bf16[8,1248]{1,0:T(8,128)(2,1)S(1)} %concatenate.33), channel_id=1, replica_groups=mesh['dp'=8,'seq'=4] {'dp','seq'}, use_global_device_ids=true, to_apply=%region_20.21 | all-reduce | flops 9984 | bytes 39936 | tf_op jit(solution)/shard_map/psum | solution.py:588
  621.3 22.0 %conv_dx.1 = f32[768,512]{1,0:T(8,128)} custom-call(bf16[768,768]{1,0:T(8,128)(2,1)} %select_bitcast_fusion.dt_ref, bf16[16,768,384]{2,1,0:T(8,128)(2,1)} %get-tuple-element.36.wn_ref, f32[3,512]{1,0:T(4,128)} %add_convert_fusion.5.sel_ref), custom_call_target="tpu_custom_call" | custom-call | tf_op jit(solution)/shard_map/conv_dx/pallas_call | solution.py:96
  648.4 4.1 collective-permute-start.14
  654.5 5.9 collective-permute-done.13
  660.4 7.7 %collective-permute-done.14 = bf16[256,768]{1,0:T(8,128)(2,1)S(1)} collective-permute-done((bf16[256,768]{1,0:T(8,128)(2,1)S(1)}, bf16[256,768]{1,0:T(8,128)(2,1)S(1)}, u32[]{:S(2)}, u32[]{:S(2)}) %collective-permute-start.14) | collective-permute-done | bytes 393248 | tf_op jit(solution)/shard_map/ppermute | solution.py:431
  669.1 7.3 %finish_dw.1 = f32[96,48,128]{2,1,0:T(8,128)} custom-call(bf16[2,384,768]{2,1,0:T(8,128)(2,1)} %get-tuple-element.65.p_ref), custom_call_target="tpu_custom_call" | custom-call | tf_op jit(solution)/shard_map/finish_dw/pallas_call | solution.py:173
  (246 shorter events, 112.2 us)
Async XLA Ops:
  7.2 94.9 %copy-start = (bf16[768,768]{1,0:T(8,128)(2,1)S(1)}, bf16[768,768]{1,0:T(8,128)(2,1)}, u32[]{:S(2)}) copy-start(bf16[768,768]{1,0:T(8,128)(2,1)} %param.30) | copy-start | bytes 3538948
  7.2 316.0 %reduce-scatter.7.cloned.1.call-start = ((), (), s32[]{:S(2)}) async-start(), calls=%async_computation.8 | async-start | bytes 1327104 | tf_op jit(solution)/shard_map/reduce_scatter | solution.py:596
  9.9 58.2 %collective-permute-start = (bf16[256,768]{0,1:T(8,128)(2,1)S(1)}, bf16[256,768]{0,1:T(8,128)(2,1)S(1)}, u32[]{:S(2)}, u32[]{:S(2)}) collective-permute-start(bf16[256,768]{0,1:T(8,128)(2,1)S(1)} %bitcast.156), channel_id=1, source_target_pairs={{0,1},{1,0},{2,5},{3,4},{4,3},{5,2},{6,7},{7,6},{8,9},{9,8},{10,13... | collective-permute-start | bytes 1179656 | tf_op jit(solution)/shard_map/ppermute | solution.py:414
  14.8 53.2 %collective-permute-start.1 = (bf16[256,768]{0,1:T(8,128)(2,1)S(1)}, bf16[256,768]{0,1:T(8,128)(2,1)S(1)}, u32[]{:S(2)}, u32[]{:S(2)}) collective-permute-start(bf16[256,768]{0,1:T(8,128)(2,1)S(1)} %bitcast.157), channel_id=1, source_target_pairs={{0,0},{1,1},{2,4},{3,5},{4,2},{5,3},{6,6},{7,7},{8,8},{9,9},{10,12... | collective-permute-start | bytes 1179656 | tf_op jit(solution)/shard_map/ppermute | solution.py:414
  68.7 2.7 collective-permute-start.3
  70.0 3.3 collective-permute-start.2
  103.0 24.7 %copy-start.1 = (bf16[512,1536]{1,0:T(8,128)(2,1)}, bf16[512,1536]{1,0:T(8,128)(2,1)S(1)}, u32[]{:S(2)}) copy-start(bf16[512,1536]{1,0:T(8,128)(2,1)S(1)} %pad_maximum_fusion.refs_3_.refs_5_.refs_6_.refs_8_) | copy-start | bytes 4718596
  103.0 27.6 %collective-permute-start.4 = (bf16[512,1536]{1,0:T(8,128)(2,1)S(1)}, bf16[512,1536]{1,0:T(8,128)(2,1)}, u32[]{:S(2)}, u32[]{:S(2)}) collective-permute-start(bf16[512,1536]{1,0:T(8,128)(2,1)S(1)} %pad_maximum_fusion.refs_3_.refs_5_.refs_6_.refs_8_), channel_id=1, source_target_pairs={{0,4},{4,0},{1,5},{5,1},{2,6},{6,2},{3,7},{7,3},{8,12},{12,8},{9,1... | collective-permute-start | bytes 4718600 | tf_op jit(solution)/shard_map/ppermute | solution.py:497
  104.8 12.9 %collective-permute-start.7 = (bf16[256,768]{0,1:T(8,128)(2,1)}, bf16[256,768]{0,1:T(8,128)(2,1)}, u32[]{:S(2)}, u32[]{:S(2)}) collective-permute-start(bf16[256,768]{0,1:T(8,128)(2,1)} %bitcast.158), channel_id=1, source_target_pairs={{0,1},{1,0},{2,5},{3,4},{4,3},{5,2},{6,7},{7,6},{8,9},{9,8},{10,13... | collective-permute-start | bytes 1179656 | tf_op jit(solution)/shard_map/ppermute | solution.py:414
  107.3 19.3 %collective-permute-start.8 = (bf16[256,768]{0,1:T(8,128)(2,1)S(1)}, bf16[256,768]{0,1:T(8,128)(2,1)}, u32[]{:S(2)}, u32[]{:S(2)}) collective-permute-start(bf16[256,768]{0,1:T(8,128)(2,1)S(1)} %bitcast.159), channel_id=1, source_target_pairs={{0,0},{1,1},{2,4},{3,5},{4,2},{5,3},{6,6},{7,7},{8,8},{9,9},{10,12... | collective-permute-start | bytes 1179656 | tf_op jit(solution)/shard_map/ppermute | solution.py:414
  151.7 49.7 %copy-start.3 = (f32[512,768]{0,1:T(8,128)}, f32[512,768]{0,1:T(8,128)S(1)}, u32[]{:S(2)}) copy-start(f32[512,768]{0,1:T(8,128)S(1)} %get-tuple-element.135) | copy-start | bytes 4718596
  152.6 48.9 %copy-start.32 = (f32[512]{0:T(512)}, f32[512]{0:T(512)S(1)}, u32[]{:S(2)}) copy-start(f32[512]{0:T(512)S(1)} %add_rsqrt_fusion.1) | copy-start | bytes 6148
  152.6 27.0 %copy-start.49 = (f32[768]{0:T(1024)S(1)}, f32[768]{0:T(1024)}, u32[]{:S(2)}) copy-start(f32[768]{0:T(1024)} %param.39) | copy-start | bytes 9220
  227.8 95.4 %reduce-scatter.13.cloned.1.call-start = ((), (), s32[]{:S(2)}) async-start(), calls=%async_computation.11 | async-start | bytes 1327104 | tf_op jit(solution)/shard_map/reduce_scatter | solution.py:596
  230.9 121.6 %reduce-scatter.9.cloned.1.call-start = ((), (), s32[]{:S(2)}) async-start(), calls=%async_computation.9 | async-start | bytes 1327104 | tf_op jit(solution)/shard_map/reduce_scatter | solution.py:596
  231.0 2.6 collective-permute-start.9
  238.0 154.7 %reduce-scatter.11.cloned.1.call-start = ((), (), s32[]{:S(2)}) async-start(), calls=%async_computation.10 | async-start | bytes 1327104 | tf_op jit(solution)/shard_map/reduce_scatter | solution.py:596
  238.1 2.6 collective-permute-start.10
  245.8 204.2 %reduce-scatter.15.cloned.1.call-start = ((), (), s32[]{:S(2)}) async-start(), calls=%async_computation.12 | async-start | bytes 5308416 | tf_op jit(solution)/shard_map/reduce_scatter | solution.py:596
  253.8 253.8 %reduce-scatter.17.cloned.1.call-start = ((), (), s32[]{:S(2)}) async-start(), calls=%async_computation.13 | async-start | bytes 5308416 | tf_op jit(solution)/shard_map/reduce_scatter | solution.py:596
  260.8 19.2 %all-to-all-start = ((bf16[8,96,768]{2,1,0:T(8,128)(2,1)}), bf16[8,96,768]{2,1,0:T(8,128)(2,1)}, u32[]{:S(2)}, u32[]{:S(2)}) async-start(bf16[8,96,768]{2,1,0:T(8,128)(2,1)} %bitcast.151), calls=%async_computation | async-start | bytes 2359296 | tf_op jit(solution)/shard_map/all_to_all | solution.py:487
  265.1 404.0 %all-reduce.19.cloned.1.call-start = ((), (), s32[]{:S(2)}) async-start(), calls=%async_computation.14 | async-start | bytes 5898240 | tf_op jit(solution)/shard_map/psum | solution.py:597
  272.3 3.5 collective-permute-start.12
  274.4 3.4 collective-permute-start.11
  515.6 21.4 %collective-permute-start.5 = (bf16[256,768]{1,0:T(8,128)(2,1)}, bf16[256,768]{1,0:T(8,128)(2,1)S(1)}, u32[]{:S(2)}, u32[]{:S(2)}) collective-permute-start(bf16[256,768]{1,0:T(8,128)(2,1)} %bitcast.160), channel_id=1, source_target_pairs={{1,0},{0,1},{5,2},{4,3},{3,4},{2,5},{7,6},{6,7},{9,8},{8,9},{13,10... | collective-permute-start | bytes 1179656 | tf_op jit(solution)/shard_map/ppermute | solution.py:431
  520.8 54.9 %collective-permute-start.6 = (bf16[256,768]{1,0:T(8,128)(2,1)}, bf16[256,768]{1,0:T(8,128)(2,1)S(1)}, u32[]{:S(2)}, u32[]{:S(2)}) collective-permute-start(bf16[256,768]{1,0:T(8,128)(2,1)} %bitcast.161), channel_id=1, source_target_pairs={{0,0},{1,1},{4,2},{5,3},{2,4},{3,5},{6,6},{7,7},{8,8},{9,9},{12,10... | collective-permute-start | bytes 1179656 | tf_op jit(solution)/shard_map/ppermute | solution.py:431
  524.7 52.1 %copy-start.36 = (bf16[768]{0:T(1024)(128)(2,1)S(1)}, bf16[768]{0:T(1024)(128)(2,1)}, u32[]{:S(2)}) copy-start(bf16[768]{0:T(1024)(128)(2,1)} %get-tuple-element.78) | copy-start | bytes 4612
  524.7 94.5 %copy-start.28 = (pred[768]{0:T(1024)(128)(4,1)S(1)}, pred[768]{0:T(1024)(128)(4,1)}, u32[]{:S(2)}) copy-start(pred[768]{0:T(1024)(128)(4,1)} %copy-done.27) | copy-start | bytes 2308
  524.7 94.5 %copy-start.30 = (pred[768]{0:T(1024)(128)(4,1)S(1)}, pred[768]{0:T(1024)(128)(4,1)}, u32[]{:S(2)}) copy-start(pred[768]{0:T(1024)(128)(4,1)} %copy-done.29) | copy-start | bytes 2308
  621.3 22.0 %copy-start.39 = (pred[512]{0:T(512)(128)(4,1)S(1)}, pred[512]{0:T(512)(128)(4,1)}, u32[]{:S(2)}) copy-start(pred[512]{0:T(512)(128)(4,1)} %copy-done.38) | copy-start | bytes 1540
  647.3 13.0 %collective-permute-start.13 = (bf16[256,768]{1,0:T(8,128)(2,1)S(1)}, bf16[256,768]{1,0:T(8,128)(2,1)S(1)}, u32[]{:S(2)}, u32[]{:S(2)}) collective-permute-start(bf16[256,768]{1,0:T(8,128)(2,1)S(1)} %bitcast.162), channel_id=1, source_target_pairs={{1,0},{0,1},{5,2},{4,3},{3,4},{2,5},{7,6},{6,7},{9,8},{8,9},{13,10... | collective-permute-start | bytes 1179656 | tf_op jit(solution)/shard_map/ppermute | solution.py:431
  648.4 19.6 %collective-permute-start.14 = (bf16[256,768]{1,0:T(8,128)(2,1)S(1)}, bf16[256,768]{1,0:T(8,128)(2,1)S(1)}, u32[]{:S(2)}, u32[]{:S(2)}) collective-permute-start(bf16[256,768]{1,0:T(8,128)(2,1)S(1)} %bitcast.163), channel_id=1, source_target_pairs={{0,0},{1,1},{4,2},{5,3},{2,4},{3,5},{6,6},{7,7},{8,8},{9,9},{12,10... | collective-permute-start | bytes 1179656 | tf_op jit(solution)/shard_map/ppermute | solution.py:431
  (46 other events, 298.7 us)
Sparse Core Ops, SparseCore 0:
  228.0 37.5 reduce-scatter.6
  269.1 43.3 reduce-scatter.12
  315.7 36.7 reduce-scatter.8
  355.9 36.7 reduce-scatter.10
  396.0 53.9 reduce-scatter.14
  453.7 53.8 reduce-scatter.16
  511.1 133.9 all-reduce.18

commit v2 on v1

v2 whole, which is shorter than its diff:
```python
import functools
import jax
import jax.numpy as jnp
from jax import lax
from jax.experimental import pallas as pl
from jax.experimental.pallas import tpu as pltpu
from jax.sharding import PartitionSpec as P


DK = 16
ANY = pl.BlockSpec(memory_space=pl.ANY)

def prep_kernel(w_ref, wt_ref):
    gw = w_ref.shape[1]
    slots = w_ref.shape[2] // gw
    lane = lax.broadcasted_iota(jnp.int32, (gw, 128), 1)
    tiles = w_ref.shape[2] // 128
    for half in range(DK // slots):
        sums = [[None] * tiles for _ in range(slots)]
        for slot in range(slots):
            w = w_ref[half * slots + slot]
            for g in range(slots):
                turn = (slot - g) % slots
                moved = w if turn == 0 else pltpu.roll(w, gw * turn, 1)
                for t in range(tiles):
                    lo, hi = gw * slot - 128 * t, gw * (slot + 1) - 128 * t
                    if hi <= 0 or lo >= 128:
                        continue
                    part = moved[:, 128 * t : 128 * (t + 1)]
                    old = sums[g][t]
                    sums[g][t] = part if old is None else jnp.where(lane >= lo, part, old)
        for g in range(slots):
            for t in range(tiles):
                at = half * slots * gw + 128 * t
                wt_ref[g, :, at : at + 128] = sums[g][t]


def prep(w):
    k, width, gw = w.shape
    groups = width // gw
    nb = k // DK
    slots = 8
    assert (slots * gw) % 128 == 0 and DK % slots == 0 and groups % slots == 0
    return pl.pallas_call(
        prep_kernel,
        grid=(groups // slots, nb),
        in_specs=[pl.BlockSpec((DK, gw, slots * gw), lambda i, b: (b, 0, i))],
        out_specs=pl.BlockSpec((slots, gw, DK * gw), lambda i, b: (i, b, 0)),
        out_shape=jax.ShapeDtypeStruct((groups, nb * gw, DK * gw), w.dtype),
        cost_estimate=pl.CostEstimate(flops=10**9, bytes_accessed=2 * k * width * gw * 2, transcendentals=0),
        name="prep",
    )(jnp.transpose(w, (0, 2, 1)))

def conv_kernel(xt_ref, wt_ref, sel_ref, out_ref, a0_ref, z_ref, *, nb, gw, F, nbound):
    tin = xt_ref.shape[1]
    x = xt_ref[...]
    for dk in range(DK):
        r = x if dk == 0 else pltpu.roll(x, tin - dk, 1)
        a0_ref[gw*dk:gw*(dk+1), :] = r.astype(a0_ref.dtype)
    z_ref[...] = jnp.dot(wt_ref[0], a0_ref[...], preferred_element_type=jnp.float32)
    acc = z_ref[0:gw, :]
    for b in range(1, nb):
        acc = acc + pltpu.roll(z_ref[gw*b:gw*(b+1), :], tin - DK*b, 1)
    out = acc[:, :F]
    for n in range(1, nbound+1):
        sh = pltpu.roll(acc, tin - 64*n, 1)[:, :F]
        out = jnp.where(sel_ref[n:n+1, :] > 0, sh, out)
    out_ref[...] = out

def conv(xt, wt, sel, F, nbound):
    width, tin = xt.shape
    g, nbgw, dkgw = wt.shape
    gw = width // g
    nb = nbgw // gw
    return pl.pallas_call(
        functools.partial(conv_kernel, nb=nb, gw=gw, F=F, nbound=nbound),
        grid=(g,),
        in_specs=[pl.BlockSpec((gw, tin), lambda i: (i, 0)),
                  pl.BlockSpec((1, nbgw, dkgw), lambda i: (i, 0, 0)),
                  pl.BlockSpec(sel.shape, lambda i: (0, 0))],
        out_specs=pl.BlockSpec((gw, F), lambda i: (i, 0)),
        out_shape=jax.ShapeDtypeStruct((width, F), jnp.float32),
        scratch_shapes=[pltpu.VMEM((dkgw, tin), jnp.bfloat16), pltpu.VMEM((nbgw, tin), jnp.float32)],
        cost_estimate=pl.CostEstimate(flops=2 * g * nbgw * dkgw * tin, bytes_accessed=2 * g * nbgw * dkgw, transcendentals=0),
        name="conv_fwd",
    )(xt, wt, sel)

def dx_kernel(dt_ref, wt_ref, sel_ref, *refs, nb, gw, F, nbound):
    out_ref, ds_ref, y_ref = refs[-3:]
    tin = dt_ref.shape[1]
    d = dt_ref[...]
    for b in range(nb):
        r = d if b == 0 else pltpu.roll(d, DK*b, 1)
        ds_ref[gw*b:gw*(b+1), :] = r.astype(ds_ref.dtype)
    y_ref[...] = jnp.dot(wt_ref[0].T, ds_ref[...], preferred_element_type=jnp.float32)
    acc = y_ref[0:gw, :]
    for dk in range(1, DK):
        acc = acc + pltpu.roll(y_ref[gw*dk:gw*(dk+1), :], dk, 1)
    acc = acc[:, 128:]
    out = acc[:, :F]
    for n in range(1, nbound+1):
        sh = pltpu.roll(acc, acc.shape[1] - 64*n, 1)[:, :F]
        out = jnp.where(sel_ref[n:n+1, :] > 0, sh, out)
    out_ref[...] = out

def conv_dx(dt, wt, sel, F, nbound, first, count, deps):
    width, tin = dt.shape
    g, nbgw, dkgw = wt.shape
    gw = width // g
    nb = nbgw // gw
    return pl.pallas_call(
        functools.partial(dx_kernel, nb=nb, gw=gw, F=F, nbound=nbound),
        grid=(count,),
        in_specs=[pl.BlockSpec((gw, tin), lambda i: (i + first, 0)),
                  pl.BlockSpec((1, nbgw, dkgw), lambda i: (i + first, 0, 0)),
                  pl.BlockSpec(sel.shape, lambda i: (0, 0))] + [ANY] * len(deps),
        out_specs=pl.BlockSpec((gw, F), lambda i: (i, 0)),
        out_shape=jax.ShapeDtypeStruct((count * gw, F), jnp.float32),
        scratch_shapes=[pltpu.VMEM((nbgw, tin), jnp.bfloat16), pltpu.VMEM((dkgw, tin), jnp.float32)],
        cost_estimate=pl.CostEstimate(flops=2 * count * nbgw * dkgw * tin, bytes_accessed=2 * count * nbgw * dkgw, transcendentals=0),
        name="conv_dx",
    )(dt, wt, sel, *deps)

def dw_kernel(*refs, nb, gw, m):
    x_refs, d_refs = refs[:m], refs[m : 2 * m]
    out_ref, a0_ref, ds_ref = refs[-3:]
    tin = x_refs[0].shape[2]
    tout = d_refs[0].shape[2]
    ones = jnp.ones((16, tout), jnp.bfloat16)
    bias = None
    for s in range(m):
        x, d = x_refs[s][0], d_refs[s][0]
        part = lax.dot_general(ones, d, (((1,), (1,)), ((), ())), preferred_element_type=jnp.float32)
        bias = part if bias is None else bias + part
        d = jnp.concatenate([d, jnp.zeros((gw, tin - tout), d.dtype)], axis=1)
        slot = s % 2
        for dk in range(DK):
            a0_ref[slot, gw*dk:gw*(dk+1), :] = x if dk == 0 else pltpu.roll(x, tin - dk, 1)
        for b in range(nb):
            ds_ref[slot, gw*b:gw*(b+1), :] = d if b == 0 else pltpu.roll(d, DK*b, 1)
        p = lax.dot_general(
            ds_ref[slot], a0_ref[slot], (((1,), (1,)), ((), ())), preferred_element_type=jnp.float32
        )
        if s == 0:
            out_ref[: nb*gw, :] = p
        else:
            out_ref[: nb*gw, :] += p
    out_ref[nb*gw :, :] = jnp.zeros((out_ref.shape[0] - nb*gw, out_ref.shape[1]), jnp.float32)
    out_ref[nb*gw : nb*gw + 16, :gw] = bias


def conv_dw(xs, ds, group, gw, nb, deps):
    m, _, tin = xs.shape
    tout = ds.shape[2]
    rows = nb*gw + 32
    flops = 2 * m * nb*gw * DK*gw * tin
    return pl.pallas_call(
        functools.partial(dw_kernel, nb=nb, gw=gw, m=m),
        grid=(1,),
        in_specs=[pl.BlockSpec((1, gw, tin), lambda i, k=k: (k, group, 0)) for k in range(m)]
        + [pl.BlockSpec((1, gw, tout), lambda i, k=k: (k, group, 0)) for k in range(m)]
        + [ANY] * len(deps),
        out_specs=pl.BlockSpec((rows, DK*gw), lambda i: (0, 0)),
        scratch_shapes=[pltpu.VMEM((2, DK*gw, tin), jnp.bfloat16), pltpu.VMEM((2, nb*gw, tin), jnp.bfloat16)],
        out_shape=jax.ShapeDtypeStruct((rows, DK*gw), jnp.float32),
        cost_estimate=pl.CostEstimate(flops=flops, bytes_accessed=4 * rows * DK*gw, transcendentals=0),
        name="conv_dw",
    )(*([xs] * m), *([ds] * m), *deps)


def join_kernel(mine_ref, ks_ref, kk_ref, gs_ref, gk_ref, *refs):
    sent_ref, kept_ref = refs[-2:]
    sent_ref[...] = (ks_ref[...].astype(jnp.float32) + gs_ref[...].astype(jnp.float32)).astype(sent_ref.dtype)
    kept_ref[...] = (kk_ref[...].astype(jnp.float32) + gk_ref[...].astype(jnp.float32)).astype(kept_ref.dtype)


def join_split(kept, got, mine, high, low, deps):
    n, rows, cols = kept.shape

    def half(other):
        def at(i, mine_ref):
            side = 1 - mine_ref[0] if other else mine_ref[0]
            return ((i // low * 2 + side) * low + i % low, 0, 0)

        return pl.BlockSpec((1, rows, cols), at)

    out = pl.BlockSpec((1, rows, cols), lambda i, mine_ref: (i, 0, 0))
    shape = jax.ShapeDtypeStruct((n // 2, rows, cols), kept.dtype)
    return pl.pallas_call(
        join_kernel,
        grid_spec=pltpu.PrefetchScalarGridSpec(
            num_scalar_prefetch=1,
            grid=(n // 2,),
            in_specs=[half(True), half(False), half(True), half(False)] + [ANY] * len(deps),
            out_specs=[out, out],
        ),
        out_shape=[shape, shape],
        cost_estimate=pl.CostEstimate(flops=n * rows * cols, bytes_accessed=6 * n * rows * cols, transcendentals=0),
        name="join",
    )(mine, kept, kept, got, got, *deps)


def join_last_kernel(k_ref, g_ref, *refs):
    refs[-1][...] = (k_ref[...].astype(jnp.float32) + g_ref[...].astype(jnp.float32)).astype(refs[-1].dtype)


def join_last(kept, got, deps):
    whole = pl.BlockSpec(memory_space=pltpu.VMEM)
    return pl.pallas_call(
        join_last_kernel,
        in_specs=[whole, whole] + [ANY] * len(deps),
        out_specs=whole,
        out_shape=jax.ShapeDtypeStruct(kept.shape, kept.dtype),
        cost_estimate=pl.CostEstimate(flops=kept.size, bytes_accessed=6 * kept.size, transcendentals=0),
        name="join_last",
    )(kept, got, *deps).reshape(-1, kept.shape[-1])


def finish_kernel(p_ref, *refs, nb, gw):
    out_ref, e_ref, q_ref = refs[-3:]
    dkgw = DK * gw
    row = lax.broadcasted_iota(jnp.int32, (dkgw, dkgw), 0)
    col = lax.broadcasted_iota(jnp.int32, (1, dkgw), 1)
    e_ref[...] = (row == (col % DK) * gw + col // DK).astype(e_ref.dtype)
    per = 128 // DK
    lane_block = lax.broadcasted_iota(jnp.int32, (gw, 128), 1) // DK
    q_ref[...] = jnp.dot(
        p_ref[: nb * gw, :], e_ref[...], preferred_element_type=jnp.float32
    ).astype(q_ref.dtype)
    for tile in range(dkgw // 128):
        outs = [None] * per
        for b in range(nb):
            piece = q_ref[gw*b:gw*(b+1), 128*tile:128*(tile+1)]
            for i in range(per):
                turn = (b - i) % per
                moved = piece if turn == 0 else pltpu.roll(piece, DK * turn, 1)
                outs[i] = moved if outs[i] is None else jnp.where(lane_block == b, moved, outs[i])
        for i in range(per):
            out_ref[tile * per + i] = outs[i].astype(out_ref.dtype)


def finish_dw(ps, gw, nb):
    assert nb * DK == 128
    g = len(ps)
    out = None
    for k, p in enumerate(ps):
        given = [] if out is None else [out]
        out = pl.pallas_call(
            functools.partial(finish_kernel, nb=nb, gw=gw),
            grid=(1,),
            in_specs=[pl.BlockSpec(p.shape, lambda i: (0, 0))] + [ANY] * len(given),
            out_specs=pl.BlockSpec((gw, gw, 128), lambda i, k=k: (k, 0, 0)),
            out_shape=jax.ShapeDtypeStruct((g*gw, gw, 128), jnp.float32),
            scratch_shapes=[pltpu.VMEM((DK*gw, DK*gw), jnp.bfloat16), pltpu.VMEM((nb*gw, DK*gw), jnp.bfloat16)],
            input_output_aliases={1: 0} if given else {},
            name="finish_dw",
        )(p, *given)
    return jnp.transpose(out, (2, 0, 1))


def wg_rows_kernel(mine_ref, lhs_ref, rhs_ref, *refs, many, dp, nextra, ndeps):
    extra_refs = refs[:nextra]
    sent_ref, kept_ref, lt_ref, ls_ref, lk_ref = refs[nextra + ndeps :]
    half = many * dp // 2
    share = lhs_ref.shape[1] // (many * dp)
    cols = sent_ref.shape[2]
    mine = mine_ref[0]

    @pl.when(pl.program_id(0) == 0)
    def _():
        lt_ref[...] = lhs_ref[...].T
        for i in range(half):
            for to_ref, side in ((ls_ref, 1 - mine), (lk_ref, mine)):
                at = pl.multiple_of((2 * i + side) * share, 16)
                to_ref[i * share : (i + 1) * share, :] = lt_ref[pl.ds(at, share), :]

    for out_ref, l_ref in ((sent_ref, ls_ref), (kept_ref, lk_ref)):
        total = jnp.dot(l_ref[...], rhs_ref[...], preferred_element_type=jnp.float32)
        for i in range(half):
            out_ref[i, :share, :] = total[i * share : (i + 1) * share, :].astype(out_ref.dtype)
    if nextra:
        for m in range(many):
            rows = []
            for r in extra_refs:
                if many > 1:
                    rows.append(r[0:1, m * cols : (m + 1) * cols])
                else:
                    rows += [r[0:1, k * cols : (k + 1) * cols] for k in range(r.shape[1] // cols)]
            rows.append(jnp.zeros((16 - len(rows), cols), jnp.float32))
            block = jnp.concatenate(rows, 0).astype(jnp.bfloat16)
            for i in range(dp // 2):
                sent_ref[m * dp // 2 + i, share:, :] = block
                kept_ref[m * dp // 2 + i, share:, :] = block


def wg_rows(mine, lhs, rhs, many, dp, chunks, extras=(), deps=(), slots=None, first=0, into=()):
    F, M = lhs.shape
    N = rhs.shape[1]
    share = M // (many * dp)
    half = many * dp // 2
    rows = share + (16 if extras else 0)
    out = pl.BlockSpec((half, rows, N // chunks), lambda i, m: (first, 0, i))
    shape = jax.ShapeDtypeStruct((slots or half, rows, N), jnp.bfloat16)
    deps = tuple(into) + tuple(deps)
    at = 3 + len(extras)
    return pl.pallas_call(
        functools.partial(wg_rows_kernel, many=many, dp=dp, nextra=len(extras), ndeps=len(deps)),
        input_output_aliases={at: 0, at + 1: 1} if into else {},
        grid_spec=pltpu.PrefetchScalarGridSpec(
            num_scalar_prefetch=1,
            grid=(chunks,),
            in_specs=[
                pl.BlockSpec((F, M), lambda i, m: (0, 0)),
                pl.BlockSpec((F, N // chunks), lambda i, m: (0, i)),
            ]
            + [pl.BlockSpec(e.shape, lambda i, m: (0, 0)) for e in extras]
            + [ANY] * len(deps),
            out_specs=[out, out],
            scratch_shapes=[
                pltpu.VMEM((M, F), jnp.bfloat16),
                pltpu.VMEM((half * share, F), jnp.bfloat16),
                pltpu.VMEM((half * share, F), jnp.bfloat16),
            ],
        ),
        out_shape=[shape, shape],
        cost_estimate=pl.CostEstimate(flops=2 * F * M * N, bytes_accessed=2 * M * N, transcendentals=0),
        name="wg_rows",
    )(mine, lhs, rhs, *extras, *deps)


def wg_cols_kernel(mine_ref, lhs_ref, rhs_ref, *refs):
    sent_ref, kept_ref, lt_ref = refs[-3:]
    half = pl.num_programs(0) // 2

    @pl.when(pl.program_id(0) == 0)
    def _():
        lt_ref[...] = lhs_ref[...].T

    total = jnp.dot(lt_ref[...], rhs_ref[...], preferred_element_type=jnp.float32).astype(jnp.bfloat16)

    @pl.when(pl.program_id(0) < half)
    def _():
        sent_ref[0] = total

    @pl.when(pl.program_id(0) >= half)
    def _():
        kept_ref[0] = total


def wg_cols(mine, lhs, rhs, dp, deps=()):
    F, M = lhs.shape
    share = rhs.shape[1] // dp
    half = dp // 2

    def of(s, m):
        side = jnp.where(s < half, 1 - m[0], m[0])
        return (0, 2 * lax.rem(s, half) + side)

    shape = jax.ShapeDtypeStruct((half, M, share), jnp.bfloat16)
    return pl.pallas_call(
        wg_cols_kernel,
        grid_spec=pltpu.PrefetchScalarGridSpec(
            num_scalar_prefetch=1,
            grid=(dp,),
            in_specs=[pl.BlockSpec((F, M), lambda s, m: (0, 0)), pl.BlockSpec((F, share), of)]
            + [ANY] * len(deps),
            out_specs=[
                pl.BlockSpec((1, M, share), lambda s, m: (jnp.minimum(s, half - 1), 0, 0)),
                pl.BlockSpec((1, M, share), lambda s, m: (jnp.maximum(s - half, 0), 0, 0)),
            ],
            scratch_shapes=[pltpu.VMEM((M, F), jnp.bfloat16)],
        ),
        out_shape=[shape, shape],
        cost_estimate=pl.CostEstimate(flops=2 * F * M * share * dp, bytes_accessed=2 * M * share * dp, transcendentals=0),
        name="wg_cols",
    )(mine, lhs, rhs, *deps)


def dpos_kernel(keep_ref, *refs, parts, far, ndeps):
    qs, ks, vs = refs[:parts], refs[parts : 2 * parts], refs[2 * parts : 3 * parts]
    far_refs, refs = refs[3 * parts : (3 + far) * parts], refs[(3 + far) * parts :]
    wq_ref, wk_ref, wv_ref, first_ref, g_ref, conv_ref = refs[:6]
    low_ref, lowv_ref, pos_ref, d_ref, qk_ref, v_ref = refs[6 + ndeps :]
    dq = jnp.concatenate([r[...] for r in qs], 1)
    dks, dvs = [], []
    for p in range(parts):
        dk, dv = ks[p][...], vs[p][...]
        for r in far_refs[p * far : (p + 1) * far]:
            dk = dk + r[0].astype(jnp.float32)
            dv = dv + r[1].astype(jnp.float32)
        dks.append(dk.astype(jnp.bfloat16))
        dvs.append(dv.astype(jnp.bfloat16))
    dk, dv = jnp.concatenate(dks, 1), jnp.concatenate(dvs, 1)
    width = dq.shape[1]
    low_ref[:, :width] = dq
    low_ref[:, width:] = dk
    lowv_ref[...] = dv
    total = first_ref[...] + (1.0 - keep_ref[0]) * g_ref[...].astype(jnp.float32)
    for low, w_ref in ((dq, wq_ref), (dk, wk_ref), (dv, wv_ref)):
        total = total + lax.dot_general(
            low, w_ref[...], (((1,), (1,)), ((), ())), preferred_element_type=jnp.float32
        )
    pos_ref[...] = total
    d_ref[...] = (total * gelu_slope(conv_ref[...])).astype(d_ref.dtype)
    sums = [jnp.sum(low.astype(jnp.float32), 0, keepdims=True) for low in (dq, dk, dv)]

    @pl.when(pl.program_id(0) == 0)
    def _():
        qk_ref[...] = jnp.zeros_like(qk_ref)
        v_ref[...] = jnp.zeros_like(v_ref)

    qk_ref[0:1, :width] += sums[0]
    qk_ref[0:1, width:] += sums[1]
    v_ref[0:1, :] += sums[2]


def dpos(keep, dqs, dks, dvs, fars, wq, wk, wv, first, g, conv_before, deps):
    F, W = first.shape
    rows = min(256, F)
    parts = len(dqs)
    part = pl.BlockSpec((rows, W // parts), lambda i, k: (i, 0))
    block = pl.BlockSpec((rows, W), lambda i, k: (i, 0))
    whole = pl.BlockSpec((W, W), lambda i, k: (0, 0))
    return pl.pallas_call(
        functools.partial(dpos_kernel, parts=parts, far=len(fars[0]), ndeps=len(deps)),
        grid_spec=pltpu.PrefetchScalarGridSpec(
            num_scalar_prefetch=1,
            grid=(F // rows,),
            in_specs=[part] * (3 * parts)
            + [pl.BlockSpec((2, rows, W // parts), lambda i, k: (0, i, 0))] * (parts * len(fars[0]))
            + [whole] * 3 + [block] * 3 + [ANY] * len(deps),
            out_specs=[
                pl.BlockSpec((rows, 2 * W), lambda i, k: (i, 0)), block, block, block,
                pl.BlockSpec((8, 2 * W), lambda i, k: (0, 0)),
                pl.BlockSpec((8, W), lambda i, k: (0, 0)),
            ],
        ),
        out_shape=[
            jax.ShapeDtypeStruct((F, 2 * W), jnp.bfloat16),
            jax.ShapeDtypeStruct((F, W), jnp.bfloat16),
            jax.ShapeDtypeStruct((F, W), jnp.float32),
            jax.ShapeDtypeStruct((F, W), jnp.bfloat16),
            jax.ShapeDtypeStruct((8, 2 * W), jnp.float32),
            jax.ShapeDtypeStruct((8, W), jnp.float32),
        ],
        cost_estimate=pl.CostEstimate(flops=6 * F * W * W, bytes_accessed=20 * F * W + 6 * W * W, transcendentals=0),
        name="dpos",
    )(keep, *dqs, *dks, *dvs, *[f for part in fars for f in part], wq, wk, wv, first, g, conv_before, *deps)


def front_kernel(conv_ref, bias_ref, x_ref, wq_ref, wk_ref, wv_ref, bq_ref, bv_ref, *refs):
    cb_ref, pos_ref, low_ref, q_ref, kv_ref = refs[-5:]
    before = conv_ref[...].T + bias_ref[...]
    cb_ref[...] = before
    pos = x_ref[...].astype(jnp.float32) + gelu(before)
    pos_ref[...] = pos
    low = pos.astype(jnp.bfloat16)
    low_ref[...] = low
    width = low.shape[1]
    q_ref[...] = (jnp.dot(low, wq_ref[...], preferred_element_type=jnp.float32) + bq_ref[...]).astype(jnp.bfloat16)
    kv_ref[:, :width] = jnp.dot(low, wk_ref[...], preferred_element_type=jnp.float32).astype(jnp.bfloat16)
    kv_ref[:, width:] = (
        jnp.dot(low, wv_ref[...], preferred_element_type=jnp.float32) + bv_ref[...]
    ).astype(jnp.bfloat16)


def front(conv_t, bias, x, wq, wk, wv, bq, bv, deps):
    W, F = conv_t.shape
    rows = min(256, F)
    block = pl.BlockSpec((rows, W), lambda i: (i, 0))
    whole = pl.BlockSpec((W, W), lambda i: (0, 0))
    vec = pl.BlockSpec((1, W), lambda i: (0, 0))
    return pl.pallas_call(
        front_kernel,
        grid=(F // rows,),
        in_specs=[pl.BlockSpec((W, rows), lambda i: (0, i)), vec, block]
        + [whole] * 3 + [vec] * 2 + [ANY] * len(deps),
        out_specs=[block] * 4 + [pl.BlockSpec((rows, 2 * W), lambda i: (i, 0))],
        out_shape=[
            jax.ShapeDtypeStruct((F, W), jnp.float32),
            jax.ShapeDtypeStruct((F, W), jnp.float32),
            jax.ShapeDtypeStruct((F, W), jnp.bfloat16),
            jax.ShapeDtypeStruct((F, W), jnp.bfloat16),
            jax.ShapeDtypeStruct((F, 2 * W), jnp.bfloat16),
        ],
        cost_estimate=pl.CostEstimate(flops=6 * F * W * W, bytes_accessed=20 * F * W + 6 * W * W, transcendentals=0),
        name="front",
    )(conv_t, bias.reshape(1, W), x, wq, wk, wv, bq.reshape(1, W), bv.reshape(1, W), *deps)


def mid_kernel(keep_ref, attn_ref, pos_ref, g_ref, wa_ref, wi_ref, wo_ref, ba_ref, g1_ref, s1_ref, bi_ref, bo_ref, g2_ref, s2_ref, *refs, ndeps, chunk):
    (
        out_ref, first_ref, inner_ref, douter_ref, dinner_ref, dattn_ref, dfirst_ref, dheads_ref,
        inner_sum_ref, sums_ref, slope_ref,
    ) = refs[ndeps:]
    keep = keep_ref[0]
    width = pos_ref.shape[1]
    ff = wi_ref.shape[1]
    pos = pos_ref[...]
    attn_out = jnp.dot(attn_ref[...], wa_ref[...], preferred_element_type=jnp.float32) + ba_ref[...]
    first_normed, first_scale = layer_norm(pos + attn_out)
    first_out = first_normed * g1_ref[...] + s1_ref[...]
    first_low = first_out.astype(jnp.bfloat16)
    first_ref[...] = first_low
    total = None
    for c in range(0, ff, chunk):
        cols = slice(c, c + chunk)
        pre = jnp.dot(first_low, wi_ref[:, cols], preferred_element_type=jnp.float32) + bi_ref[:, cols]
        phi = 0.5 * (1.0 + lax.erf(pre * root_half))
        slope_ref[:, cols] = phi + pre * jnp.exp(-0.5 * pre * pre) * inv_root_two_pi
        low = (pre * phi).astype(jnp.bfloat16)
        inner_ref[:, cols] = low
        part = jnp.dot(low, wo_ref[cols, :], preferred_element_type=jnp.float32)
        total = part if total is None else total + part
    second_normed, second_scale = layer_norm(first_out + (total + bo_ref[...]))
    second_out = second_normed * g2_ref[...] + s2_ref[...]
    out_ref[...] = (keep * second_out + (1.0 - keep) * pos).astype(jnp.bfloat16)

    grad_layer = keep * g_ref[...].astype(jnp.float32)
    d_second = norm_back(grad_layer * g2_ref[...], second_normed, second_scale)
    d_outer = d_second.astype(jnp.bfloat16)
    douter_ref[...] = d_outer

    @pl.when(pl.program_id(0) == 0)
    def _():
        inner_sum_ref[...] = jnp.zeros_like(inner_sum_ref)
        sums_ref[...] = jnp.zeros_like(sums_ref)

    d_first_out = d_second
    for c in range(0, ff, chunk):
        cols = slice(c, c + chunk)
        d_inner = (
            lax.dot_general(d_outer, wo_ref[cols, :], (((1,), (1,)), ((), ())), preferred_element_type=jnp.float32)
            * slope_ref[:, cols]
        ).astype(jnp.bfloat16)
        dinner_ref[:, cols] = d_inner
        inner_sum_ref[0:1, cols] += jnp.sum(d_inner.astype(jnp.float32), 0, keepdims=True)
        d_first_out = d_first_out + lax.dot_general(
            d_inner, wi_ref[:, cols], (((1,), (1,)), ((), ())), preferred_element_type=jnp.float32
        )
    d_first = norm_back(d_first_out * g1_ref[...], first_normed, first_scale)
    dfirst_ref[...] = d_first
    d_attn = d_first.astype(jnp.bfloat16)
    dattn_ref[...] = d_attn
    dheads_ref[...] = lax.dot_general(
        d_attn, wa_ref[...], (((1,), (1,)), ((), ())), preferred_element_type=jnp.float32
    ).astype(jnp.bfloat16)
    for k, v in enumerate((
        d_attn.astype(jnp.float32), d_first_out * first_normed, d_first_out,
        d_outer.astype(jnp.float32), grad_layer * second_normed, grad_layer,
    )):
        sums_ref[0:1, k * width : (k + 1) * width] += jnp.sum(v, 0, keepdims=True)


def mid(keep, attn_low, pos_out, g, wa, wi, wo, ba, g1, s1, bi, bo, g2, s2, deps):
    F, W = pos_out.shape
    ff = wi.shape[1]
    rows = min(256, F)
    block = pl.BlockSpec((rows, W), lambda i, k: (i, 0))
    wide = pl.BlockSpec((rows, ff), lambda i, k: (i, 0))

    def whole(*shape):
        return pl.BlockSpec(shape, lambda i, k: (0,) * len(shape))

    vec = whole(1, W)
    out = lambda cols, kind: jax.ShapeDtypeStruct((F, cols), kind)
    bf, fl = jnp.bfloat16, jnp.float32
    return pl.pallas_call(
        functools.partial(mid_kernel, ndeps=len(deps), chunk=min(768, ff)),
        grid_spec=pltpu.PrefetchScalarGridSpec(
            num_scalar_prefetch=1,
            grid=(F // rows,),
            in_specs=[block, block, block, whole(W, W), whole(W, ff), whole(ff, W), vec, vec, vec, whole(1, ff), vec, vec, vec]
            + [ANY] * len(deps),
            out_specs=[block, block, wide, block, wide, block, block, block, whole(8, ff), whole(8, 6 * W)],
            scratch_shapes=[pltpu.VMEM((rows, ff), jnp.float32)],
        ),
        out_shape=[
            out(W, bf), out(W, bf), out(ff, bf), out(W, bf), out(ff, bf), out(W, bf), out(W, fl), out(W, bf),
            jax.ShapeDtypeStruct((8, ff), fl), jax.ShapeDtypeStruct((8, 6 * W), fl),
        ],
        cost_estimate=pl.CostEstimate(flops=8 * F * W * ff + 4 * F * W * W, bytes_accessed=16 * W * ff, transcendentals=0),
        name="mid",
    )(
        keep, attn_low, pos_out, g, wa, wi, wo, ba.reshape(1, W), g1.reshape(1, W), s1.reshape(1, W),
        bi.reshape(1, ff), bo.reshape(1, W), g2.reshape(1, W), s2.reshape(1, W), *deps,
    )


def place(ext, before, gaps, length):
    rows, have = ext.shape
    ext = jnp.concatenate([ext, jnp.zeros((rows, length - have), ext.dtype)], 1) if length > have else ext
    if length > have:
        before = jnp.concatenate([before, jnp.full((before.shape[0], length - have), -1, before.dtype)], 1)
    total = None
    for k in range(gaps + 1):
        moved = ext if k == 0 else pltpu.roll(ext, HALO * k, 1)
        here = (before if k == 0 else pltpu.roll(before, HALO * k, 1))[0:1, :] == k
        total = jnp.where(here, moved, jnp.zeros((), ext.dtype) if total is None else total)
    return total


def window_of(seg_ref, wide_ref, row, member, F):
    T = seg_ref.shape[1]
    wide_ref[...] = jnp.zeros_like(wide_ref)
    wide_ref[:, 128 : 128 + T] = jnp.broadcast_to(seg_ref[pl.ds(row % 8, 1), :], (8, T))
    start = pl.multiple_of(member * F, 128)
    window = wide_ref[:, pl.ds(start, F + 256)]
    return pltpu.roll(window, F + 256 - HALO, 1)[:, : F + 2 * HALO]


def ordinals(window, F):
    lane = lax.broadcasted_iota(jnp.int32, window.shape, 1)
    local = (lane >= HALO) & (lane < HALO + F)
    most = jnp.max(jnp.where(local, window, 0), axis=1, keepdims=True)
    first = jnp.sum(jnp.where(lane == HALO, window, 0), axis=1, keepdims=True)
    last = jnp.sum(jnp.where(lane == HALO + F - 1, window, 0), axis=1, keepdims=True)
    number = jnp.where(window > 0, window, most + 1)
    number_first = jnp.where(first > 0, first, most + 1)
    number_last = jnp.where(last > 0, last, most + 1)
    before = number - number_first
    before = jnp.where((lane < HALO) & (window != first), -1, before)
    right = jnp.where(window == last, number_last - number_first, -1)
    return jnp.where(lane >= HALO + F, right, before)


def column(row):
    return row.astype(jnp.float32).T[:, 0:1]


def build_x_kernel(at_ref, seg_ref, *refs, n, nlow, nhigh, team, F, gaps, spread):
    row, member = at_ref[0], at_ref[1]
    j = at_ref[2]
    got, lows, highs = refs[:n], refs[n : n + nlow], refs[n + nlow : n + nlow + nhigh]
    x_ref, spread_ref, sel_ref, qc_ref, kc_ref, wide_ref = refs[-6:]
    zero = jnp.zeros((), jnp.bfloat16)
    blocks = []
    for w in range(n):
        part = got[0][...]
        for m in range(1, n):
            part = jnp.where((j - w + n) % n == m, got[m][...], part)
        blocks.append(part)

    def edge(parts, on):
        part = parts[0][...]
        for m in range(1, len(parts)):
            part = jnp.where(j == m, parts[m][...], part)
        return jnp.where(on, part, zero)

    window = window_of(seg_ref, wide_ref, row, member, F)
    before = ordinals(window, F)
    ext = jnp.concatenate([edge(lows, member > 0)] + blocks + [edge(highs, member < team - 1)], 0)
    ext_t = jnp.where(window[0:1, :] > 0, ext.T, zero)
    spread_ref[...] = place(ext_t, before, gaps, spread)
    local = pltpu.roll(window, F + 2 * HALO - HALO, 1)[:, :F]
    before_local = pltpu.roll(before, F + 2 * HALO - HALO, 1)[:, :F]
    which = lax.broadcasted_iota(jnp.int32, (8, F), 0)
    sel_ref[...] = (before_local == which).astype(jnp.float32)
    seg_col = column(local)
    length = F // n
    for w in range(n):
        rows = slice(w * length, (w + 1) * length)
        x_ref[rows, :] = jnp.where(seg_col[rows] > 0, blocks[w], zero)
    lane = lax.broadcasted_iota(jnp.int32, (1, 128), 1) % 64
    qc_ref[...] = (seg_col == lane.astype(jnp.float32)).astype(jnp.bfloat16)
    for s in range(team):
        start = pl.multiple_of(128 + (member - s + team) % team * F, 128)
        keys = column(wide_ref[:, pl.ds(start, F)])
        kc_ref[s * F : (s + 1) * F, :] = jnp.where(
            (keys == lane.astype(jnp.float32)) & (lane > 0), 0.0, -1e30
        ).astype(jnp.bfloat16)


def build_x(at, segments, got, lows, highs, team, F, gaps, spread, deps):
    n, W = len(got), got[0].shape[1]
    T = segments.shape[1]
    whole = pl.BlockSpec(memory_space=pltpu.VMEM)
    out = lambda r, c, kind: jax.ShapeDtypeStruct((r, c), kind)

    def full(r, c):
        return pl.BlockSpec((r, c), lambda i, at: (0, 0))

    return pl.pallas_call(
        functools.partial(
            build_x_kernel, n=n, nlow=len(lows), nhigh=len(highs), team=team, F=F, gaps=gaps, spread=spread
        ),
        grid_spec=pltpu.PrefetchScalarGridSpec(
            num_scalar_prefetch=1,
            grid=(1,),
            in_specs=[pl.BlockSpec((8, T), lambda i, at: (at[0] // 8, 0))]
            + [full(*a.shape) for a in (*got, *lows, *highs)] + [ANY] * len(deps),
            out_specs=[full(F, W), full(W, spread), full(8, F), full(F, 128), full(team * F, 128)],
            scratch_shapes=[pltpu.VMEM((8, T + 256), jnp.int32)],
        ),
        out_shape=[
            out(F, W, jnp.bfloat16), out(W, spread, jnp.bfloat16), out(8, F, jnp.float32),
            out(F, 128, jnp.bfloat16), out(team * F, 128, jnp.bfloat16),
        ],
        cost_estimate=pl.CostEstimate(flops=8 * W * spread, bytes_accessed=6 * W * spread, transcendentals=0),
        name="build_x",
    )(at, segments, *got, *lows, *highs, *deps)


def build_d_kernel(at_ref, seg_ref, d_ref, *refs, edges, team, F, gaps, length):
    row, member = at_ref[0], at_ref[1]
    out_ref, wide_ref = refs[-2:]
    window = window_of(seg_ref, wide_ref, row, member, F)
    before = ordinals(window, F)
    zero = jnp.zeros((), jnp.bfloat16)
    if edges:
        low, high = refs[0][...], refs[1][...]
        ext = jnp.concatenate(
            [jnp.where(member > 0, low, zero), d_ref[...], jnp.where(member < team - 1, high, zero)], 0
        ).T
    else:
        ext = d_ref[...].T
        before = pltpu.roll(before, F + 2 * HALO - HALO, 1)[:, :F]
    out_ref[...] = place(ext, before, gaps, length)


def build_d(at, segments, d, edges, team, gaps, length, deps=()):
    F, W = d.shape
    T = segments.shape[1]

    def full(r, c):
        return pl.BlockSpec((r, c), lambda i, at: (0, 0))

    return pl.pallas_call(
        functools.partial(build_d_kernel, edges=bool(edges), team=team, F=F, gaps=gaps, length=length),
        grid_spec=pltpu.PrefetchScalarGridSpec(
            num_scalar_prefetch=1,
            grid=(1,),
            in_specs=[pl.BlockSpec((8, T), lambda i, at: (at[0] // 8, 0)), full(F, W)]
            + [full(*a.shape) for a in edges] + [ANY] * len(deps),
            out_specs=full(W, length),
            scratch_shapes=[pltpu.VMEM((8, T + 256), jnp.int32)],
        ),
        out_shape=jax.ShapeDtypeStruct((W, length), jnp.bfloat16),
        cost_estimate=pl.CostEstimate(flops=8 * W * length, bytes_accessed=6 * W * length, transcendentals=0),
        name="build_d",
    )(at, segments, d, *edges, *deps)


def widen_kernel(*refs, n):
    for k in range(n):
        refs[len(refs) - n + k][...] = refs[k][...].astype(jnp.float32)


def widen(arrays, deps):
    whole = pl.BlockSpec(memory_space=pltpu.VMEM)
    size = sum(a.size for a in arrays)
    return pl.pallas_call(
        functools.partial(widen_kernel, n=len(arrays)),
        in_specs=[whole] * len(arrays) + [ANY] * len(deps),
        out_specs=[whole] * len(arrays),
        out_shape=[jax.ShapeDtypeStruct(a.shape, jnp.float32) for a in arrays],
        cost_estimate=pl.CostEstimate(flops=size, bytes_accessed=6 * size, transcendentals=0),
        name="widen",
    )(*arrays, *deps)

HEAD = 64

def nt(a, b):
    return lax.dot_general(a, b, (((1,), (1,)), ((), ())), preferred_element_type=jnp.float32)

def attn_fwd_kernel(*refs, P, chunk):
    q_ref, qc_ref, kc_ref = refs[:3]
    k_refs = refs[3:3+P]
    v_refs = refs[3+P:3+2*P]
    o_ref, lse_ref, ka_ref = refs[-3:]
    F = q_ref.shape[0]
    low_k = lax.broadcasted_iota(jnp.int32, (F, 128), 1) < HEAD
    low_q = lax.broadcasted_iota(jnp.int32, (chunk, 128), 1) < HEAD
    for h in range(2):
        pick = low_k if h == 0 else jnp.logical_not(low_k)
        for p in range(P):
            ka_ref[h, p*F:(p+1)*F, :] = jnp.where(pick, k_refs[p][...], kc_ref[p*F:(p+1)*F, :])
    for c in range(F // chunk):
        rows = slice(c*chunk, (c+1)*chunk)
        q = q_ref[rows, :] * jnp.asarray(0.125, jnp.bfloat16)
        outs, lses = [], []
        for h in range(2):
            pick = low_q if h == 0 else jnp.logical_not(low_q)
            qa = jnp.where(pick, q, qc_ref[rows, :])
            s = nt(qa, ka_ref[h])
            m = jnp.maximum(jnp.max(s, axis=1, keepdims=True), -1e20)
            e = jnp.exp(s - m)
            l = jnp.maximum(jnp.sum(e, axis=1, keepdims=True), 1.0)
            pb = (e * (1.0 / l)).astype(jnp.bfloat16)
            o = sum(jnp.dot(pb[:, p*F:(p+1)*F], v_refs[p][...], preferred_element_type=jnp.float32) for p in range(P))
            outs.append(o)
            lses.append(m + jnp.log(l))
        o_ref[rows, :] = jnp.where(low_q, outs[0], outs[1]).astype(o_ref.dtype)
        lse_ref[rows, :] = jnp.where(low_q, lses[0], lses[1])

def attn_fwd(q, kvs, qc, kc, deps, chunk=128):
    F, W = q.shape
    P = len(kvs)
    T = P * F
    npair = W // 128
    return pl.pallas_call(
        functools.partial(attn_fwd_kernel, P=P, chunk=min(chunk, F)),
        grid=(npair,),
        in_specs=[pl.BlockSpec((F, 128), lambda a: (0, a)),
                  pl.BlockSpec((F, 128), lambda a: (0, 0)),
                  pl.BlockSpec((T, 128), lambda a: (0, 0))]
                 + [pl.BlockSpec((F, 128), lambda a: (0, a))] * P
                 + [pl.BlockSpec((F, 128), lambda a, n=npair: (0, a + n))] * P
                 + [ANY] * len(deps),
        out_specs=[pl.BlockSpec((F, 128), lambda a: (0, a)), pl.BlockSpec((F, 128), lambda a: (0, a))],
        out_shape=[jax.ShapeDtypeStruct((F, W), jnp.bfloat16), jax.ShapeDtypeStruct((F, W), jnp.float32)],
        scratch_shapes=[pltpu.VMEM((2, T, 128), jnp.bfloat16)],
        cost_estimate=pl.CostEstimate(flops=16 * F * T * W, bytes_accessed=16 * T * W, transcendentals=0),
        name="attn_fwd",
    )(q, qc, kc, *kvs, *kvs, *deps)

def attn_bwd_kernel(*refs, P, chunk):
    q_ref, do_ref, o_ref, lse_ref, qc_ref, kc_ref = refs[:6]
    k_refs = refs[6:6+P]
    v_refs = refs[6+P:6+2*P]
    dq_ref, dk_ref, dv_ref = refs[-2-P:1-P]
    far_refs = refs[1-P:]
    F = q_ref.shape[0]
    low_q = lax.broadcasted_iota(jnp.int32, (F, 128), 1) < HEAD
    low_c = lax.broadcasted_iota(jnp.int32, (chunk, 128), 1) < HEAD
    q = q_ref[...] * jnp.asarray(0.125, jnp.bfloat16)
    do = do_ref[...]
    lse_t = lse_ref[...].T
    prod_t = (do.astype(jnp.float32) * o_ref[...].astype(jnp.float32)).T
    lse_row = [lse_t[h*HEAD:h*HEAD+1, :] for h in range(2)]
    delta_row = [jnp.sum(prod_t[h*HEAD:(h+1)*HEAD, :], axis=0, keepdims=True) for h in range(2)]
    qa = [jnp.where(low_q if h == 0 else jnp.logical_not(low_q), q, qc_ref[...]) for h in range(2)]
    zero = jnp.zeros((), jnp.bfloat16)
    dqt = [jnp.zeros((HEAD, F), jnp.float32) for _ in range(2)]
    for p in range(P):
        for c in range(F // chunk):
            rows = slice(c*chunk, (c+1)*chunk)
            k = k_refs[p][rows, :]
            v = v_refs[p][rows, :]
            kc = kc_ref[p*F + c*chunk: p*F + (c+1)*chunk, :]
            kt = k.T
            dks, dvs = [], []
            for h in range(2):
                pick = low_c if h == 0 else jnp.logical_not(low_c)
                st = nt(jnp.where(pick, k, kc), qa[h])
                pt = jnp.exp(st - lse_row[h])
                dpt = nt(jnp.where(pick, v, zero), do)
                dst = (pt * (dpt - delta_row[h])).astype(jnp.bfloat16)
                dvs.append(jnp.dot(pt.astype(jnp.bfloat16), do, preferred_element_type=jnp.float32))
                dks.append(jnp.dot(dst, q, preferred_element_type=jnp.float32))
                dqt[h] = dqt[h] + jnp.dot(kt[h*HEAD:(h+1)*HEAD, :], dst, preferred_element_type=jnp.float32)
            dk = jnp.where(low_c, dks[0], dks[1])
            dv = jnp.where(low_c, dvs[0], dvs[1])
            if p == 0:
                dk_ref[rows, :] = dk
                dv_ref[rows, :] = dv
            else:
                far_refs[p-1][0, rows, :] = dk.astype(jnp.bfloat16)
                far_refs[p-1][1, rows, :] = dv.astype(jnp.bfloat16)
    dq = jnp.concatenate(dqt, axis=0).T * 0.125
    dq_ref[...] = dq.astype(dq_ref.dtype)

def attn_bwd(q, do, o, lse, kvs, qc, kc, first, count, deps, chunk=128):
    F, W = q.shape
    P = len(kvs)
    T = P * F
    npair = W // 128
    own = pl.BlockSpec((F, 128), lambda a: (0, a + first))
    out = pl.BlockSpec((F, 128), lambda a: (0, a))
    return pl.pallas_call(
        functools.partial(attn_bwd_kernel, P=P, chunk=min(chunk, F)),
        grid=(count,),
        in_specs=[own, own, own, own,
                  pl.BlockSpec((F, 128), lambda a: (0, 0)),
                  pl.BlockSpec((T, 128), lambda a: (0, 0))]
                 + [own] * P
                 + [pl.BlockSpec((F, 128), lambda a, n=npair: (0, a + first + n))] * P
                 + [ANY] * len(deps),
        out_specs=[out] * 3 + [pl.BlockSpec((2, F, 128), lambda a: (0, 0, a))] * (P - 1),
        out_shape=[jax.ShapeDtypeStruct((F, 128 * count), t) for t in (jnp.bfloat16, jnp.float32, jnp.float32)]
                  + [jax.ShapeDtypeStruct((2, F, 128 * count), jnp.bfloat16)] * (P - 1),
        cost_estimate=pl.CostEstimate(flops=20 * F * T * 128 * count, bytes_accessed=16 * T * W, transcendentals=0),
        name="attn_bwd",
    )(q, do, o, lse, qc, kc, *kvs, *kvs, *deps)

HALO = 64
UTT_LEAST = 256
root_half = 0.7071067811865476
inv_root_two_pi = 0.3989422804014327
f32 = jnp.float32
bf16 = jnp.bfloat16


def layer_norm(hidden):
    centred = hidden - jnp.mean(hidden, axis=-1, keepdims=True)
    inv_scale = lax.rsqrt(jnp.mean(centred * centred, axis=-1, keepdims=True) + 1e-05)
    return (centred * inv_scale, inv_scale)


def norm_back(grad_normed, normed, inv_scale):
    return inv_scale * (
        grad_normed
        - jnp.mean(grad_normed, axis=-1, keepdims=True)
        - normed * jnp.mean(grad_normed * normed, axis=-1, keepdims=True)
    )


def gelu(entries):
    return 0.5 * entries * (1.0 + lax.erf(entries * root_half))


def gelu_slope(entries):
    return (
        0.5 * (1.0 + lax.erf(entries * root_half))
        + entries * jnp.exp(-0.5 * entries * entries) * inv_root_two_pi
    )


def mm(a, b):
    return jnp.dot(a, b, preferred_element_type=f32)


def mm_back(a, b):
    return lax.dot_general(a, b, (((1,), (1,)), ((), ())), preferred_element_type=f32)


def wgrad(a, b):
    return lax.dot_general(a, b, (((0,), (0,)), ((), ())), preferred_element_type=f32)


class Plan:
    def __init__(self, dp, seq, rows_dev):
        self.dp, self.seq, self.n = dp, seq, rows_dev
        self.q = seq // (2 * rows_dev)
        self.P = 2 * self.q
        assert dp % 2 == 0 and self.q * 2 * rows_dev == seq and rows_dev > 1

    def out_pairs(self, m):
        pairs = []
        for d in range(self.dp):
            for z in range(self.seq):
                rho = self.n * (d % 2) + (z + m) % self.n
                u = z // self.n
                pairs.append((d * self.seq + z, self.member(d // 2, rho, u)))
        return pairs

    def edge_pairs(self):
        heads = [[] for _ in range(self.n)]
        tails = [[] for _ in range(self.n)]
        for d in range(self.dp):
            for z in range(self.seq):
                u = z // self.n
                for j in range(self.n):
                    rho = self.n * (d % 2) + j
                    if z % self.n == self.n - 1 and u + 1 < self.P:
                        tails[j].append((d * self.seq + z, self.member(d // 2, rho, u + 1)))
                    if z % self.n == 0 and u > 0:
                        heads[j].append((d * self.seq + z, self.member(d // 2, rho, u - 1)))
        return heads, tails

    def member(self, e, rho, u):
        return (2 * e + u % 2) * self.seq + rho * self.q + u // 2

    def team_pairs(self, shift, wrap):
        pairs = []
        for e in range(self.dp // 2):
            for rho in range(2 * self.n):
                for u in range(self.P):
                    to = u + shift
                    if wrap or 0 <= to < self.P:
                        pairs.append((self.member(e, rho, u), self.member(e, rho, to % self.P)))
        return pairs


BOTH = ("dp", "seq")


def on_device(
    frames,
    output_gradient,
    segments,
    layer_keep,
    conv_weight,
    convolution_bias,
    query_matrix,
    query_offset_bias,
    key_matrix,
    value_matrix,
    value_offset_bias,
    attn_weight,
    attn_bias,
    first_gain,
    first_shift,
    inner_weight,
    inner_bias,
    outer_weight,
    outer_bias,
    second_gain,
    second_shift,
):
    rows_dev, local_len, width = frames.shape
    total_rows, row_len = segments.shape
    dp_count, seq_count = lax.axis_size("dp"), lax.axis_size("seq")
    dp_index, seq_index = lax.axis_index("dp"), lax.axis_index("seq")
    plan = Plan(dp_count, seq_count, rows_dev)
    n, q, team = plan.n, plan.q, plan.P
    F = row_len // team
    taps, _, gw = conv_weight.shape
    tap_blocks = taps // DK
    rho = seq_index // q
    member = (seq_index % q) * 2 + dp_index % 2
    row_id = (dp_index // 2) * (2 * n) + rho

    def pick(parts, index):
        out = parts[0]
        for k in range(1, len(parts)):
            out = jnp.where(index == k, parts[k], out)
        return out

    def blocks_to_team(a):
        got = []
        for m in range(n):
            sent = pick([a[j] for j in range(n)], (seq_index + m) % n)
            got.append(lax.ppermute(sent, BOTH, plan.out_pairs(m)))
        return got

    def to_team(a):
        got = blocks_to_team(a)
        j = rho % n
        return jnp.concatenate([pick(got, (j - w) % n) for w in range(n)], 0)

    def from_team(sent):
        back = [
            lax.ppermute(sent[m], BOTH, [(t, s) for s, t in plan.out_pairs(m)]) for m in range(n)
        ]
        return jnp.stack([pick(back, (row - seq_index) % n) for row in range(n)], 0)

    def edges_to_team(a):
        heads, tails = plan.edge_pairs()
        lows, highs = [], []
        for j in range(n):
            tail, head = a[j, local_len - HALO :], a[j, :HALO]
            if team == 2:
                got = lax.ppermute(
                    jnp.where(seq_index % n == 0, head, tail), BOTH, heads[j] + tails[j]
                )
                lows.append(got)
                highs.append(got)
            else:
                lows.append(lax.ppermute(tail, BOTH, tails[j]))
                highs.append(lax.ppermute(head, BOTH, heads[j]))
        return lows, highs

    def edges(a):
        if team == 2:
            got = lax.ppermute(
                jnp.where(member == 0, a[F - HALO :], a[:HALO]), BOTH, plan.team_pairs(1, True)
            )
            return got, got
        low = lax.ppermute(a[F - HALO :], BOTH, plan.team_pairs(1, False))
        high = lax.ppermute(a[:HALO], BOTH, plan.team_pairs(-1, False))
        return low, high

    def pairs_of(axis, bit):
        pairs = []
        for d in range(dp_count):
            for z in range(seq_count):
                to = (d ^ bit, z) if axis == "dp" else (d, z ^ bit)
                pairs.append((d * seq_count + z, to[0] * seq_count + to[1]))
        return pairs

    def halve(a, axis, index, bit, high, low):
        mine = (index // bit) % 2
        a = a.reshape((high, 2, low) + a.shape[1:])
        sent = pick([a[:, 0], a[:, 1]], 1 - mine).reshape((high * low,) + a.shape[3:])
        kept = pick([a[:, 0], a[:, 1]], mine).reshape(sent.shape)
        return kept, lax.ppermute(sent, BOTH, pairs_of(axis, bit)), sent

    class Scatter:
        def __init__(self, halves, swap, many=1):
            bits = [1 << i for i in range(dp_count.bit_length() - 1)]
            order = [1] + (bits[1:] if swap else bits[:0:-1])
            left = list(reversed(bits))
            self.steps = []
            for bit in order:
                at = left.index(bit)
                self.steps.append((bit, many * 2**at, 2 ** (len(left) - 1 - at)))
                left.remove(bit)
            self.steps.pop(0)
            self.sent, self.kept = halves
            self.got = lax.ppermute(self.sent, BOTH, pairs_of("dp", 1))

        def step(self, *deps):
            bit, high, low = self.steps.pop(0)
            mine = ((dp_index // bit) % 2).astype(jnp.int32).reshape(1)
            self.sent, self.kept = join_split(self.kept, self.got, mine, high, low, deps)
            self.got = lax.ppermute(self.sent, BOTH, pairs_of("dp", bit))

        def last(self, *deps):
            while self.steps:
                self.step(*deps)
            return join_last(self.kept, self.got, deps)

    class SeqSum:
        def __init__(self, a):
            self.shape = a.shape
            self.a = a.astype(bf16).reshape(seq_count, -1, a.shape[1])
            bits = [1 << i for i in range(seq_count.bit_length() - 1)]
            left = list(reversed(bits))
            self.steps = []
            for bit in bits:
                at = left.index(bit)
                self.steps.append((bit, 2**at, 2 ** (len(left) - 1 - at)))
                left.remove(bit)
            self.back = list(reversed(bits))
            bit, high, low = self.steps.pop(0)
            self.kept, self.got, self.sent = halve(self.a, "seq", seq_index, bit, high, low)

        def step(self, *deps):
            if self.steps:
                bit, high, low = self.steps.pop(0)
                mine = ((seq_index // bit) % 2).astype(jnp.int32).reshape(1)
                self.sent, self.kept = join_split(self.kept, self.got, mine, high, low, deps)
                self.got = lax.ppermute(self.sent, BOTH, pairs_of("seq", bit))

        def whole(self):
            self.add()
            return self.finish()

        def add(self, *deps):
            while self.steps:
                self.step(*deps)
            self.a = join_last(self.kept, self.got, deps).reshape(self.kept.shape)

        def finish(self, *deps):
            a = self.a
            for bit in self.back:
                other = lax.ppermute(a, BOTH, pairs_of("seq", bit))
                low_half = (seq_index // bit) % 2 == 0
                pair = jnp.where(low_half, jnp.stack([a, other], 1), jnp.stack([other, a], 1))
                a = pair.reshape((-1,) + a.shape[1:])
            return a.reshape(self.shape)

    def by_dp(a):
        return a.reshape(dp_count, -1, a.shape[-1])

    def by_share(a):
        a = a.reshape(dp_count, width // dp_count, a.shape[1])
        out, sent = [], []
        for k in range(dp_count):
            piece = lax.dynamic_index_in_dim(a, dp_index ^ k, 0, keepdims=False)
            sent.append(piece)
            out.append(piece if k == 0 else lax.ppermute(piece, BOTH, pairs_of("dp", k)))
        return out, sent

    weight_tr = prep(conv_weight)

    x_blocks = blocks_to_team(frames)
    x_lows, x_highs = edges_to_team(frames)
    grad_out = to_team(output_gradient)

    keep = (lax.dynamic_index_in_dim(layer_keep, row_id, 0, keepdims=False) > 0).astype(f32)
    gaps = 1 + max(F - 2, 0) // UTT_LEAST
    spread = -(-(F + 2 * HALO + HALO * gaps) // 128) * 128
    out_spread = -(-(F + HALO * gaps) // 128) * 128
    where_at = jnp.stack([row_id, member, rho % n]).astype(jnp.int32)
    x, spread_x, select, q_codes, k_codes = build_x(
        where_at, segments, x_blocks, x_lows, x_highs, team, F, gaps, spread, (weight_tr,)
    )
    conv_t = conv(spread_x, weight_tr, select, F, gaps)
    x_shares = lax.all_to_all(
        spread_x.reshape(dp_count, width // dp_count, spread), "dp", 0, 0, tiled=True
    )

    conv_before, pos_out, pos_low, query, kv = front(
        conv_t, convolution_bias, x, query_matrix, key_matrix, value_matrix, query_offset_bias,
        value_offset_bias, (),
    )
    kvs = [kv] + [lax.ppermute(kv, BOTH, plan.team_pairs(s, True)) for s in range(1, team)]
    attn_low, lse = attn_fwd(query, kvs, q_codes, k_codes, (x_shares,), 256)

    back_at = ((rho % n - jnp.arange(n, dtype=jnp.int32)) % n).astype(jnp.int32)
    (
        layer_sent, first_low, inner_low, grad_outer_low, grad_inner_low, grad_attn_low,
        grad_first_sum, grad_heads, inner_sums, mid_sums,
    ) = mid(
        keep.reshape(1), attn_low, pos_out, grad_out, attn_weight, inner_weight, outer_weight,
        attn_bias, first_gain, first_shift, inner_bias, outer_bias, second_gain, second_shift, (),
    )
    layer_sent = [layer_sent[k * local_len : (k + 1) * local_len] for k in range(n)]
    layer_sent = [pick(layer_sent, back_at[m]) for m in range(n)]
    layer_out = from_team(layer_sent)
    core = (dp_index % 2).astype(jnp.int32).reshape(1)
    outer_sum = Scatter(wg_rows(core, grad_outer_low, inner_low, 1, dp_count, 4, (), tuple(layer_sent)), False)
    by_rows = (inner_weight.shape[1] // dp_count) % 128 != 0
    if by_rows:
        halves = wg_rows(core, grad_inner_low, first_low, 1, dp_count, 1, (), (outer_sum.sent,))
    else:
        halves = wg_cols(core, first_low, grad_inner_low, dp_count, (outer_sum.sent,))
    inner_sum = Scatter(halves, True)
    extras = (inner_sums, mid_sums)
    pairs = width // 128
    grads = []
    deps = (outer_sum.sent, inner_sum.sent)
    for k in range(2):
        grads.append(
            attn_bwd(
                query, grad_heads, attn_low, lse, kvs, q_codes, k_codes, k * pairs // 2, pairs // 2,
                deps, 256,
            )
        )
        if k == 0:
            outer_sum.step(grads[0][0])
            inner_sum.step(outer_sum.sent)
            deps = (inner_sum.sent,)
    fars = [
        [lax.ppermute(g[2 + s], BOTH, plan.team_pairs(-s, True)) for s in range(1, team)]
        for g in grads
    ]
    low_qk, low_v, grad_pos, grad_conv_low, qk_sums, v_sums = dpos(
        keep.reshape(1), *[[g[k] for g in grads] for k in range(3)], fars, query_matrix,
        key_matrix, value_matrix, grad_first_sum, grad_out, conv_before, (),
    )

    d_pieces = build_d(where_at, segments, grad_conv_low, (), team, gaps, out_spread).reshape(
        dp_count, width // dp_count, out_spread
    )
    d_shares = lax.all_to_all(d_pieces, "dp", 0, 0, tiled=True)
    low, high = edges(grad_conv_low)
    outer_sum.step(d_pieces)
    inner_sum.step(outer_sum.sent)
    slots = 2 * dp_count // 2
    qk_sum = Scatter(
        wg_rows(core, low_qk, pos_low, 2, dp_count, 1, (qk_sums,), (inner_sum.sent,)), True, 2
    )
    halves = wg_rows(core, low_v, pos_low, 1, dp_count, 1, (v_sums,), (qk_sum.sent,), slots)
    halves = wg_rows(core, grad_attn_low, attn_low, 1, dp_count, 1, extras, (), slots, 1, halves)
    va_sum = Scatter(halves, False, 2)
    spread_d = build_d(
        where_at, segments, grad_conv_low, (low, high), team, gaps, spread, (va_sum.sent,)
    )
    outer_share = outer_sum.last(va_sum.sent)
    inner_share = inner_sum.last(outer_share)
    o_g, i_g = lax.psum((outer_share, inner_share), "seq")

    group_count = width // dp_count // gw
    deps = (inner_share, spread_d)
    conv_sums = []
    for group in range(group_count):
        part = conv_dw(x_shares, d_shares, group, gw, tap_blocks, deps)
        conv_sums.append(SeqSum(part))
        deps = (conv_sums[-1].sent,)
        if group == 0:
            qk_sum.step(*deps)
            va_sum.step(qk_sum.sent)
            deps = (va_sum.sent,)
    groups = width // gw
    back_a = conv_dx(spread_d, weight_tr, select, F, gaps, 0, groups // 2, deps)
    deps = (back_a,)
    for c in conv_sums:
        c.step(*deps)
        deps = (c.sent,)
    qk_sum.step(*deps)
    va_sum.step(qk_sum.sent)
    deps = (va_sum.sent,)
    back_b = conv_dx(spread_d, weight_tr, select, F, gaps, groups // 2, groups - groups // 2, deps)
    deps = (back_b,)
    for c in conv_sums:
        c.add(*deps)
        deps = (c.a,)
    qk_share = qk_sum.last(*deps)
    va_share = va_sum.last(qk_share)
    conv_back = jnp.concatenate([back_a, back_b], 0)
    seg_row = lax.dynamic_index_in_dim(segments, row_id, 0, keepdims=False)
    live = lax.dynamic_slice_in_dim(seg_row, member * F, F) > 0
    grad_in = jnp.where(live[:, None], grad_pos + conv_back.T, 0.0).astype(bf16)
    grad_in = [grad_in[k * local_len : (k + 1) * local_len] for k in range(n)]
    grad_in = [pick(grad_in, back_at[m]) for m in range(n)]
    grad_input = from_team(grad_in)
    proj = SeqSum(jnp.concatenate([qk_share, va_share], 0))
    conv_sums = [c.finish() for c in conv_sums]
    proj_pack = proj.whole().astype(f32)
    o_g, i_g = widen((o_g, i_g), tuple(conv_sums))
    o_g = o_g.T
    i_g = i_g.T if by_rows else i_g
    grad_conv_weight = finish_dw(conv_sums, gw, tap_blocks)
    grad_conv_bias = jnp.concatenate([c[tap_blocks * gw, :gw] for c in conv_sums]).astype(f32)

    share = width // dp_count
    ff = inner_bias.shape[0]
    pieces = proj_pack.reshape(4, -1, width)
    q_g, k_g, v_g, a_g = (pieces[k, :share].T for k in range(4))
    small = pieces[3, share : share + ff // width + 6]
    inner_bias_share = lax.dynamic_slice_in_dim(
        small[: ff // width].reshape(-1), dp_index * (ff // dp_count), ff // dp_count
    )
    rows_ = jnp.concatenate(
        [small[ff // width :], pieces[0, share : share + 1], pieces[2, share : share + 1]]
    )
    rows_ = lax.dynamic_slice_in_dim(rows_, dp_index * share, share, 1)
    vecs = [rows_[6], rows_[7]] + [rows_[k] for k in range(6)] + [grad_conv_bias]
    return (
        layer_out,
        grad_input,
        grad_conv_weight,
        vecs[8],
        q_g,
        vecs[0],
        k_g,
        v_g,
        vecs[1],
        a_g,
        vecs[2],
        vecs[3],
        vecs[4],
        i_g,
        inner_bias_share,
        o_g,
        vecs[5],
        vecs[6],
        vecs[7],
    )


def solution(mesh):
    rows = P("dp", "seq", None)
    by_col, vec = P(None, "dp"), P("dp")
    out_specs = (
        rows, rows, P(None, "dp", None), vec, by_col, vec, by_col, by_col, vec, by_col, vec, vec,
        vec, by_col, vec, by_col, vec, vec, vec,
    )
    return jax.shard_map(
        on_device, mesh=mesh, in_specs=(rows, rows) + (P(),) * 19, out_specs=out_specs, check_vma=False
    )
```

time: 694 us -> 434 us (0.63)
  the two profiles are of different devices: /device:TPU:1 before, /device:TPU:0 now
where the time goes in v2:
time: 434 us; the launch traced here: 427 us
  Pallas kernels  247 us (57%)
  starting transfers between devices  61.7 us (14%)
  waiting for transfers between devices  48.4 us (11%)
  local copies, waits for them, and re-layouts  33.8 us (8%)
  other arithmetic  18.8 us (4%)
  between operations  17.2 us (4%)
    pallas_call x11, Pallas kernels, join_split(): pl.pallas_call(join_kernel, grid_spec=pltpu.PrefetchScalarGridSpec(num_sc...  30.7 us
    pallas_call x2, Pallas kernels, conv_dx(): pl.pallas_call(functools.partial(dx_kernel, nb=nb, gw=gw, F=F, nbound=nbo...  24.5 us
    pallas_call x1, Pallas kernels, mid(): pl.pallas_call(functools.partial(mid_kernel, ndeps=len(deps), chunk=min(7...  23.1 us
    pallas_call x2, Pallas kernels, attn_bwd(): pl.pallas_call(functools.partial(attn_bwd_kernel, P=P, chunk=min(chunk, F...  22.4 us
    ppermute x6, waiting for transfers between devices, finish(): other = lax.ppermute(a, BOTH, pairs_of('seq', bit))  20.6 us
    pallas_call x1, Pallas kernels, prep(): pl.pallas_call(prep_kernel, grid=(groups // slots, nb), in_specs=[pl.Bloc...  19.1 us
    pallas_call x1, Pallas kernels, conv(): pl.pallas_call(functools.partial(conv_kernel, nb=nb, gw=gw, F=F, nbound=n...  18.8 us
    pallas_call x1, Pallas kernels, attn_fwd(): pl.pallas_call(functools.partial(attn_fwd_kernel, P=P, chunk=min(chunk, F...  18.6 us
  transfers between devices with their start and end apart: 41, of which 7 were waited for; matrix products, arithmetic and copies ran while one was open for 7% of the time, Pallas kernels for 40%

profile of v2, /device:TPU:0, one launch (start us, length us, event | category | flops | bytes accessed | tf_op | source)
XLA Modules:
  0.0 426.8 jit_solution(8480966113004254098)
XLA Ops:
  16.7 19.1 %prep.1.refs_6_.wt_ref = bf16[16,384,768]{2,1,0:T(8,128)(2,1)} custom-call(bf16[128,48,768]{2,1,0:T(8,128)(2,1)} %bitcast.159), custom_call_target="tpu_custom_call" | custom-call | flops 1000000000 | bytes 18874368 | tf_op jit(solution)/shard_map/prep/pallas_call | solution.py:44
  37.3 4.4 %build_x.1 = (bf16[512,768]{1,0:T(8,128)(2,1)}, bf16[768,768]{1,0:T(8,128)(2,1)}, f32[8,512]{1,0:T(8,128)}, bf16[512,128]{1,0:T(8,128)(2,1)}, bf16[1024,128]{1,0:T(8,128)(2,1)}) custom-call(s32[3]{0:T(128)} %pad_add_fusion.at_ref, s32[16,1024]{1,0:T(8,128)} %seg_ref.5, bf16[256,768]{1,0:T(8,128)(2,1)} %copy-done.23, bf16[256,768]{1,0:T(8,128)(2,1)} %copy-done.24, ...), custom_call_target="tpu_custom_call" | custom-call | flops 4718592 | bytes 3538944 | tf_op jit(solution)/shard_map/build_x/pallas_call | solution.py:683
  41.7 18.8 %conv_fwd.1.conv_ref = f32[768,512]{1,0:T(8,128)} custom-call(bf16[768,768]{1,0:T(8,128)(2,1)} %get-tuple-element.89.xt_ref, bf16[16,384,768]{2,1,0:T(8,128)(2,1)} %prep.1.refs_6_.wt_ref, f32[8,512]{1,0:T(8,128)} %get-tuple-element.90.sel_ref), custom_call_target="tpu_custom_call" | custom-call | flops 7247757312 | bytes 9437184 | tf_op jit(solution)/shard_map/conv_fwd/pallas_call | solution.py:75
  60.5 6.0 %front.1 = (f32[512,768]{1,0:T(8,128)}, f32[512,768]{1,0:T(8,128)}, bf16[512,768]{1,0:T(8,128)(2,1)}, bf16[512,768]{1,0:T(8,128)(2,1)}, bf16[512,1536]{1,0:T(8,128)(2,1)}) custom-call(f32[768,512]{1,0:T(8,128)} %conv_fwd.1.conv_ref, f32[1,768]{1,0:T(1,128)} %reshape.460.bias_ref, bf16[512,768]{1,0:T(8,128)(2,1)} %get-tuple-element.91.x_ref, ...), custom_call_target="tpu_custom_call" | custom-call | flops 1811939328 | bytes 11403264 | tf_op jit(solution)/shard_map/front/pallas_call | solution.py:473
  70.0 3.9 all-to-all-start
  74.8 3.6 collective-permute-start.5
  92.2 18.6 %attn_fwd.1 = (bf16[512,768]{1,0:T(8,128)(2,1)}, f32[512,768]{1,0:T(8,128)}) custom-call(bf16[512,768]{1,0:T(8,128)(2,1)} %get-tuple-element.92.refs_0_, bf16[512,128]{1,0:T(8,128)(2,1)} %get-tuple-element.93.refs_1_.refs_4_, bf16[1024,128]{1,0:T(8,128)(2,1)} %get-tuple-element.94.refs_2_.refs_5_, ...), custom_call_target="tpu_custom_call" | custom-call | flops 6442450944 | bytes 12582912 | tf_op jit(solution)/shard_map/attn_fwd/pallas_call | solution.py:801
  110.8 23.1 %mid.1 = (bf16[512,768]{1,0:T(8,128)(2,1)}, bf16[512,768]{1,0:T(8,128)(2,1)}, bf16[512,3072]{1,0:T(8,128)(2,1)}, bf16[512,768]{1,0:T(8,128)(2,1)}, bf16[512,3072...) custom-call(f32[1]{0:T(128)S(6)} %convert_element_type.23.keep_ref, ...), custom_call_target="tpu_custom_call" | custom-call | flops 10871635968 | bytes 37748736 | tf_op jit(solution)/shard_map/mid/pallas_call | solution.py:568
  140.2 6.4 %wg_rows.4 = (bf16[4,96,3072]{2,1,0:T(8,128)(2,1)}, bf16[4,96,3072]{2,1,0:T(8,128)(2,1)}) custom-call(s32[1]{0:T(128)} %bitcast.2.mine_ref, bf16[512,768]{1,0:T(8,128)(2,1)} %get-tuple-element.101.lhs_ref, bf16[512,3072]{1,0:T(8,128)(2,1)} %get-tuple-element.102.rhs_ref, bf16[256,768]{1,0:T(8,128)(2,1)} %copy.56.refs_0_, bf16[256,768]{1,0:T(8,128)(2,1)} %copy.57.refs_1_), custom_call_target="tpu_custom_call" | custom-call | flops 2415919104 | bytes 4718592 | tf_op jit(solution)/shard_map/wg_rows/pallas_call | solution.py:306
  146.5 7.5 %collective-permute-start.10 = (bf16[4,96,3072]{2,1,0:T(8,128)(2,1)}, bf16[4,96,3072]{2,1,0:T(8,128)(2,1)S(1)}, u32[]{:S(2)}, u32[]{:S(2)}) collective-permute-start(bf16[4,96,3072]{2,1,0:T(8,128)(2,1)} %get-tuple-element.103.refs_0_.refs_10_), channel_id=1, source_target_pairs={{0,4},{1,5},{2,6},{3,7},{4,0},{5,1},{6,2},{7,3},{8,12},{9,13},{10,... | collective-permute-start | bytes 7077896 | tf_op jit(solution)/shard_map/ppermute | solution.py:1091
  154.0 9.7 %wg_cols.1 = (bf16[4,768,384]{2,1,0:T(8,128)(2,1)}, bf16[4,768,384]{2,1,0:T(8,128)(2,1)}) custom-call(s32[1]{0:T(128)} %bitcast.2.mine_ref, bf16[512,768]{1,0:T(8,128)(2,1)} %get-tuple-element.104.lhs_ref, bf16[512,3072]{1,0:T(8,128)(2,1)} %get-tuple-element.105.rhs_ref, bf16[4,96,3072]{2,1,0:T(8,128)(2,1)} %get-tuple-element.103.refs_0_.refs_10_), custom_call_target="tpu_custom_call" | custom-call | flops 2415919104 | bytes 4718592 | tf_op jit(solution)/shard_map/wg_cols/pallas_call | solution.py:360
  163.7 11.2 %attn_bwd.2 = (bf16[512,384]{1,0:T(8,128)(2,1)}, f32[512,384]{1,0:T(8,128)}, f32[512,384]{1,0:T(8,128)}, bf16[2,512,384]{2,1,0:T(8,128)(2,1)}) custom-call(bf16[512,768]{1,0:T(8,128)(2,1)} %get-tuple-element.92.refs_0_, bf16[512,768]{1,0:T(8,128)(2,1)} %get-tuple-element.99.refs_1_, bf16[512,768]{1,0:T(8,128)(2,1)} %get-tuple-element.96.attn_ref.refs_2_.rhs_ref, ...), custom_call_target="tpu_custom_call" | custom-call | flops 4026531840 | bytes 12582912 | tf_op jit(solution)/shard_map/attn_bwd/pallas_call | solution.py:870
  176.9 3.5 join.11
  182.0 3.5 join.12
  187.0 11.2 %attn_bwd.3 = (bf16[512,384]{1,0:T(8,128)(2,1)}, f32[512,384]{1,0:T(8,128)}, f32[512,384]{1,0:T(8,128)}, bf16[2,512,384]{2,1,0:T(8,128)(2,1)}) custom-call(bf16[512,768]{1,0:T(8,128)(2,1)} %get-tuple-element.92.refs_0_, bf16[512,768]{1,0:T(8,128)(2,1)} %get-tuple-element.99.refs_1_, bf16[512,768]{1,0:T(8,128)(2,1)} %get-tuple-element.96.attn_ref.refs_2_.rhs_ref, ...), custom_call_target="tpu_custom_call" | custom-call | flops 4026531840 | bytes 12582912 | tf_op jit(solution)/shard_map/attn_bwd/pallas_call | solution.py:870
  198.4 4.5 %collective-permute-start.8 = (bf16[256,768]{0,1:T(8,128)(2,1)}, bf16[256,768]{0,1:T(8,128)(2,1)}, u32[]{:S(2)}, u32[]{:S(2)}) collective-permute-start(bf16[256,768]{0,1:T(8,128)(2,1)} %get-tuple-element.211), channel_id=1, source_target_pairs={{0,0},{1,1},{4,2},{5,3},{2,4},{3,5},{6,6},{7,7},{8,8},{9,9},{12,10... | collective-permute-start | bytes 1179656 | tf_op jit(solution)/shard_map/ppermute | solution.py:1034
  203.7 7.5 %dpos.1 = (bf16[512,1536]{1,0:T(8,128)(2,1)}, bf16[512,768]{1,0:T(8,128)(2,1)}, f32[512,768]{1,0:T(8,128)}, bf16[512,768]{1,0:T(8,128)(2,1)}, f32[8,1536]{1,0:T(8,128)}, /*index=5*/f32[8,768]{1,0:T(8,128)}) custom-call(f32[1]{0:T(128)S(6)} %convert_element_type.23.keep_ref, bf16[512,384]{1,0:T(8,128)(2,1)} %get-tuple-element.107.refs_0_, ...), custom_call_target="tpu_custom_call" | custom-call | flops 1811939328 | bytes 11403264 | tf_op jit(solution)/shard_map/dpos/pallas_call | solution.py:424
  211.2 3.6 build_d.2
  214.8 3.8 all-to-all-start.1
  226.2 5.0 %wg_rows.5 = (bf16[8,112,768]{2,1,0:T(8,128)(2,1)}, bf16[8,112,768]{2,1,0:T(8,128)(2,1)}) custom-call(s32[1]{0:T(128)} %bitcast.2.mine_ref, bf16[512,1536]{1,0:T(8,128)(2,1)} %get-tuple-element.129.lhs_ref, bf16[512,768]{1,0:T(8,128)(2,1)} %get-tuple-element.127.rhs_ref, f32[8,1536]{1,0:T(8,128)} %get-tuple-element.130.refs_0_, ...), custom_call_target="tpu_custom_call" | custom-call | flops 1207959552 | bytes 2359296 | tf_op jit(solution)/shard_map/wg_rows/pallas_call | solution.py:306
  235.0 3.5 wg_rows.7
  248.9 3.8 build_d.3.refs_17_.dt_ref
  260.6 6.7 %conv_dw.2 = f32[416,768]{1,0:T(8,128)} custom-call(bf16[8,96,768]{2,1,0:T(8,128)(2,1)} %copy-done, bf16[8,96,768]{2,1,0:T(8,128)(2,1)} %copy-done, bf16[8,96,768]{2,1,0:T(8,128)(2,1)} %copy-done, bf16[8,96,768]{2,1,0:T(8,128)(2,1)} %copy-done, bf16[8,96,768]{2,1,0:T(8,128)(2,1)} %copy-done, bf16[8,96,768]{2,1,0:T(8,128)(2,1)} %copy-done, ...), custom_call_target="tpu_custom_call" | custom-call | flops 3623878656 | bytes 1277952 | tf_op jit(solution)/shard_map/conv_dw/pallas_call | solution.py:157
  272.4 4.1 join.15
  278.2 3.9 join.16
  283.5 6.7 %conv_dw.3 = f32[416,768]{1,0:T(8,128)} custom-call(bf16[8,96,768]{2,1,0:T(8,128)(2,1)} %copy-done, bf16[8,96,768]{2,1,0:T(8,128)(2,1)} %copy-done, bf16[8,96,768]{2,1,0:T(8,128)(2,1)} %copy-done, bf16[8,96,768]{2,1,0:T(8,128)(2,1)} %copy-done, bf16[8,96,768]{2,1,0:T(8,128)(2,1)} %copy-done, bf16[8,96,768]{2,1,0:T(8,128)(2,1)} %copy-done, ...), custom_call_target="tpu_custom_call" | custom-call | flops 3623878656 | bytes 1277952 | tf_op jit(solution)/shard_map/conv_dw/pallas_call | solution.py:157
  292.5 12.2 %conv_dx.2.refs_0_ = f32[384,512]{1,0:T(8,128)} custom-call(bf16[768,768]{1,0:T(8,128)(2,1)} %build_d.3.refs_17_.dt_ref, bf16[16,384,768]{2,1,0:T(8,128)(2,1)} %prep.1.refs_6_.wt_ref, f32[8,512]{1,0:T(8,128)} %get-tuple-element.90.sel_ref, bf16[2,104,768]{2,1,0:T(8,128)(2,1)} %get-tuple-element.225.refs_0_), custom_call_target="tpu_custom_call" | custom-call | flops 3623878656 | bytes 4718592 | tf_op jit(solution)/shard_map/conv_dx/pallas_call | solution.py:111
  318.2 12.3 %conv_dx.3.refs_0_ = f32[384,512]{1,0:T(8,128)} custom-call(bf16[768,768]{1,0:T(8,128)(2,1)} %build_d.3.refs_17_.dt_ref, bf16[16,384,768]{2,1,0:T(8,128)(2,1)} %prep.1.refs_6_.wt_ref, f32[8,512]{1,0:T(8,128)} %get-tuple-element.90.sel_ref, bf16[2,112,768]{2,1,0:T(8,128)(2,1)} %get-tuple-element.150.refs_0_), custom_call_target="tpu_custom_call" | custom-call | flops 3623878656 | bytes 4718592 | tf_op jit(solution)/shard_map/conv_dx/pallas_call | solution.py:111
  344.5 12.4 %collective-permute-done.30 = bf16[1,104,768]{2,1,0:T(8,128)(2,1)S(1)} collective-permute-done((bf16[1,104,768]{2,1,0:T(8,128)(2,1)}, bf16[1,104,768]{2,1,0:T(8,128)(2,1)S(1)}, u32[]{:S(2)}, u32[]{:S(2)}) %collective-permute-start.30) | collective-permute-done | bytes 159776 | tf_op jit(solution)/shard_map/ppermute | solution.py:1138
  367.1 13.3 %collective-permute-done.34.gs_ref.gk_ref = bf16[2,112,768]{2,1,0:T(8,128)(2,1)S(1)} collective-permute-done((bf16[2,112,768]{2,1,0:T(8,128)(2,1)S(1)}, bf16[2,112,768]{2,1,0:T(8,128)(2,1)S(1)}, u32[]{:S(2)}, u32[]{:S(2)}) %collective-permute-start.34) | collective-permute-done | bytes 344096 | tf_op jit(solution)/shard_map/ppermute | solution.py:1077
  386.5 7.6 %collective-permute-done.35.g_ref = bf16[1,112,768]{2,1,0:T(8,128)(2,1)S(1)} collective-permute-done((bf16[1,112,768]{2,1,0:T(8,128)(2,1)}, bf16[1,112,768]{2,1,0:T(8,128)(2,1)S(1)}, u32[]{:S(2)}, u32[]{:S(2)}) %collective-permute-start.35) | collective-permute-done | bytes 172064 | tf_op jit(solution)/shard_map/ppermute | solution.py:1124
  398.2 8.2 %collective-permute-done.36 = bf16[1,112,768]{2,1,0:T(8,128)(2,1)S(1)} collective-permute-done((bf16[1,112,768]{2,1,0:T(8,128)(2,1)}, bf16[1,112,768]{2,1,0:T(8,128)(2,1)S(1)}, u32[]{:S(2)}, u32[]{:S(2)}) %collective-permute-start.36) | collective-permute-done | bytes 172064 | tf_op jit(solution)/shard_map/ppermute | solution.py:1138
  (225 shorter events, 140.1 us)
Async XLA Ops:
  8.5 27.3 %collective-permute-start = (bf16[256,768]{1,0:T(8,128)(2,1)S(1)}, bf16[256,768]{1,0:T(8,128)(2,1)S(1)}, u32[]{:S(2)}, u32[]{:S(2)}) collective-permute-start(bf16[256,768]{1,0:T(8,128)(2,1)S(1)} %get-tuple-element.220), channel_id=1, source_target_pairs={{0,0},{1,1},{2,4},{3,5},{4,2},{5,3},{6,6},{7,7},{8,8},{9,9},{10,12... | collective-permute-start | bytes 1179656 | tf_op jit(solution)/shard_map/ppermute | solution.py:1024
  9.2 26.6 %collective-permute-start.1 = (bf16[256,768]{1,0:T(8,128)(2,1)S(1)}, bf16[256,768]{1,0:T(8,128)(2,1)S(1)}, u32[]{:S(2)}, u32[]{:S(2)}) collective-permute-start(bf16[256,768]{1,0:T(8,128)(2,1)S(1)} %get-tuple-element.219), channel_id=1, source_target_pairs={{0,1},{1,0},{2,5},{3,4},{4,3},{5,2},{6,7},{7,6},{8,9},{9,8},{10,13... | collective-permute-start | bytes 1179656 | tf_op jit(solution)/shard_map/ppermute | solution.py:1024
  12.3 23.5 %collective-permute-start.2 = (bf16[64,768]{1,0:T(8,128)(2,1)S(1)}, bf16[64,768]{1,0:T(8,128)(2,1)S(1)}, u32[]{:S(2)}, u32[]{:S(2)}) collective-permute-start(bf16[64,768]{1,0:T(8,128)(2,1)S(1)} %get-tuple-element.218), channel_id=1, source_target_pairs={{2,0},{6,2},{10,8},{14,10},{18,16},{22,18},{26,24},{30,26},{1,4},{... | collective-permute-start | bytes 294920 | tf_op jit(solution)/shard_map/ppermute | solution.py:1044
  13.6 22.2 %collective-permute-start.3 = (bf16[64,768]{1,0:T(8,128)(2,1)S(1)}, bf16[64,768]{1,0:T(8,128)(2,1)S(1)}, u32[]{:S(2)}, u32[]{:S(2)}) collective-permute-start(bf16[64,768]{1,0:T(8,128)(2,1)S(1)} %get-tuple-element.217), channel_id=1, source_target_pairs={{2,1},{6,3},{10,9},{14,11},{18,17},{22,19},{26,25},{30,27},{1,5},{... | collective-permute-start | bytes 294920 | tf_op jit(solution)/shard_map/ppermute | solution.py:1044
  66.5 24.1 %collective-permute-start.4 = (bf16[512,1536]{1,0:T(8,128)(2,1)}, bf16[512,1536]{1,0:T(8,128)(2,1)S(1)}, u32[]{:S(2)}, u32[]{:S(2)}) collective-permute-start(bf16[512,1536]{1,0:T(8,128)(2,1)} %get-tuple-element.95.refs_3_.refs_5_.refs_6_.refs_8_), channel_id=1, source_target_pairs={{0,4},{4,0},{1,5},{5,1},{2,6},{6,2},{3,7},{7,3},{8,12},{12,8},{9,1... | collective-permute-start | bytes 4718600 | tf_op jit(solution)/shard_map/ppermute | solution.py:1179
  70.0 20.7 %all-to-all-start = ((bf16[8,96,768]{2,1,0:T(8,128)(2,1)}), bf16[8,96,768]{2,1,0:T(8,128)(2,1)S(1)}, u32[]{:S(2)}, u32[]{:S(2)}) async-start(bf16[8,96,768]{2,1,0:T(8,128)(2,1)} %bitcast.186), calls=%async_computation | async-start | bytes 2359296 | tf_op jit(solution)/shard_map/all_to_all | solution.py:1171
  146.5 28.9 %collective-permute-start.10 = (bf16[4,96,3072]{2,1,0:T(8,128)(2,1)}, bf16[4,96,3072]{2,1,0:T(8,128)(2,1)S(1)}, u32[]{:S(2)}, u32[]{:S(2)}) collective-permute-start(bf16[4,96,3072]{2,1,0:T(8,128)(2,1)} %get-tuple-element.103.refs_0_.refs_10_), channel_id=1, source_target_pairs={{0,4},{1,5},{2,6},{3,7},{4,0},{5,1},{6,2},{7,3},{8,12},{9,13},{10,... | collective-permute-start | bytes 7077896 | tf_op jit(solution)/shard_map/ppermute | solution.py:1091
  163.7 18.3 %collective-permute-start.9 = (bf16[4,768,384]{2,1,0:T(8,128)(2,1)}, bf16[4,768,384]{2,1,0:T(8,128)(2,1)}, u32[]{:S(2)}, u32[]{:S(2)}) collective-permute-start(bf16[4,768,384]{2,1,0:T(8,128)(2,1)} %get-tuple-element.106.refs_11_), channel_id=1, source_target_pairs={{0,4},{1,5},{2,6},{3,7},{4,0},{5,1},{6,2},{7,3},{8,12},{9,13},{10,... | collective-permute-start | bytes 7077896 | tf_op jit(solution)/shard_map/ppermute | solution.py:1091
  174.9 23.5 %collective-permute-start.11 = (bf16[2,512,384]{2,1,0:T(8,128)(2,1)}, bf16[2,512,384]{2,1,0:T(8,128)(2,1)}, u32[]{:S(2)}, u32[]{:S(2)}) collective-permute-start(bf16[2,512,384]{2,1,0:T(8,128)(2,1)} %get-tuple-element.117), channel_id=1, source_target_pairs={{0,4},{4,0},{1,5},{5,1},{2,6},{6,2},{3,7},{7,3},{8,12},{12,8},{9,1... | collective-permute-start | bytes 2359304 | tf_op jit(solution)/shard_map/ppermute | solution.py:1217
  180.4 38.2 %collective-permute-start.15 = (bf16[2,96,3072]{2,1,0:T(8,128)(2,1)}, bf16[2,96,3072]{2,1,0:T(8,128)(2,1)S(1)}, u32[]{:S(2)}, u32[]{:S(2)}) collective-permute-start(bf16[2,96,3072]{2,1,0:T(8,128)(2,1)} %get-tuple-element.110.refs_0_), channel_id=1, source_target_pairs={{0,16},{1,17},{2,18},{3,19},{4,20},{5,21},{6,22},{7,23},{8,24},{9,... | collective-permute-start | bytes 3538952 | tf_op jit(solution)/shard_map/ppermute | solution.py:1097
  185.5 36.9 %collective-permute-start.14 = (bf16[2,768,384]{2,1,0:T(8,128)(2,1)}, bf16[2,768,384]{2,1,0:T(8,128)(2,1)S(1)}, u32[]{:S(2)}, u32[]{:S(2)}) collective-permute-start(bf16[2,768,384]{2,1,0:T(8,128)(2,1)} %get-tuple-element.111.refs_10_), channel_id=1, source_target_pairs={{0,8},{1,9},{2,10},{3,11},{4,12},{5,13},{6,14},{7,15},{8,0},{9,1},... | collective-permute-start | bytes 3538952 | tf_op jit(solution)/shard_map/ppermute | solution.py:1097
  198.3 43.2 %collective-permute-start.7 = (bf16[256,768]{0,1:T(8,128)(2,1)}, bf16[256,768]{0,1:T(8,128)(2,1)}, u32[]{:S(2)}, u32[]{:S(2)}) collective-permute-start(bf16[256,768]{0,1:T(8,128)(2,1)} %get-tuple-element.212), channel_id=1, source_target_pairs={{1,0},{0,1},{5,2},{4,3},{3,4},{2,5},{7,6},{6,7},{9,8},{8,9},{13,10... | collective-permute-start | bytes 1179656 | tf_op jit(solution)/shard_map/ppermute | solution.py:1034
  198.4 44.6 %collective-permute-start.8 = (bf16[256,768]{0,1:T(8,128)(2,1)}, bf16[256,768]{0,1:T(8,128)(2,1)}, u32[]{:S(2)}, u32[]{:S(2)}) collective-permute-start(bf16[256,768]{0,1:T(8,128)(2,1)} %get-tuple-element.211), channel_id=1, source_target_pairs={{0,0},{1,1},{4,2},{5,3},{2,4},{3,5},{6,6},{7,7},{8,8},{9,9},{12,10... | collective-permute-start | bytes 1179656 | tf_op jit(solution)/shard_map/ppermute | solution.py:1034
  214.8 44.8 %all-to-all-start.1 = ((bf16[8,96,640]{2,1,0:T(8,128)(2,1)}), bf16[8,96,640]{2,1,0:T(8,128)(2,1)S(1)}, u32[]{:S(2)}, u32[]{:S(2)}) async-start(bf16[8,96,640]{2,1,0:T(8,128)(2,1)} %bitcast.161), calls=%async_computation.1 | async-start | bytes 1966080 | tf_op jit(solution)/shard_map/all_to_all | solution.py:1228
  231.2 41.2 %collective-permute-start.17 = (bf16[8,112,768]{2,1,0:T(8,128)(2,1)}, bf16[8,112,768]{2,1,0:T(8,128)(2,1)}, u32[]{:S(2)}, u32[]{:S(2)}) collective-permute-start(bf16[8,112,768]{2,1,0:T(8,128)(2,1)} %get-tuple-element.135.refs_1_), channel_id=1, source_target_pairs={{0,4},{1,5},{2,6},{3,7},{4,0},{5,1},{6,2},{7,3},{8,12},{9,13},{10,... | collective-permute-start | bytes 4128776 | tf_op jit(solution)/shard_map/ppermute | solution.py:1091
  238.5 39.6 %collective-permute-start.16 = (bf16[8,112,768]{2,1,0:T(8,128)(2,1)}, bf16[8,112,768]{2,1,0:T(8,128)(2,1)}, u32[]{:S(2)}, u32[]{:S(2)}) collective-permute-start(bf16[8,112,768]{2,1,0:T(8,128)(2,1)} %get-tuple-element.138.refs_2_.refs_0_), channel_id=1, source_target_pairs={{0,4},{1,5},{2,6},{3,7},{4,0},{5,1},{6,2},{7,3},{8,12},{9,13},{10,... | collective-permute-start | bytes 4128776 | tf_op jit(solution)/shard_map/ppermute | solution.py:1091
  267.4 146.1 %all-reduce.3.cloned.1.call-start = ((), (), s32[]{:S(2)}) async-start(), calls=%async_computation.2 | async-start | bytes 2359296 | tf_op jit(solution)/shard_map/psum | solution.py:1244
  270.4 34.4 %collective-permute-start.23 = (bf16[2,104,768]{2,1,0:T(8,128)(2,1)}, bf16[2,104,768]{2,1,0:T(8,128)(2,1)}, u32[]{:S(2)}, u32[]{:S(2)}) collective-permute-start(bf16[2,104,768]{2,1,0:T(8,128)(2,1)} %get-tuple-element.224.refs_0_), channel_id=1, source_target_pairs={{0,1},{1,0},{2,3},{3,2},{4,5},{5,4},{6,7},{7,6},{8,9},{9,8},{10,11... | collective-permute-start | bytes 958472 | tf_op jit(solution)/shard_map/ppermute | solution.py:1077
  276.5 35.0 %collective-permute-start.21 = (bf16[4,112,768]{2,1,0:T(8,128)(2,1)}, bf16[4,112,768]{2,1,0:T(8,128)(2,1)S(1)}, u32[]{:S(2)}, u32[]{:S(2)}) collective-permute-start(bf16[4,112,768]{2,1,0:T(8,128)(2,1)} %get-tuple-element.143.refs_0_), channel_id=1, source_target_pairs={{0,8},{1,9},{2,10},{3,11},{4,12},{5,13},{6,14},{7,15},{8,0},{9,1},... | collective-permute-start | bytes 2064392 | tf_op jit(solution)/shard_map/ppermute | solution.py:1097
  282.0 33.1 %collective-permute-start.20 = (bf16[4,112,768]{2,1,0:T(8,128)(2,1)}, bf16[4,112,768]{2,1,0:T(8,128)(2,1)S(1)}, u32[]{:S(2)}, u32[]{:S(2)}) collective-permute-start(bf16[4,112,768]{2,1,0:T(8,128)(2,1)} %get-tuple-element.144.refs_16_), channel_id=1, source_target_pairs={{0,16},{1,17},{2,18},{3,19},{4,20},{5,21},{6,22},{7,23},{8,24},{9,... | collective-permute-start | bytes 2064392 | tf_op jit(solution)/shard_map/ppermute | solution.py:1097
  292.5 16.7 %collective-permute-start.22 = (bf16[2,104,768]{2,1,0:T(8,128)(2,1)}, bf16[2,104,768]{2,1,0:T(8,128)(2,1)}, u32[]{:S(2)}, u32[]{:S(2)}) collective-permute-start(bf16[2,104,768]{2,1,0:T(8,128)(2,1)} %get-tuple-element.225.refs_0_), channel_id=1, source_target_pairs={{0,1},{1,0},{2,3},{3,2},{4,5},{5,4},{6,7},{7,6},{8,9},{9,8},{10,11... | collective-permute-start | bytes 958472 | tf_op jit(solution)/shard_map/ppermute | solution.py:1077
  306.7 24.6 %collective-permute-start.27 = (bf16[1,104,768]{2,1,0:T(8,128)(2,1)}, bf16[1,104,768]{2,1,0:T(8,128)(2,1)S(1)}, u32[]{:S(2)}, u32[]{:S(2)}) collective-permute-start(bf16[1,104,768]{2,1,0:T(8,128)(2,1)} %get-tuple-element.147.refs_0_), channel_id=1, source_target_pairs={{0,2},{1,3},{2,0},{3,1},{4,6},{5,7},{6,4},{7,5},{8,10},{9,11},{10,... | collective-permute-start | bytes 479240 | tf_op jit(solution)/shard_map/ppermute | solution.py:1124
  311.0 28.2 %collective-permute-start.26 = (bf16[1,104,768]{2,1,0:T(8,128)(2,1)}, bf16[1,104,768]{2,1,0:T(8,128)(2,1)S(1)}, u32[]{:S(2)}, u32[]{:S(2)}) collective-permute-start(bf16[1,104,768]{2,1,0:T(8,128)(2,1)} %get-tuple-element.148.refs_0_), channel_id=1, source_target_pairs={{0,2},{1,3},{2,0},{3,1},{4,6},{5,7},{6,4},{7,5},{8,10},{9,11},{10,... | collective-permute-start | bytes 479240 | tf_op jit(solution)/shard_map/ppermute | solution.py:1124
  314.6 44.0 %collective-permute-start.32 = (bf16[2,112,768]{2,1,0:T(8,128)(2,1)}, bf16[2,112,768]{2,1,0:T(8,128)(2,1)}, u32[]{:S(2)}, u32[]{:S(2)}) collective-permute-start(bf16[2,112,768]{2,1,0:T(8,128)(2,1)} %get-tuple-element.149.refs_0_), channel_id=1, source_target_pairs={{0,16},{1,17},{2,18},{3,19},{4,20},{5,21},{6,22},{7,23},{8,24},{9,... | collective-permute-start | bytes 1032200 | tf_op jit(solution)/shard_map/ppermute | solution.py:1097
  330.5 30.0 %collective-permute-start.33 = (bf16[2,112,768]{2,1,0:T(8,128)(2,1)}, bf16[2,112,768]{2,1,0:T(8,128)(2,1)}, u32[]{:S(2)}, u32[]{:S(2)}) collective-permute-start(bf16[2,112,768]{2,1,0:T(8,128)(2,1)} %get-tuple-element.150.refs_0_), channel_id=1, source_target_pairs={{0,8},{1,9},{2,10},{3,11},{4,12},{5,13},{6,14},{7,15},{8,0},{9,1},... | collective-permute-start | bytes 1032200 | tf_op jit(solution)/shard_map/ppermute | solution.py:1097
  333.6 23.2 %collective-permute-start.30 = (bf16[1,104,768]{2,1,0:T(8,128)(2,1)}, bf16[1,104,768]{2,1,0:T(8,128)(2,1)S(1)}, u32[]{:S(2)}, u32[]{:S(2)}) collective-permute-start(bf16[1,104,768]{2,1,0:T(8,128)(2,1)} %join_last.9.refs_0_), channel_id=1, source_target_pairs={{0,2},{1,3},{2,0},{3,1},{4,6},{5,7},{6,4},{7,5},{8,10},{9,11},{10,... | collective-permute-start | bytes 479240 | tf_op jit(solution)/shard_map/ppermute | solution.py:1138
  341.6 24.7 %collective-permute-start.28 = (bf16[1,104,768]{2,1,0:T(8,128)(2,1)}, bf16[1,104,768]{2,1,0:T(8,128)(2,1)S(1)}, u32[]{:S(2)}, u32[]{:S(2)}) collective-permute-start(bf16[1,104,768]{2,1,0:T(8,128)(2,1)} %join_last.10.refs_0_), channel_id=1, source_target_pairs={{0,2},{1,3},{2,0},{3,1},{4,6},{5,7},{6,4},{7,5},{8,10},{9,11},{10,... | collective-permute-start | bytes 479240 | tf_op jit(solution)/shard_map/ppermute | solution.py:1138
  342.1 43.1 %collective-permute-start.24 = (bf16[256,768]{0,1:T(8,128)(2,1)S(1)}, bf16[256,768]{0,1:T(8,128)(2,1)S(1)}, u32[]{:S(2)}, u32[]{:S(2)}) collective-permute-start(bf16[256,768]{0,1:T(8,128)(2,1)S(1)} %get-tuple-element.208), channel_id=1, source_target_pairs={{1,0},{0,1},{5,2},{4,3},{3,4},{2,5},{7,6},{6,7},{9,8},{8,9},{13,10... | collective-permute-start | bytes 1179656 | tf_op jit(solution)/shard_map/ppermute | solution.py:1034
  356.8 28.4 %collective-permute-start.25 = (bf16[256,768]{0,1:T(8,128)(2,1)S(1)}, bf16[256,768]{0,1:T(8,128)(2,1)S(1)}, u32[]{:S(2)}, u32[]{:S(2)}) collective-permute-start(bf16[256,768]{0,1:T(8,128)(2,1)S(1)} %get-tuple-element.207), channel_id=1, source_target_pairs={{0,0},{1,1},{4,2},{5,3},{2,4},{3,5},{6,6},{7,7},{8,8},{9,9},{12,10... | collective-permute-start | bytes 1179656 | tf_op jit(solution)/shard_map/ppermute | solution.py:1034
  358.6 37.9 %collective-permute-start.31 = (bf16[2,104,768]{2,1,0:T(8,128)(2,1)}, bf16[2,104,768]{2,1,0:T(8,128)(2,1)S(1)}, u32[]{:S(2)}, u32[]{:S(2)}) collective-permute-start(bf16[2,104,768]{2,1,0:T(8,128)(2,1)} %maximum_select_fusion.7), channel_id=1, source_target_pairs={{0,1},{1,0},{2,3},{3,2},{4,5},{5,4},{6,7},{7,6},{8,9},{9,8},{10,11... | collective-permute-start | bytes 958472 | tf_op jit(solution)/shard_map/ppermute | solution.py:1138
  364.3 16.2 %collective-permute-start.34 = (bf16[2,112,768]{2,1,0:T(8,128)(2,1)S(1)}, bf16[2,112,768]{2,1,0:T(8,128)(2,1)S(1)}, u32[]{:S(2)}, u32[]{:S(2)}) collective-permute-start(bf16[2,112,768]{2,1,0:T(8,128)(2,1)S(1)} %get-tuple-element.221), channel_id=1, source_target_pairs={{0,1},{1,0},{2,3},{3,2},{4,5},{5,4},{6,7},{7,6},{8,9},{9,8},{10,11... | collective-permute-start | bytes 1032200 | tf_op jit(solution)/shard_map/ppermute | solution.py:1077
  367.0 29.6 %collective-permute-start.29 = (bf16[2,104,768]{2,1,0:T(8,128)(2,1)}, bf16[2,104,768]{2,1,0:T(8,128)(2,1)}, u32[]{:S(2)}, u32[]{:S(2)}) collective-permute-start(bf16[2,104,768]{2,1,0:T(8,128)(2,1)} %maximum_select_fusion.6), channel_id=1, source_target_pairs={{0,1},{1,0},{2,3},{3,2},{4,5},{5,4},{6,7},{7,6},{8,9},{9,8},{10,11... | collective-permute-start | bytes 958472 | tf_op jit(solution)/shard_map/ppermute | solution.py:1138
  (45 other events, 282.8 us)
Sparse Core Ops, SparseCore 0:
  270.6 86.4 all-reduce.2
